TPU v7x, 32 devices: a whole 2x2x4 slice. The times are simulated.
32 devices in a mesh: dp: 4 (over z), expert: 8 (over y, x, core).
Axes of the slice: x: 2, y: 2, z: 4, core: 2. Of those that a mesh axis runs over, the one named last changes fastest.
Arguments:
- row_codes: bfloat16 [1024, 4096], P('expert', 'dp'), may hold values from -6 to 6
- scales: bfloat16 [1024, 32], P('expert', 'dp'), may hold values from 0.125 to 2
- routes: int32 [1024, 8], P('expert'), may hold values from 0 to 255, as said below
- mix_weights: float32 [1024, 8], P('expert'), may hold values from 0.05 to 1
- w_gate: bfloat16 [8, 4096, 1024], P('expert', 'dp'), may hold values from -0.09375 to 0.09375
- w_up: bfloat16 [8, 4096, 1024], P('expert', 'dp'), may hold values from -0.09375 to 0.09375
- w_down: bfloat16 [8, 1024, 4096], P('expert', None, 'dp'), may hold values from -0.1875 to 0.1875
- grad_out: bfloat16 [1024, 4096], P('expert', 'dp'), may hold values from -6 to 6
Outputs:
- mixed_out: bfloat16 [1024, 4096], P('expert', 'dp')
- grad_rows: bfloat16 [1024, 4096], P('expert', 'dp')
- grad_gate: bfloat16 [8, 4096, 1024], P('expert', 'dp')
- grad_up: bfloat16 [8, 4096, 1024], P('expert', 'dp')
- grad_down: bfloat16 [8, 1024, 4096], P('expert', None, 'dp')
Inputs may be any that keep to these rules, and one draw needn't show every extreme that they name: `routes`: each row names 8 different routed experts; the ids below 8 are the experts of the window, id e held on index e of expert. In each aligned block of 128 rows (the tokens of one index of expert) no id is named by more than 8 rows, and one id below 8, the same in every block, is named by exactly 8 rows.
All inputs are finite; a program needn't handle non-finite values.
Results may differ from a plain program's by a relative error of at most 0.018.
Values may be sent and summed in bfloat16 or wider, within the bound.
No kernel may reach another device: no remote copies, remote signals or barrier semaphores. Data moves between devices by JAX's collectives and lax.ppermute only.
A program may use at most 64 MiB of HBM per device.

v0:
```python
import jax
import jax.numpy as jnp
from jax import lax
from jax.sharding import PartitionSpec as P

CAP = 8


def swap_rows(rows):
    return lax.all_to_all(rows, "expert", split_axis=0, concat_axis=0, tiled=True)


def contract_last(left, right):
    return lax.dot_general(
        left, right, (((1,), (1,)), ((), ())), preferred_element_type=jnp.float32
    )


def contract_first(left, right):
    return lax.dot_general(
        left, right, (((0,), (0,)), ((), ())), preferred_element_type=jnp.float32
    )


def gating_grads(hidden_grad, gate_act, up_act):
    sig_gate = jax.nn.sigmoid(gate_act)
    gate_grad = (hidden_grad * up_act * sig_gate * (1.0 + gate_act * (1.0 - sig_gate))).astype(
        jnp.bfloat16
    )
    up_grad = (hidden_grad * gate_act * sig_gate).astype(jnp.bfloat16)
    return (gate_grad, up_grad)


def on_device(row_codes, scales, routes, mix_weights, w_gate, w_up, w_down, grad_out):
    owners = lax.axis_size("expert")
    token_count, features = row_codes.shape
    slot_total = owners * CAP
    flat_ids = routes.reshape(-1)
    one_hot = (flat_ids[:, None] == jnp.arange(owners, dtype=jnp.int32)[None, :]).astype(jnp.int32)
    ranking = jnp.sum((jnp.cumsum(one_hot, axis=0) - one_hot) * one_hot, axis=1)
    target = jnp.where(flat_ids < owners, flat_ids * CAP + ranking, -1).reshape(routes.shape)
    matches = target[None, :, :] == jnp.arange(slot_total, dtype=jnp.int32)[:, None, None]
    placing = jnp.any(matches, axis=2).astype(jnp.bfloat16)
    blending = jnp.sum(jnp.where(matches, mix_weights[None, :, :], 0.0), axis=2)
    send_codes = jnp.dot(placing, row_codes, preferred_element_type=jnp.float32).astype(
        jnp.bfloat16
    )
    send_scales = jnp.dot(placing, scales, preferred_element_type=jnp.float32).astype(jnp.bfloat16)
    got_codes, got_scales = (
        lax.all_to_all(send_codes, "expert", split_axis=0, concat_axis=0, tiled=True),
        lax.all_to_all(send_scales, "expert", split_axis=0, concat_axis=0, tiled=True),
    )
    groups = features // 128
    expert_rows = (
        (
            got_codes.astype(jnp.float32).reshape(slot_total, groups, 128)
            * got_scales.astype(jnp.float32)[:, :, None]
        )
        .reshape(slot_total, features)
        .astype(jnp.bfloat16)
    )
    gate_w = w_gate[0]
    up_w = w_up[0]
    down_w = w_down[0]
    gate_share, up_share = (
        lax.psum_scatter(
            jnp.dot(expert_rows, gate_w, preferred_element_type=jnp.float32).astype(jnp.bfloat16),
            "dp",
            scatter_dimension=0,
            tiled=True,
        ).astype(jnp.float32),
        lax.psum_scatter(
            jnp.dot(expert_rows, up_w, preferred_element_type=jnp.float32).astype(jnp.bfloat16),
            "dp",
            scatter_dimension=0,
            tiled=True,
        ).astype(jnp.float32),
    )
    gate_act, up_act = (
        lax.all_gather(gate_share.astype(jnp.bfloat16), "dp", axis=0, tiled=True).astype(
            gate_share.dtype
        ),
        lax.all_gather(up_share.astype(jnp.bfloat16), "dp", axis=0, tiled=True).astype(
            up_share.dtype
        ),
    )
    hidden = (jax.nn.silu(gate_act) * up_act).astype(jnp.bfloat16)
    expert_out = jnp.dot(hidden, down_w, preferred_element_type=jnp.float32).astype(jnp.bfloat16)
    returned = swap_rows(expert_out)
    mixed_out = jnp.dot(
        blending.T, returned.astype(jnp.float32), precision=lax.Precision.HIGHEST
    ).astype(jnp.bfloat16)
    grad_slots = jnp.dot(
        blending, grad_out.astype(jnp.float32), precision=lax.Precision.HIGHEST
    ).astype(jnp.bfloat16)
    slot_grads = swap_rows(grad_slots)
    grad_share = lax.psum_scatter(
        contract_last(slot_grads, down_w).astype(jnp.bfloat16),
        "dp",
        scatter_dimension=0,
        tiled=True,
    ).astype(jnp.float32)
    hidden_grad = lax.all_gather(grad_share.astype(jnp.bfloat16), "dp", axis=0, tiled=True).astype(
        grad_share.dtype
    )
    gate_grad, up_grad = gating_grads(hidden_grad, gate_act, up_act)
    row_grad = (contract_last(gate_grad, gate_w) + contract_last(up_grad, up_w)).astype(
        jnp.bfloat16
    )
    gate_sum = contract_first(expert_rows, gate_grad)
    up_sum = contract_first(expert_rows, up_grad)
    down_sum = contract_first(hidden, slot_grads)
    row_back = swap_rows(row_grad)
    grad_rows = jnp.dot(placing.T, row_back, preferred_element_type=jnp.float32).astype(
        jnp.bfloat16
    )
    return (
        mixed_out,
        grad_rows,
        gate_sum.astype(jnp.bfloat16)[None],
        up_sum.astype(jnp.bfloat16)[None],
        down_sum.astype(jnp.bfloat16)[None],
    )


def solution(mesh):
    placed = (
        P("expert", "dp"),
        P("expert", "dp"),
        P("expert", None),
        P("expert", None),
        P("expert", "dp", None),
        P("expert", "dp", None),
        P("expert", None, "dp"),
        P("expert", "dp"),
    )
    return jax.shard_map(
        on_device,
        mesh=mesh,
        in_specs=placed,
        out_specs=(
            P("expert", "dp"),
            P("expert", "dp"),
            P("expert", "dp", None),
            P("expert", "dp", None),
            P("expert", None, "dp"),
        ),
        check_vma=False,
    )
```

profile of v0, /device:TPU:0, one launch (start us, length us, event | category | flops | bytes accessed | tf_op | source)
XLA Modules:
  0.0 141.3 jit_solution(4925963523814405255)
XLA Ops:
  7.2 0.9 copy.52
  8.3 2.3 %reduce-window.6 = s32[8,8,128]{2,1,0:T(8,128)S(1)} reduce-window(s32[8,8,128]{2,1,0:T(8,128)S(1)} %fusion.63, s32[]{:T(128)} %constant.4.clone.1), window={size=1x1x128 pad=0_0x0_0x127_0}, to_apply=%region_0.0 | reduce-window | flops 1040384 | bytes 65540 | tf_op jit(solution)/shard_map/reduce-window
  11.3 0.7 add_select_fusion
  12.1 0.8 convolution_convert_fusion.4
  13.6 5.2 %all-to-all-start.1 = ((bf16[8,8,8]{1,2,0:T(8,128)(2,1)}), bf16[8,8,8]{1,2,0:T(8,128)(2,1)S(1)}, u32[]{:S(2)}, u32[]{:S(2)}) async-start(bf16[8,8,8]{1,2,0:T(8,128)(2,1)} %copy.55), calls=%async_computation.1 | async-start | bytes 32768 | tf_op jit(solution)/shard_map/all_to_all | solution.py:51
  18.8 1.8 %fusion.33 = bf16[8,8,1024]{2,1,0:T(8,128)(2,1)} fusion(pred[64,128]{1,0:T(8,128)(4,1)S(1)} %fusion.51, bf16[128,1024]{1,0:T(8,128)(2,1)} %param.8), kind=kOutput, calls=%fused_computation.26 | convolution fusion | flops 16842752 | bytes 401408 | tf_op jit(solution)/shard_map/dot_general | solution.py:45
  20.6 0.8 select_reduce_fusion
  21.3 2.2 %all-to-all-done.1 = bf16[8,8,8]{1,2,0:T(8,128)(2,1)S(1)} async-done(((bf16[8,8,8]{1,2,0:T(8,128)(2,1)}), bf16[8,8,8]{1,2,0:T(8,128)(2,1)S(1)}, u32[]{:S(2)}, u32[]{:S(2)}) %all-to-all-start.1) | async-done | bytes 1056 | tf_op jit(solution)/shard_map/all_to_all | solution.py:51
  23.5 3.4 %all-to-all-start = ((bf16[8,8,1024]{2,1,0:T(8,128)(2,1)}), bf16[8,8,1024]{2,1,0:T(8,128)(2,1)S(1)}, u32[]{:S(2)}, u32[]{:S(2)}) async-start(bf16[8,8,1024]{2,1,0:T(8,128)(2,1)} %fusion.33), calls=%async_computation | async-start | bytes 262144 | tf_op jit(solution)/shard_map/all_to_all | solution.py:50
  26.9 1.9 %fusion.34 = bf16[8,8,1024]{2,1,0:T(8,128)(2,1)} fusion(f32[64,128]{1,0:T(8,128)S(1)} %select_reduce_fusion, bf16[128,1024]{1,0:T(8,128)(2,1)} %param.15), kind=kOutput, calls=%fused_computation.27 | convolution fusion | flops 100728832 | bytes 425984 | tf_op jit(solution)/shard_map/dot_general | solution.py:93
  28.9 3.5 %all-to-all-done = bf16[8,8,1024]{2,1,0:T(8,128)(2,1)S(1)} async-done(((bf16[8,8,1024]{2,1,0:T(8,128)(2,1)}), bf16[8,8,1024]{2,1,0:T(8,128)(2,1)S(1)}, u32[]{:S(2)}, u32[]{:S(2)}) %all-to-all-start) | async-done | bytes 131104 | tf_op jit(solution)/shard_map/all_to_all | solution.py:50
  32.4 3.4 %all-to-all-start.3 = ((bf16[8,8,1024]{2,1,0:T(8,128)(2,1)}), bf16[8,8,1024]{2,1,0:T(8,128)(2,1)S(1)}, u32[]{:S(2)}, u32[]{:S(2)}) async-start(bf16[8,8,1024]{2,1,0:T(8,128)(2,1)} %fusion.34), calls=%async_computation.5 | async-start | bytes 262144 | tf_op jit(solution)/shard_map/all_to_all | solution.py:10
  36.0 2.7 %fusion.21 = bf16[64,1024]{1,0:T(8,128)(2,1)} fusion(bf16[1,1024,1024]{2,1,0:T(8,128)(2,1)} %param.13, bf16[8,8,8,128]{3,2,1,0:T(8,128)(2,1)S(1)} %bitcast.114), kind=kOutput, calls=%fused_computation.20 | convolution fusion | flops 134283264 | bytes 2359296 | tf_op jit(solution)/shard_map/dot_general | solution.py:73
  38.8 2.7 %fusion.18 = bf16[64,1024]{1,0:T(8,128)(2,1)} fusion(bf16[1,1024,1024]{2,1,0:T(8,128)(2,1)} %param.12, bf16[8,8,8,128]{3,2,1,0:T(8,128)(2,1)S(1)} %bitcast.115), kind=kOutput, calls=%fused_computation.19 | convolution fusion | flops 134283264 | bytes 2359296 | tf_op jit(solution)/shard_map/dot_general | solution.py:67
  41.7 1.4 %fusion.27 = bf16[64,1024]{1,0:T(8,128)(2,1)} fusion(bf16[1,1024,1024]{2,1,0:T(8,128)(2,1)S(1)} %copy-done, bf16[8,8,1024]{2,1,0:T(8,128)(2,1)S(1)} %all-to-all-done.3), kind=kOutput, calls=%fused_computation.22 | convolution fusion | flops 134283264 | bytes 2359296 | tf_op jit(solution)/shard_map/dot_general | solution.py:14
  43.1 17.2 %reduce-scatter.6.cloned.1.call-done = bf16[16,1024]{1,0:T(8,128)(2,1)} async-done(((bf16[64,1024]{1,0:T(8,128)(2,1)}), bf16[16,1024]{1,0:T(8,128)(2,1)}) %reduce-scatter.6.cloned.1.call-update) | async-done | bytes 32784 | tf_op jit(solution)/shard_map/reduce_scatter | solution.py:72
  60.3 13.8 %all_gather.10 = bf16[64,1024]{1,0:T(8,128)(2,1)S(1)} all-gather(bf16[16,1024]{1,0:T(8,128)(2,1)} %reduce-scatter.6.cloned.1.call-done), channel_id=1, replica_groups=mesh['dp'=4,'expert'=8] {'dp'}, dimensions={0}, use_global_device_ids=true | all-gather | bytes 163840 | tf_op jit(solution)/shard_map/all_gather | solution.py:83
  74.1 6.5 %reduce-scatter.4.cloned.1.call-done = bf16[16,1024]{1,0:T(8,128)(2,1)} async-done(((bf16[64,1024]{1,0:T(8,128)(2,1)}), bf16[16,1024]{1,0:T(8,128)(2,1)}) %reduce-scatter.4.cloned.1.call-update) | async-done | bytes 32784 | tf_op jit(solution)/shard_map/reduce_scatter | solution.py:66
  80.6 13.8 %all_gather.9 = bf16[64,1024]{1,0:T(8,128)(2,1)S(1)} all-gather(bf16[16,1024]{1,0:T(8,128)(2,1)} %reduce-scatter.4.cloned.1.call-done), channel_id=1, replica_groups=mesh['dp'=4,'expert'=8] {'dp'}, dimensions={0}, use_global_device_ids=true | all-gather | bytes 163840 | tf_op jit(solution)/shard_map/all_gather | solution.py:80
  94.3 1.1 fusion.35
  95.5 3.8 %all-to-all-start.2 = ((bf16[8,8,1024]{2,1,0:T(8,128)(2,1)}), bf16[8,8,1024]{2,1,0:T(8,128)(2,1)S(1)}, u32[]{:S(2)}, u32[]{:S(2)}) async-start(bf16[8,8,1024]{2,1,0:T(8,128)(2,1)} %fusion.35), calls=%async_computation.4 | async-start | bytes 262144 | tf_op jit(solution)/shard_map/all_to_all | solution.py:10
  99.2 1.6 %reduce-scatter.8.cloned.1.call-done = bf16[16,1024]{1,0:T(8,128)(2,1)} async-done(((bf16[64,1024]{1,0:T(8,128)(2,1)}), bf16[16,1024]{1,0:T(8,128)(2,1)}) %reduce-scatter.8.cloned.1.call-update) | async-done | bytes 32784 | tf_op jit(solution)/shard_map/reduce_scatter | solution.py:97
  100.8 13.7 %all_gather.11 = bf16[64,1024]{1,0:T(8,128)(2,1)S(1)} all-gather(bf16[16,1024]{1,0:T(8,128)(2,1)} %reduce-scatter.8.cloned.1.call-done), channel_id=1, replica_groups=mesh['dp'=4,'expert'=8] {'dp'}, dimensions={0}, use_global_device_ids=true | all-gather | bytes 163840 | tf_op jit(solution)/shard_map/all_gather | solution.py:103
  114.5 2.4 %fusion.4 = f32[64,1024]{1,0:T(8,128)S(1)} fusion(bf16[1,1024,1024]{2,1,0:T(8,128)(2,1)} %param.13, bf16[64,1024]{1,0:T(8,128)(2,1)S(1)} %all_gather.9, bf16[64,1024]{1,0:T(8,128)(2,1)S(1)} %all_gather.11), kind=kOutput, calls=%fused_computation.4 | convolution fusion | flops 134742016 | bytes 2621440 | tf_op jit(solution)/shard_map/dot_general | solution.py:14
  116.8 1.4 %fusion.30 = bf16[8,8,1024]{2,1,0:T(8,128)(2,1)} fusion(f32[64,1024]{1,0:T(8,128)S(1)} %fusion.4, bf16[1,1024,1024]{2,1,0:T(8,128)(2,1)S(1)} %copy-done.1, bf16[64,1024]{1,0:T(8,128)(2,1)S(1)} %all_gather.10, bf16[64,1024]{1,0:T(8,128)(2,1)S(1)} %all_gather.11, bf16[64,1024]{1,0:T(8,128)(2,1)S(1)} %all_gather.9), kind=kOutput, calls=%fused_computation.25 | convolution fusion | flops 135200768 | bytes 2883584 | tf_op jit(solution)/shard_map/dot_general | solution.py:14
  118.4 2.1 %convert_bitcast_fusion.2 = bf16[1,1024,1024]{2,1,0:T(8,128)(2,1)} fusion(bf16[8,8,1024]{2,1,0:T(8,128)(2,1)S(1)} %all-to-all-done, f32[8,8,8,128]{3,2,1,0:T(8,128)S(1)} %bitcast.112, bf16[64,1024]{1,0:T(8,128)(2,1)S(1)} %all_gather.10, bf16[64,1024]{1,0:T(8,128)(2,1)S(1)} %all_gather.11, bf16[64,1024]{1,0:T(8,128)(2,1)S(1)} %all_gather.9), kind=kOutput, calls=%fused_computation.14 | convolution fusion | flops 136314880 | bytes 2883584 | tf_op jit(solution)/shard_map/dot_general | solution.py:20
  120.5 2.1 %convert_bitcast_fusion.1 = bf16[1,1024,1024]{2,1,0:T(8,128)(2,1)} fusion(bf16[8,8,1024]{2,1,0:T(8,128)(2,1)S(1)} %all-to-all-done, f32[8,8,8,128]{3,2,1,0:T(8,128)S(1)} %bitcast.113, bf16[64,1024]{1,0:T(8,128)(2,1)S(1)} %all_gather.9, bf16[64,1024]{1,0:T(8,128)(2,1)S(1)} %all_gather.11), kind=kOutput, calls=%fused_computation.13 | convolution fusion | flops 135987200 | bytes 2752512 | tf_op jit(solution)/shard_map/dot_general | solution.py:20
  122.6 2.1 %convert_bitcast_fusion = bf16[1,1024,1024]{2,1,0:T(8,128)(2,1)} fusion(bf16[8,8,1024]{2,1,0:T(8,128)(2,1)S(1)} %all-to-all-done.3, bf16[64,1024]{1,0:T(8,128)(2,1)S(1)} %all_gather.10, bf16[64,1024]{1,0:T(8,128)(2,1)S(1)} %all_gather.9), kind=kOutput, calls=%fused_computation.12 | convolution fusion | flops 135790592 | bytes 2490368 | tf_op jit(solution)/shard_map/dot_general | solution.py:20
  124.6 3.7 %all-to-all-start.4 = ((bf16[8,8,1024]{2,1,0:T(8,128)(2,1)}), bf16[8,8,1024]{2,1,0:T(8,128)(2,1)S(1)}, u32[]{:S(2)}, u32[]{:S(2)}) async-start(bf16[8,8,1024]{2,1,0:T(8,128)(2,1)} %fusion.30), calls=%async_computation.7 | async-start | bytes 262144 | tf_op jit(solution)/shard_map/all_to_all | solution.py:10
  128.3 1.1 convolution_convert_fusion.1
  129.4 4.4 %all-to-all-done.4 = bf16[8,8,1024]{2,1,0:T(8,128)(2,1)S(1)} async-done(((bf16[8,8,1024]{2,1,0:T(8,128)(2,1)}), bf16[8,8,1024]{2,1,0:T(8,128)(2,1)S(1)}, u32[]{:S(2)}, u32[]{:S(2)}) %all-to-all-start.4) | async-done | bytes 131104 | tf_op jit(solution)/shard_map/all_to_all | solution.py:10
  133.8 1.0 convolution_convert_fusion
  (29 shorter events, 2.3 us)
Async XLA Ops:
  7.2 34.5 %copy-start = (bf16[1,1024,1024]{2,1,0:T(8,128)(2,1)S(1)}, bf16[1,1024,1024]{2,1,0:T(8,128)(2,1)}, u32[]{:S(2)}) copy-start(bf16[1,1024,1024]{2,1,0:T(8,128)(2,1)} %param.14) | copy-start | bytes 6291460
  13.6 9.9 %all-to-all-start.1 = ((bf16[8,8,8]{1,2,0:T(8,128)(2,1)}), bf16[8,8,8]{1,2,0:T(8,128)(2,1)S(1)}, u32[]{:S(2)}, u32[]{:S(2)}) async-start(bf16[8,8,8]{1,2,0:T(8,128)(2,1)} %copy.55), calls=%async_computation.1 | async-start | bytes 32768 | tf_op jit(solution)/shard_map/all_to_all | solution.py:51
  23.5 8.8 %all-to-all-start = ((bf16[8,8,1024]{2,1,0:T(8,128)(2,1)}), bf16[8,8,1024]{2,1,0:T(8,128)(2,1)S(1)}, u32[]{:S(2)}, u32[]{:S(2)}) async-start(bf16[8,8,1024]{2,1,0:T(8,128)(2,1)} %fusion.33), calls=%async_computation | async-start | bytes 262144 | tf_op jit(solution)/shard_map/all_to_all | solution.py:50
  32.4 9.3 %all-to-all-start.3 = ((bf16[8,8,1024]{2,1,0:T(8,128)(2,1)}), bf16[8,8,1024]{2,1,0:T(8,128)(2,1)S(1)}, u32[]{:S(2)}, u32[]{:S(2)}) async-start(bf16[8,8,1024]{2,1,0:T(8,128)(2,1)} %fusion.34), calls=%async_computation.5 | async-start | bytes 262144 | tf_op jit(solution)/shard_map/all_to_all | solution.py:10
  35.8 24.5 %reduce-scatter.6.cloned.1.call-start = ((), (), s32[]{:S(2)}) async-start(), calls=%async_computation.9 | async-start | bytes 163840 | tf_op jit(solution)/shard_map/reduce_scatter | solution.py:72
  38.8 41.8 %reduce-scatter.4.cloned.1.call-start = ((), (), s32[]{:S(2)}) async-start(), calls=%async_computation.8 | async-start | bytes 163840 | tf_op jit(solution)/shard_map/reduce_scatter | solution.py:66
  41.6 59.2 %reduce-scatter.8.cloned.1.call-start = ((), (), s32[]{:S(2)}) async-start(), calls=%async_computation.10 | async-start | bytes 163840 | tf_op jit(solution)/shard_map/reduce_scatter | solution.py:97
  95.5 29.2 %all-to-all-start.2 = ((bf16[8,8,1024]{2,1,0:T(8,128)(2,1)}), bf16[8,8,1024]{2,1,0:T(8,128)(2,1)S(1)}, u32[]{:S(2)}, u32[]{:S(2)}) async-start(bf16[8,8,1024]{2,1,0:T(8,128)(2,1)} %fusion.35), calls=%async_computation.4 | async-start | bytes 262144 | tf_op jit(solution)/shard_map/all_to_all | solution.py:10
  100.8 16.0 %copy-start.1 = (bf16[1,1024,1024]{2,1,0:T(8,128)(2,1)S(1)}, bf16[1,1024,1024]{2,1,0:T(8,128)(2,1)}, u32[]{:S(2)}) copy-start(bf16[1,1024,1024]{2,1,0:T(8,128)(2,1)} %param.12) | copy-start | bytes 6291460
  124.6 9.2 %all-to-all-start.4 = ((bf16[8,8,1024]{2,1,0:T(8,128)(2,1)}), bf16[8,8,1024]{2,1,0:T(8,128)(2,1)S(1)}, u32[]{:S(2)}, u32[]{:S(2)}) async-start(bf16[8,8,1024]{2,1,0:T(8,128)(2,1)} %fusion.30), calls=%async_computation.7 | async-start | bytes 262144 | tf_op jit(solution)/shard_map/all_to_all | solution.py:10
Sparse Core Ops, SparseCore 0:
  39.4 20.8 reduce-scatter.5
  63.2 17.3 reduce-scatter.3
  83.4 17.3 reduce-scatter.7
where the time goes:
time: 142 us; the launch traced here: 141 us
  blocking collectives  41.2 us (29%)
  waiting for transfers between devices  35.4 us (25%)
  matrix products  24.6 us (17%)
  starting transfers between devices  19.5 us (14%)
  between operations  13.9 us (10%)
  other arithmetic  4.27 us (3%)
  local copies, waits for them, and re-layouts  2.5 us (2%)
    reduce_scatter x1, waiting for transfers between devices, on_device(): lax.psum_scatter(jnp.dot(expert_rows, up_w, preferred_element_type=jnp.fl...  17.2 us
    all_gather x1, blocking collectives, on_device(): lax.all_gather(up_share.astype(jnp.bfloat16), 'dp', axis=0, tiled=True)  13.8 us
    all_gather x1, blocking collectives, on_device(): lax.all_gather(gate_share.astype(jnp.bfloat16), 'dp', axis=0, tiled=True)  13.8 us
    all_gather x1, blocking collectives, on_device(): lax.all_gather(grad_share.astype(jnp.bfloat16), 'dp', axis=0, tiled=True)  13.7 us
    all_to_all x3, starting transfers between devices, swap_rows(): lax.all_to_all(rows, 'expert', split_axis=0, concat_axis=0, tiled=True)  10.8 us
    reduce_scatter x1, waiting for transfers between devices, on_device(): lax.psum_scatter(jnp.dot(expert_rows, gate_w, preferred_element_type=jnp....  6.52 us
    dot_general x3, matrix products, contract_first(): lax.dot_general(left, right, (((0,), (0,)), ((), ())), preferred_element_...  6.24 us
    dot_general x3, matrix products, contract_last(): lax.dot_general(left, right, (((1,), (1,)), ((), ())), preferred_element_...  5.19 us
  transfers between devices with their start and end apart: 8, of which 6 were waited for; matrix products, arithmetic and copies ran while one was open for 17% of the time, Pallas kernels for 0%

commit v1 on v0

v1 whole, which is shorter than its diff:
```python
import functools

import jax
import jax.numpy as jnp
from jax import lax
from jax.experimental import pallas as pl
from jax.experimental.pallas import tpu as pltpu
from jax.sharding import PartitionSpec as P

CAP = 8
F32 = jnp.float32
BF16 = jnp.bfloat16
VMEM_SPEC = pl.BlockSpec(memory_space=pltpu.VMEM)


def dot(left, right, left_dim, right_dim):
    return lax.dot_general(
        left, right, (((left_dim,), (right_dim,)), ((), ())), preferred_element_type=F32
    )


def call(kernel, out_shape, flops=0, bytes_accessed=0, mib=24):
    many = isinstance(out_shape, (tuple, list))
    return pl.pallas_call(
        kernel,
        out_shape=out_shape,
        out_specs=[VMEM_SPEC] * len(out_shape) if many else VMEM_SPEC,
        compiler_params=pltpu.CompilerParams(vmem_limit_bytes=mib << 20),
        cost_estimate=pl.CostEstimate(
            flops=flops, bytes_accessed=bytes_accessed, transcendentals=0
        ),
    )


def route_kernel(routes_ref, mix_ref, scales_ref, codes_ref, grad_ref, send_ref, place_ref, blend_ref):
    owners = send_ref.shape[0]
    picks, tokens = routes_ref.shape
    slots = owners * CAP
    ids = lax.broadcasted_iota(jnp.int32, (owners, tokens), 0)
    match = jnp.zeros((owners, tokens), F32)
    weight = jnp.zeros((owners, tokens), F32)
    for k in range(picks):
        hit = routes_ref[k : k + 1, :] == ids
        match = jnp.where(hit, 1.0, match)
        weight = jnp.where(hit, mix_ref[k : k + 1, :], weight)
    before = (
        lax.broadcasted_iota(jnp.int32, (tokens, tokens), 0)
        < lax.broadcasted_iota(jnp.int32, (tokens, tokens), 1)
    ).astype(BF16)
    rank = dot(match.astype(BF16), before, 1, 0).astype(jnp.int32)
    rank = jnp.where(match > 0.0, rank, -1)
    position = lax.broadcasted_iota(jnp.int32, (owners, CAP, tokens), 1)
    taken = (rank[:, None, :] == position).reshape(slots, tokens)
    weights = jnp.broadcast_to(weight[:, None, :], (owners, CAP, tokens)).reshape(slots, tokens)
    blend = jnp.where(taken, weights, 0.0)
    place = jnp.where(taken, 1.0, 0.0).astype(BF16)
    place_ref[...] = place
    blend_ref[...] = blend.astype(BF16)
    slot_weight = jnp.sum(blend, axis=1, keepdims=True)
    slot_scale = dot(place, scales_ref[...], 1, 1)
    codes = dot(place, codes_ref[...], 1, 0)
    features = codes.shape[1]
    groups = scales_ref.shape[0]
    width = features // groups
    rows = jnp.concatenate(
        [codes[:, g * width : (g + 1) * width] * slot_scale[:, g : g + 1] for g in range(groups)],
        axis=1,
    )
    grads = dot(place, grad_ref[...], 1, 0) * slot_weight
    both = jnp.concatenate(
        [rows.reshape(owners, CAP, features), grads.reshape(owners, CAP, features)], axis=1
    )
    send_ref[...] = both.astype(BF16)


def split_pair(ref):
    owners, both, features = ref.shape
    wide = ref[...].astype(F32).reshape(owners, 2, CAP, features)
    return (
        wide[:, 0].reshape(owners * CAP, features).astype(BF16),
        wide[:, 1].reshape(owners * CAP, features).astype(BF16),
    )


def partial_kernel(got_ref, gate_ref, up_ref, down_ref, send_ref):
    rows, grads = split_pair(got_ref)
    owners, _, share, hidden = send_ref.shape
    send_ref[:, 0] = dot(rows, gate_ref[...], 1, 0).astype(BF16).reshape(owners, share, hidden)
    send_ref[:, 1] = dot(rows, up_ref[...], 1, 0).astype(BF16).reshape(owners, share, hidden)
    send_ref[:, 2] = dot(grads, down_ref[...], 1, 1).astype(BF16).reshape(owners, share, hidden)


def gating_kernel(got_ref, out_ref):
    gate, up, hidden_grad = (jnp.sum(got_ref[:, i].astype(F32), axis=0) for i in range(3))
    sig = jax.nn.sigmoid(gate)
    silu = gate * sig
    out_ref[0] = (silu * up).astype(BF16)
    out_ref[1] = (hidden_grad * up * sig * (1.0 + gate * (1.0 - sig))).astype(BF16)
    out_ref[2] = (hidden_grad * silu).astype(BF16)


def output_kernel(acts_ref, gate_ref, up_ref, down_ref, send_ref):
    shares, _, share, width = acts_ref.shape
    slots = shares * share
    owners, _, features = send_ref.shape
    hidden, gate_grad, up_grad = (acts_ref[:, i].reshape(slots, width) for i in range(3))
    out = dot(hidden, down_ref[...], 1, 0)
    back = dot(gate_grad, gate_ref[...], 1, 1) + dot(up_grad, up_ref[...], 1, 1)
    both = jnp.concatenate(
        [out.reshape(owners, CAP, features), back.reshape(owners, CAP, features)], axis=1
    )
    send_ref[...] = both.astype(BF16)


def weight_kernel(got_ref, acts_ref, gate_ref, up_ref, down_ref):
    rows, grads = split_pair(got_ref)
    shares, _, share, width = acts_ref.shape
    hidden, gate_grad, up_grad = (acts_ref[:, i].reshape(shares * share, width) for i in range(3))
    gate_ref[0] = dot(rows, gate_grad, 0, 0).astype(BF16)
    up_ref[0] = dot(rows, up_grad, 0, 0).astype(BF16)
    down_ref[0] = dot(hidden, grads, 0, 0).astype(BF16)


def combine_kernel(got_ref, place_ref, blend_ref, mixed_ref, rows_ref):
    outs, backs = split_pair(got_ref)
    mixed_ref[...] = dot(blend_ref[...], outs, 0, 0).astype(BF16)
    rows_ref[...] = dot(place_ref[...], backs, 0, 0).astype(BF16)


def swap(array, axis):
    return lax.all_to_all(array, axis, split_axis=0, concat_axis=0, tiled=True)


def gather_dp(array):
    return lax.all_to_all(
        jnp.broadcast_to(array[None], (lax.axis_size("dp"),) + array.shape),
        "dp",
        split_axis=0,
        concat_axis=0,
        tiled=True,
    )


def on_device(row_codes, scales, routes, mix_weights, w_gate, w_up, w_down, grad_out):
    owners = lax.axis_size("expert")
    shares = lax.axis_size("dp")
    tokens, features = row_codes.shape
    width = w_gate.shape[2]
    slots = owners * CAP
    share = slots // shares
    gate_w, up_w, down_w = w_gate[0], w_up[0], w_down[0]
    shape = jax.ShapeDtypeStruct
    one = 2 * slots * features * width
    send, place, blend = call(
        route_kernel,
        (
            shape((owners, 2 * CAP, features), BF16),
            shape((slots, tokens), BF16),
            shape((slots, tokens), BF16),
        ),
    )(routes.T, mix_weights.T, scales.T, row_codes, grad_out)
    got = swap(send, "expert")
    partials = call(partial_kernel, shape((shares, 3, share, width), BF16), 3 * one)(
        got, gate_w, up_w, down_w
    )
    summed = swap(partials, "dp")
    acts = gather_dp(call(gating_kernel, shape((3, share, width), BF16))(summed))
    back = swap(
        call(output_kernel, shape((owners, 2 * CAP, features), BF16), 3 * one)(
            acts, gate_w, up_w, down_w
        ),
        "expert",
    )
    grad_gate, grad_up, grad_down = call(
        weight_kernel,
        (
            shape((1, features, width), BF16),
            shape((1, features, width), BF16),
            shape((1, width, features), BF16),
        ),
        3 * one,
        6 * features * width,
    )(got, acts)
    mixed_out, grad_rows = call(
        combine_kernel, (shape((tokens, features), BF16), shape((tokens, features), BF16))
    )(back, place, blend)
    return mixed_out, grad_rows, grad_gate, grad_up, grad_down


def solution(mesh):
    placed = (
        P("expert", "dp"),
        P("expert", "dp"),
        P("expert", None),
        P("expert", None),
        P("expert", "dp", None),
        P("expert", "dp", None),
        P("expert", None, "dp"),
        P("expert", "dp"),
    )
    return jax.shard_map(
        on_device,
        mesh=mesh,
        in_specs=placed,
        out_specs=(
            P("expert", "dp"),
            P("expert", "dp"),
            P("expert", "dp", None),
            P("expert", "dp", None),
            P("expert", None, "dp"),
        ),
        check_vma=False,
    )
```

time: 142 us -> 67.3 us (0.47)
  waiting for transfers between devices: 35.4 us -> 3.43 us
  matrix products: 24.6 us -> 0 us
  starting transfers between devices: 19.5 us -> 3.41 us
  between operations: 13.9 us -> 0.69 us
  Pallas kernels: 0 us -> 8.93 us
  local copies, waits for them, and re-layouts: 2.5 us -> 8.77 us
  other arithmetic: 4.27 us -> 0 us
    all_to_all x0 -> x3, blocking collectives: none -> 41.5 us  [the longest x2 27.7 us: swap(): return lax.all_to_all(array, axis, split_axis=0, concat_axis=0, tiled=True)]
    all_gather x3 -> x0, blocking collectives: 41.2 us -> none  [the longest x1 13.8 us: on_device(): lax.all_gather(up_share.astype(jnp.bfloat16), 'dp', axis=0, tiled=True)]
    reduce_scatter x3 -> x0, waiting for transfers between devices: 25.2 us -> none  [the longest x1 17.2 us: on_device(): lax.psum_scatter(jnp.dot(expert_rows, up_w, preferred_element_type=jnp.fl...]
    dot_general x14 -> x0, matrix products: 24.6 us -> none  [the longest x3 6.24 us: contract_first(): lax.dot_general(left, right, (((0,), (0,)), ((), ())), preferred_element_...]
    all_to_all x5 -> x1, starting transfers between devices: 19.3 us -> 3.41 us  [swap(): return lax.all_to_all(array, axis, split_axis=0, concat_axis=0, tiled=True)]
    pallas_call x0 -> x6, Pallas kernels: none -> 8.93 us  [the longest x1 3.44 us: on_device(): call(weight_kernel, (shape((1, features, width), BF16), shape((1, feature...]
    unnamed x6 -> x22, local copies, waits for them, and re-layouts: 1 us -> 8.73 us
    all_to_all x5 -> x1, waiting for transfers between devices: 10.1 us -> 3.43 us  [swap(): return lax.all_to_all(array, axis, split_axis=0, concat_axis=0, tiled=True)]
  transfers between devices with their start and end apart: 8 -> 1, of which waited for: 6 -> 1; matrix products, arithmetic and copies ran while one was open for 17% -> 0% of each run, Pallas kernels for 0% -> 5%
where the time goes in v1:
time: 67.3 us; the launch traced here: 66.7 us
  blocking collectives  41.5 us (62%)
  Pallas kernels  8.93 us (13%)
  local copies, waits for them, and re-layouts  8.77 us (13%)
  waiting for transfers between devices  3.43 us (5%)
  starting transfers between devices  3.41 us (5%)
  between operations  0.69 us (1%)
    all_to_all x2, blocking collectives, swap(): return lax.all_to_all(array, axis, split_axis=0, concat_axis=0, tiled=True)  27.7 us
    all_to_all x1, blocking collectives, gather_dp(): lax.all_to_all(jnp.broadcast_to(array[None], (lax.axis_size('dp'),) + arr...  13.8 us
    unnamed x22, local copies, waits for them, and re-layouts  8.73 us
    pallas_call x1, Pallas kernels, on_device(): call(weight_kernel, (shape((1, features, width), BF16), shape((1, feature...  3.44 us
    all_to_all x1, waiting for transfers between devices, swap(): return lax.all_to_all(array, axis, split_axis=0, concat_axis=0, tiled=True)  3.43 us
    all_to_all x1, starting transfers between devices, swap(): return lax.all_to_all(array, axis, split_axis=0, concat_axis=0, tiled=True)  3.41 us
    pallas_call x1, Pallas kernels, on_device(): call(output_kernel, shape((owners, 2 * CAP, features), BF16), 3 * one)  2.46 us
    pallas_call x1, Pallas kernels, on_device(): call(partial_kernel, shape((shares, 3, share, width), BF16), 3 * one)  1.47 us
  transfers between devices with their start and end apart: 1, of which 1 were waited for; matrix products, arithmetic and copies ran while one was open for 0% of the time, Pallas kernels for 5%

profile of v1, /device:TPU:0, one launch (start us, length us, event | category | flops | bytes accessed | tf_op | source)
XLA Modules:
  0.0 66.7 jit_solution(6569585000697737578)
XLA Ops:
  0.6 0.0 copy-start.6
  0.6 0.9 %copy-done.6 = bf16[128,1024]{1,0:T(8,128)(2,1)S(1)} copy-done((bf16[128,1024]{1,0:T(8,128)(2,1)S(1)}, bf16[128,1024]{1,0:T(8,128)(2,1)}, u32[]{:S(2)}) %copy-start.6) | copy-done | bytes 262168
  1.6 0.0 copy-start.7
  1.6 0.9 %copy-done.7 = bf16[128,1024]{1,0:T(8,128)(2,1)S(1)} copy-done((bf16[128,1024]{1,0:T(8,128)(2,1)S(1)}, bf16[128,1024]{1,0:T(8,128)(2,1)}, u32[]{:S(2)}) %copy-start.7) | copy-done | bytes 262168
  2.5 0.0 copy-start.8
  2.5 0.7 %copy-done.8 = s32[128,8]{0,1:T(8,128)S(1)} copy-done((s32[128,8]{0,1:T(8,128)S(1)}, s32[128,8]{0,1:T(8,128)}, u32[]{:S(2)}) %copy-start.8) | copy-done | bytes 4120
  3.2 0.0 copy-start.9
  3.2 0.7 %copy-done.9 = f32[128,8]{0,1:T(8,128)S(1)} copy-done((f32[128,8]{0,1:T(8,128)S(1)}, f32[128,8]{0,1:T(8,128)}, u32[]{:S(2)}) %copy-start.9) | copy-done | bytes 4120
  3.9 0.0 copy-start.10
  3.9 0.7 %copy-done.10 = bf16[128,8]{0,1:T(8,128)(2,1)S(1)} copy-done((bf16[128,8]{0,1:T(8,128)(2,1)S(1)}, bf16[128,8]{0,1:T(8,128)(2,1)}, u32[]{:S(2)}) %copy-start.10) | copy-done | bytes 2072
  4.6 0.5 shard_map.119
  5.0 11.9 %all_to_all.20.got_ref = bf16[8,16,1024]{2,1,0:T(8,128)(2,1)S(1)} all-to-all(bf16[8,16,1024]{2,1,0:T(8,128)(2,1)S(1)} %get-tuple-element.13), channel_id=1, replica_groups=mesh['dp'=4,'expert'=8] {'expert'}, dimensions={0} | all-to-all | bytes 524288 | tf_op jit(solution)/shard_map/all_to_all | solution.py:131
  16.9 0.0 copy-start
  17.0 1.6 %copy-done = bf16[1,1024,1024]{2,1,0:T(8,128)(2,1)S(1)} copy-done((bf16[1,1024,1024]{2,1,0:T(8,128)(2,1)S(1)}, bf16[1,1024,1024]{2,1,0:T(8,128)(2,1)}, u32[]{:S(2)}) %copy-start) | copy-done | bytes 2097176
  18.5 1.6 %copy-done.2 = bf16[1,1024,1024]{2,1,0:T(8,128)(2,1)S(1)} copy-done((bf16[1,1024,1024]{2,1,0:T(8,128)(2,1)S(1)}, bf16[1,1024,1024]{2,1,0:T(8,128)(2,1)}, u32[]{:S(2)}) %copy-start.2) | copy-done | bytes 2097176
  20.1 0.0 copy-start.4
  20.1 1.6 %copy-done.4 = bf16[1,1024,1024]{2,1,0:T(8,128)(2,1)S(1)} copy-done((bf16[1,1024,1024]{2,1,0:T(8,128)(2,1)S(1)}, bf16[1,1024,1024]{2,1,0:T(8,128)(2,1)}, u32[]{:S(2)}) %copy-start.4) | copy-done | bytes 2097176
  21.7 0.0 copy-start.3
  21.7 0.0 copy-start.5
  21.7 1.5 %shard_map.120 = bf16[4,3,16,1024]{3,2,1,0:T(8,128)(2,1)S(1)} custom-call(bf16[8,16,1024]{2,1,0:T(8,128)(2,1)S(1)} %all_to_all.20.got_ref, bf16[1024,1024]{1,0:T(8,128)(2,1)S(1)} %bitcast.6, bf16[1024,1024]{1,0:T(8,128)(2,1)S(1)} %bitcast.8, bf16[1024,1024]{1,0:T(8,128)(2,1)S(1)} %bitcast.10), custom_call_target="tpu_custom_call" | custom-call | flops 402653184 | tf_op jit(solution)/shard_map/pallas_call | solution.py:163
  23.2 0.0 copy-start.1
  23.2 15.8 %all_to_all.21.got_ref = bf16[4,3,16,1024]{3,2,1,0:T(8,128)(2,1)S(1)} all-to-all(bf16[4,3,16,1024]{3,2,1,0:T(8,128)(2,1)S(1)} %shard_map.120), channel_id=1, replica_groups=mesh['dp'=4,'expert'=8] {'dp'}, dimensions={0} | all-to-all | bytes 786432 | tf_op jit(solution)/shard_map/all_to_all | solution.py:131
  39.0 0.1 shard_map.121
  39.2 13.8 %all_to_all.22.acts_ref = bf16[4,3,16,1024]{3,2,1,0:T(8,128)(2,1)S(1)} all-to-all(bf16[4,3,16,1024]{3,2,1,0:T(8,128)(2,1)S(1)} %broadcast_in_dim.2), channel_id=1, replica_groups=mesh['dp'=4,'expert'=8] {'dp'}, dimensions={0} | all-to-all | bytes 786432 | tf_op jit(solution)/shard_map/all_to_all | solution.py:135
  52.9 0.0 copy-done.3
  52.9 0.0 copy-done.5
  52.9 0.0 copy-done.1
  52.9 2.5 %shard_map.122 = bf16[8,16,1024]{2,1,0:T(8,128)(2,1)} custom-call(bf16[4,3,16,1024]{3,2,1,0:T(8,128)(2,1)S(1)} %all_to_all.22.acts_ref, bf16[1024,1024]{1,0:T(8,128)(2,1)S(1)} %bitcast.7, bf16[1024,1024]{1,0:T(8,128)(2,1)S(1)} %bitcast.9, bf16[1024,1024]{1,0:T(8,128)(2,1)S(1)} %bitcast.11), custom_call_target="tpu_custom_call" | custom-call | flops 402653184 | tf_op jit(solution)/shard_map/pallas_call | solution.py:169
  55.4 3.4 %all-to-all-start.3 = ((bf16[8,16,1024]{2,1,0:T(8,128)(2,1)}), bf16[8,16,1024]{2,1,0:T(8,128)(2,1)S(1)}, u32[]{:S(2)}, u32[]{:S(2)}) async-start(bf16[8,16,1024]{2,1,0:T(8,128)(2,1)} %shard_map.122), calls=%async_computation.3 | async-start | bytes 524288 | tf_op jit(solution)/shard_map/all_to_all | solution.py:131
  58.8 3.4 %shard_map.124 = (bf16[1,1024,1024]{2,1,0:T(8,128)(2,1)}, bf16[1,1024,1024]{2,1,0:T(8,128)(2,1)}, bf16[1,1024,1024]{2,1,0:T(8,128)(2,1)}) custom-call(bf16[8,16,1024]{2,1,0:T(8,128)(2,1)S(1)} %all_to_all.20.got_ref, bf16[4,3,16,1024]{3,2,1,0:T(8,128)(2,1)S(1)} %all_to_all.22.acts_ref), custom_call_target="tpu_custom_call" | custom-call | flops 402653184 | bytes 6291456 | tf_op jit(solution)/shard_map/pallas_call | solution.py:174
  62.3 3.4 %all-to-all-done.3.got_ref = bf16[8,16,1024]{2,1,0:T(8,128)(2,1)S(1)} async-done(((bf16[8,16,1024]{2,1,0:T(8,128)(2,1)}), bf16[8,16,1024]{2,1,0:T(8,128)(2,1)S(1)}, u32[]{:S(2)}, u32[]{:S(2)}) %all-to-all-start.3) | async-done | bytes 262176 | tf_op jit(solution)/shard_map/all_to_all | solution.py:131
  65.7 1.0 %shard_map.123 = (bf16[128,1024]{1,0:T(8,128)(2,1)}, bf16[128,1024]{1,0:T(8,128)(2,1)}) custom-call(bf16[8,16,1024]{2,1,0:T(8,128)(2,1)S(1)} %all-to-all-done.3.got_ref, bf16[64,128]{1,0:T(8,128)(2,1)S(1)} %get-tuple-element.14.place_ref, bf16[64,128]{1,0:T(8,128)(2,1)S(1)} %get-tuple-element.15.blend_ref), custom_call_target="tpu_custom_call" | custom-call | tf_op jit(solution)/shard_map/pallas_call | solution.py:184
  (2 shorter events, 0.0 us)
Async XLA Ops:
  0.6 1.0 %copy-start.6 = (bf16[128,1024]{1,0:T(8,128)(2,1)S(1)}, bf16[128,1024]{1,0:T(8,128)(2,1)}, u32[]{:S(2)}) copy-start(bf16[128,1024]{1,0:T(8,128)(2,1)} %codes_ref.1) | copy-start | bytes 786436
  1.6 0.9 %copy-start.7 = (bf16[128,1024]{1,0:T(8,128)(2,1)S(1)}, bf16[128,1024]{1,0:T(8,128)(2,1)}, u32[]{:S(2)}) copy-start(bf16[128,1024]{1,0:T(8,128)(2,1)} %grad_ref.1) | copy-start | bytes 786436
  2.5 0.7 %copy-start.8 = (s32[128,8]{0,1:T(8,128)S(1)}, s32[128,8]{0,1:T(8,128)}, u32[]{:S(2)}) copy-start(s32[128,8]{0,1:T(8,128)} %param.10) | copy-start | bytes 12292
  3.2 0.7 %copy-start.9 = (f32[128,8]{0,1:T(8,128)S(1)}, f32[128,8]{0,1:T(8,128)}, u32[]{:S(2)}) copy-start(f32[128,8]{0,1:T(8,128)} %param.11) | copy-start | bytes 12292
  3.9 0.7 %copy-start.10 = (bf16[128,8]{0,1:T(8,128)(2,1)S(1)}, bf16[128,8]{0,1:T(8,128)(2,1)}, u32[]{:S(2)}) copy-start(bf16[128,8]{0,1:T(8,128)(2,1)} %param.9) | copy-start | bytes 6148
  16.9 1.6 %copy-start = (bf16[1,1024,1024]{2,1,0:T(8,128)(2,1)S(1)}, bf16[1,1024,1024]{2,1,0:T(8,128)(2,1)}, u32[]{:S(2)}) copy-start(bf16[1,1024,1024]{2,1,0:T(8,128)(2,1)} %param.12) | copy-start | bytes 6291460
  18.5 1.6 %copy-start.2 = (bf16[1,1024,1024]{2,1,0:T(8,128)(2,1)S(1)}, bf16[1,1024,1024]{2,1,0:T(8,128)(2,1)}, u32[]{:S(2)}) copy-start(bf16[1,1024,1024]{2,1,0:T(8,128)(2,1)} %param.13) | copy-start | bytes 6291460
  20.1 1.6 %copy-start.4 = (bf16[1,1024,1024]{2,1,0:T(8,128)(2,1)S(1)}, bf16[1,1024,1024]{2,1,0:T(8,128)(2,1)}, u32[]{:S(2)}) copy-start(bf16[1,1024,1024]{2,1,0:T(8,128)(2,1)} %param.14) | copy-start | bytes 6291460
  21.7 31.2 %copy-start.3 = (bf16[1,1024,1024]{2,1,0:T(8,128)(2,1)S(1)}, bf16[1,1024,1024]{2,1,0:T(8,128)(2,1)}, u32[]{:S(2)}) copy-start(bf16[1,1024,1024]{2,1,0:T(8,128)(2,1)} %param.13) | copy-start | bytes 6291460
  21.7 31.2 %copy-start.5 = (bf16[1,1024,1024]{2,1,0:T(8,128)(2,1)S(1)}, bf16[1,1024,1024]{2,1,0:T(8,128)(2,1)}, u32[]{:S(2)}) copy-start(bf16[1,1024,1024]{2,1,0:T(8,128)(2,1)} %param.14) | copy-start | bytes 6291460
  23.2 29.7 %copy-start.1 = (bf16[1,1024,1024]{2,1,0:T(8,128)(2,1)S(1)}, bf16[1,1024,1024]{2,1,0:T(8,128)(2,1)}, u32[]{:S(2)}) copy-start(bf16[1,1024,1024]{2,1,0:T(8,128)(2,1)} %param.12) | copy-start | bytes 6291460
  55.4 10.3 %all-to-all-start.3 = ((bf16[8,16,1024]{2,1,0:T(8,128)(2,1)}), bf16[8,16,1024]{2,1,0:T(8,128)(2,1)S(1)}, u32[]{:S(2)}, u32[]{:S(2)}) async-start(bf16[8,16,1024]{2,1,0:T(8,128)(2,1)} %shard_map.122), calls=%async_computation.3 | async-start | bytes 524288 | tf_op jit(solution)/shard_map/all_to_all | solution.py:131

commit v2 on v1

v2 whole, which is shorter than its diff:
```python
import jax
import jax.numpy as jnp
from jax import lax
from jax.experimental import pallas as pl
from jax.experimental.pallas import tpu as pltpu
from jax.sharding import PartitionSpec as P

CAP = 8
CORES = 2
F32 = jnp.float32
BF16 = jnp.bfloat16
VMEM_SPEC = pl.BlockSpec(memory_space=pltpu.VMEM)
HBM_SPEC = pl.BlockSpec(memory_space=pltpu.HBM)


def dot(left, right, left_dim, right_dim):
    return lax.dot_general(
        left, right, (((left_dim,), (right_dim,)), ((), ())), preferred_element_type=F32
    )


def call(kernel, out_shape, in_specs=None, scratch=(), flops=0, bytes_accessed=0, mib=8):
    many = isinstance(out_shape, (tuple, list))

    def run(*args):
        return pl.pallas_call(
            kernel,
            out_shape=out_shape,
            in_specs=in_specs or [VMEM_SPEC] * len(args),
            out_specs=[VMEM_SPEC] * len(out_shape) if many else VMEM_SPEC,
            scratch_shapes=scratch,
            compiler_params=pltpu.CompilerParams(vmem_limit_bytes=mib << 20),
            cost_estimate=pl.CostEstimate(
                flops=flops, bytes_accessed=bytes_accessed, transcendentals=0
            ),
        )(*args)

    return run


def in_hbm(array):
    return pltpu.with_memory_space_constraint(array, pltpu.HBM)


def load_all(sources, targets, sems):
    copies = [
        pltpu.make_async_copy(source, target, sems.at[i])
        for i, (source, target) in enumerate(zip(sources, targets))
    ]
    for copy in copies:
        copy.start()
    return copies


def route_kernel(
    routes_hbm, mix_hbm, scales_hbm, codes_hbm, grad_hbm,
    mine_ref, theirs_ref, place_ref, blend_ref,
    routes_ref, mix_ref, scales_ref, codes_ref, grad_ref, sems,
):
    copies = load_all(
        (routes_hbm, mix_hbm, scales_hbm, codes_hbm, grad_hbm),
        (routes_ref, mix_ref, scales_ref, codes_ref, grad_ref),
        sems,
    )
    owners = CORES * mine_ref.shape[0]
    picks, tokens = routes_ref.shape
    slots = owners * CAP
    ids = lax.broadcasted_iota(jnp.int32, (owners, tokens), 0) ^ lax.axis_index("expert")
    match = jnp.zeros((owners, tokens), F32)
    weight = jnp.zeros((owners, tokens), F32)
    copies[0].wait()
    copies[1].wait()
    for k in range(picks):
        hit = routes_ref[k : k + 1, :] == ids
        match = jnp.where(hit, 1.0, match)
        weight = jnp.where(hit, mix_ref[k : k + 1, :], weight)
    before = (
        lax.broadcasted_iota(jnp.int32, (tokens, tokens), 0)
        < lax.broadcasted_iota(jnp.int32, (tokens, tokens), 1)
    ).astype(BF16)
    rank = dot(match.astype(BF16), before, 1, 0).astype(jnp.int32)
    rank = jnp.where(match > 0.0, rank, -1)
    position = lax.broadcasted_iota(jnp.int32, (owners, CAP, tokens), 1)
    taken = (rank[:, None, :] == position).reshape(slots, tokens)
    weights = jnp.broadcast_to(weight[:, None, :], (owners, CAP, tokens)).reshape(slots, tokens)
    blend = jnp.where(taken, weights, 0.0)
    place = jnp.where(taken, 1.0, 0.0).astype(BF16)
    place_ref[...] = place
    blend_ref[...] = blend.astype(BF16)
    slot_weight = jnp.sum(blend, axis=1, keepdims=True)
    copies[2].wait()
    slot_scale = dot(place, scales_ref[...], 1, 1)
    copies[3].wait()
    codes = dot(place, codes_ref[...], 1, 0)
    features = codes.shape[1]
    groups = scales_ref.shape[0]
    width = features // groups
    rows = jnp.concatenate(
        [codes[:, g * width : (g + 1) * width] * slot_scale[:, g : g + 1] for g in range(groups)],
        axis=1,
    )
    copies[4].wait()
    grads = dot(place, grad_ref[...], 1, 0) * slot_weight
    store_pairs(rows, grads, mine_ref, theirs_ref)


def store_pairs(first, second, mine_ref, theirs_ref):
    chips, _, features = mine_ref.shape
    both = jnp.concatenate(
        [
            first.reshape(chips, CORES, CAP, features),
            second.reshape(chips, CORES, CAP, features),
        ],
        axis=2,
    ).astype(BF16)
    mine_ref[...] = both[:, 0]
    theirs_ref[...] = both[:, 1]


def pack_kernel(mine_ref, got_ref, *outs):
    for k, out in enumerate(outs):
        out[0] = mine_ref[k]
        out[1] = got_ref[k]


def fetch_kernel(after_hbm, gate_hbm, up_hbm, down_hbm, gate_ref, up_ref, down_ref, sems):
    for copy in load_all((gate_hbm, up_hbm, down_hbm), (gate_ref, up_ref, down_ref), sems):
        copy.wait()


def unpack(blocks):
    count, _, features = blocks.shape
    wide = blocks.astype(F32).reshape(count, 2, CAP, features)
    return (
        wide[:, 0].reshape(count * CAP, features).astype(BF16),
        wide[:, 1].reshape(count * CAP, features).astype(BF16),
    )


def partial_kernel(*refs, shares):
    blocks_ref = refs[-1]
    sends = refs[-1 - shares - 2 : -3]
    rows_ref, grads_ref = refs[-3:-1]
    gate_ref, up_ref, down_ref = refs[-1 - shares - 5 : -1 - shares - 2]
    got = refs[: -1 - shares - 5]
    for k, ref in enumerate(got):
        blocks_ref[CORES * k : CORES * k + CORES] = ref[...]
    owners = blocks_ref.shape[0]
    step = owners // shares
    me = lax.axis_index("dp")
    rows, grads = unpack(
        jnp.concatenate([blocks_ref[pl.ds((me ^ s) * step, step)] for s in range(shares)], axis=0)
    )
    rows_ref[...] = rows
    grads_ref[...] = grads
    share = step * CAP
    for i, part in enumerate(
        (
            dot(rows, gate_ref[...], 1, 0),
            dot(rows, up_ref[...], 1, 0),
            dot(grads, down_ref[...], 1, 1),
        )
    ):
        for s, send in enumerate(sends):
            send[i] = part[s * share : (s + 1) * share].astype(BF16)


def gating_kernel(*refs):
    parts, out_ref = refs[:-1], refs[-1]
    gate, up, hidden_grad = (sum(part[i].astype(F32) for part in parts) for i in range(3))
    sig = jax.nn.sigmoid(gate)
    silu = gate * sig
    out_ref[0] = (silu * up).astype(BF16)
    out_ref[1] = (hidden_grad * up * sig * (1.0 + gate * (1.0 - sig))).astype(BF16)
    out_ref[2] = (hidden_grad * silu).astype(BF16)


def output_kernel(*refs):
    (gate_ref, up_ref, down_ref), acts = refs[:3], refs[3:-3]
    mine_ref, theirs_ref, blocks_ref = refs[-3:]
    owners, _, features = blocks_ref.shape
    step = owners // len(acts)
    hidden, gate_grad, up_grad = (jnp.concatenate([a[i] for a in acts], axis=0) for i in range(3))
    out = dot(hidden, down_ref[...], 1, 0)
    back = dot(gate_grad, gate_ref[...], 1, 1) + dot(up_grad, up_ref[...], 1, 1)
    both = jnp.concatenate(
        [out.reshape(owners, CAP, features), back.reshape(owners, CAP, features)], axis=1
    ).astype(BF16)
    me = lax.axis_index("dp")
    for s in range(len(acts)):
        blocks_ref[pl.ds((me ^ s) * step, step)] = both[s * step : (s + 1) * step]
    for k in range(owners // CORES):
        mine_ref[k] = blocks_ref[CORES * k]
        theirs_ref[k] = blocks_ref[CORES * k + 1]


def weight_kernel(*refs):
    (rows_ref, grads_ref), acts = refs[:2], refs[2:-3]
    gate_ref, up_ref, down_ref = refs[-3:]
    rows, grads = rows_ref[...], grads_ref[...]
    hidden, gate_grad, up_grad = (jnp.concatenate([a[i] for a in acts], axis=0) for i in range(3))
    gate_ref[0] = dot(rows, gate_grad, 0, 0).astype(BF16)
    up_ref[0] = dot(rows, up_grad, 0, 0).astype(BF16)
    down_ref[0] = dot(hidden, grads, 0, 0).astype(BF16)


def combine_kernel(*refs):
    got, (place_ref, blend_ref, mixed_ref, rows_ref) = refs[:-4], refs[-4:]
    outs, backs = unpack(jnp.concatenate([ref[...] for ref in got], axis=0))
    mixed_ref[...] = dot(blend_ref[...], outs, 0, 0).astype(BF16)
    rows_ref[...] = dot(place_ref[...], backs, 0, 0).astype(BF16)


def trade(array, axis, distance):
    count = lax.axis_size(axis)
    return lax.ppermute(array, axis, [(i, i ^ distance) for i in range(count)])


def swap(mine, theirs):
    chips, rows, features = mine.shape
    got = trade(theirs, "expert", 1)
    packed = call(
        pack_kernel, (jax.ShapeDtypeStruct((CORES, rows, features), BF16),) * chips
    )(mine, got)
    return [packed[0]] + [trade(packed[k], "expert", CORES * k) for k in range(1, chips)]


def on_device(row_codes, scales, routes, mix_weights, w_gate, w_up, w_down, grad_out):
    owners = lax.axis_size("expert")
    shares = lax.axis_size("dp")
    chips = owners // CORES
    tokens, features = row_codes.shape
    width = w_gate.shape[2]
    slots = owners * CAP
    share = slots // shares
    shape = jax.ShapeDtypeStruct
    one = 2 * slots * features * width
    half = shape((chips, 2 * CAP, features), BF16)
    blocks = pltpu.VMEM((owners, 2 * CAP, features), BF16)
    loads = tuple(
        in_hbm(x) for x in (routes.T, mix_weights.T, scales.T, row_codes, grad_out)
    )
    mine, theirs, place, blend = call(
        route_kernel,
        (half, half, shape((slots, tokens), BF16), shape((slots, tokens), BF16)),
        in_specs=[HBM_SPEC] * 5,
        scratch=[pltpu.VMEM(x.shape, x.dtype) for x in loads] + [pltpu.SemaphoreType.DMA((5,))],
    )(*loads)
    got = swap(mine, theirs)
    weights = tuple(in_hbm(w[0]) for w in (w_gate, w_up, w_down))
    weights = call(
        fetch_kernel,
        tuple(pltpu.VMEM(w.shape, w.dtype) for w in weights),
        in_specs=[HBM_SPEC] * 4,
        scratch=[pltpu.SemaphoreType.DMA((3,))],
        bytes_accessed=6 * features * width,
    )(got[0], *weights)
    *partials, rows, grads = call(
        lambda *refs: partial_kernel(*refs, shares=shares),
        (shape((3, share, width), BF16),) * shares + (shape((slots, features), BF16),) * 2,
        scratch=[blocks],
        flops=3 * one,
    )(*got, *weights)
    summed = [partials[0]] + [trade(partials[s], "dp", s) for s in range(1, shares)]
    act = call(gating_kernel, shape((3, share, width), BF16))(*summed)
    acts = [act] + [trade(act, "dp", s) for s in range(1, shares)]
    back = swap(
        *call(output_kernel, (half, half), scratch=[blocks], flops=3 * one)(*weights, *acts)
    )
    grad_gate, grad_up, grad_down = call(
        weight_kernel,
        (
            shape((1, features, width), BF16),
            shape((1, features, width), BF16),
            shape((1, width, features), BF16),
        ),
        flops=3 * one,
        bytes_accessed=6 * features * width,
        mib=16,
    )(rows, grads, *acts)
    mixed_out, grad_rows = call(
        combine_kernel, (shape((tokens, features), BF16), shape((tokens, features), BF16))
    )(*back, place, blend)
    return mixed_out, grad_rows, grad_gate, grad_up, grad_down


def solution(mesh):
    placed = (
        P("expert", "dp"),
        P("expert", "dp"),
        P("expert", None),
        P("expert", None),
        P("expert", "dp", None),
        P("expert", "dp", None),
        P("expert", None, "dp"),
        P("expert", "dp"),
    )
    return jax.shard_map(
        on_device,
        mesh=mesh,
        in_specs=placed,
        out_specs=(
            P("expert", "dp"),
            P("expert", "dp"),
            P("expert", "dp", None),
            P("expert", "dp", None),
            P("expert", None, "dp"),
        ),
        check_vma=False,
    )
```

time: 67.3 us -> 47.8 us (0.71)
  blocking collectives: 41.5 us -> 0 us
  starting transfers between devices: 3.41 us -> 17.5 us
  waiting for transfers between devices: 3.43 us -> 17.2 us
  local copies, waits for them, and re-layouts: 8.77 us -> 0 us
  Pallas kernels: 8.93 us -> 12.2 us
    all_to_all x3 -> x0, blocking collectives: 41.5 us -> none  [the longest x2 27.7 us: swap(): return lax.all_to_all(array, axis, split_axis=0, concat_axis=0, tiled=True)]
    ppermute x0 -> x14, starting transfers between devices: none -> 17.5 us  [trade(): return lax.ppermute(array, axis, [(i, i ^ distance) for i in range(count)])]
    ppermute x0 -> x14, waiting for transfers between devices: none -> 17.2 us  [trade(): return lax.ppermute(array, axis, [(i, i ^ distance) for i in range(count)])]
    unnamed x22 -> x0, local copies, waits for them, and re-layouts: 8.73 us -> none
    all_to_all x1 -> x0, waiting for transfers between devices: 3.43 us -> none  [swap(): return lax.all_to_all(array, axis, split_axis=0, concat_axis=0, tiled=True)]
    all_to_all x1 -> x0, starting transfers between devices: 3.41 us -> none  [swap(): return lax.all_to_all(array, axis, split_axis=0, concat_axis=0, tiled=True)]
    pallas_call x6 -> x9, Pallas kernels: 8.93 us -> 12.2 us  [run(): pl.pallas_call(kernel, out_shape=out_shape, in_specs=in_specs or [VMEM_SP...]
  transfers between devices with their start and end apart: 1 -> 14, of which waited for: 1 -> 9; matrix products, arithmetic and copies ran while one was open for 0% -> 0% of each run, Pallas kernels for 5% -> 13%
where the time goes in v2:
time: 47.8 us; the launch traced here: 47.6 us
  starting transfers between devices  17.5 us (37%)
  waiting for transfers between devices  17.2 us (36%)
  Pallas kernels  12.2 us (26%)
  between operations  0.71 us (1%)
    ppermute x14, starting transfers between devices, trade(): return lax.ppermute(array, axis, [(i, i ^ distance) for i in range(count)])  17.5 us
    ppermute x14, waiting for transfers between devices, trade(): return lax.ppermute(array, axis, [(i, i ^ distance) for i in range(count)])  17.2 us
    pallas_call x9, Pallas kernels, run(): pl.pallas_call(kernel, out_shape=out_shape, in_specs=in_specs or [VMEM_SP...  12.2 us
  transfers between devices with their start and end apart: 14, of which 9 were waited for; matrix products, arithmetic and copies ran while one was open for 0% of the time, Pallas kernels for 13%

profile of v2, /device:TPU:0, one launch (start us, length us, event | category | flops | bytes accessed | tf_op | source)
XLA Modules:
  0.0 47.6 jit_solution(9862206780110027724)
XLA Ops:
  0.6 1.5 %shard_map.119 = (bf16[4,16,1024]{2,1,0:T(8,128)(2,1)S(1)}, bf16[4,16,1024]{2,1,0:T(8,128)(2,1)S(1)}, bf16[64,128]{1,0:T(8,128)(2,1)S(1)}, bf16[64,128]{1,0:T(8,128)(2,1)S(1)}) custom-call(s32[8,128]{1,0:T(8,128)} %bitcast.9, f32[8,128]{1,0:T(8,128)} %bitcast.10, bf16[8,128]{1,0:T(8,128)(2,1)} %bitcast.11, bf16[128,1024]{1,0:T(8,128)(2,1)} %codes_hbm.1, ...), custom_call_target="tpu_custom_call" | custom-call | tf_op jit(solution)/shard_map/pallas_call | solution.py:26
  2.1 0.5 %collective-permute-start = (bf16[4,16,1024]{2,1,0:T(8,128)(2,1)S(1)}, bf16[4,16,1024]{2,1,0:T(8,128)(2,1)S(1)}, u32[]{:S(2)}, u32[]{:S(2)}) collective-permute-start(bf16[4,16,1024]{2,1,0:T(8,128)(2,1)S(1)} %get-tuple-element.34), channel_id=1, source_target_pairs={{0,1},{1,0},{2,3},{3,2},{4,5},{5,4},{6,7},{7,6},{8,9},{9,8},{10,11... | collective-permute-start | bytes 393224 | tf_op jit(solution)/shard_map/ppermute | solution.py:216
  2.6 1.0 %collective-permute-done.got_ref = bf16[4,16,1024]{2,1,0:T(8,128)(2,1)S(1)} collective-permute-done((bf16[4,16,1024]{2,1,0:T(8,128)(2,1)S(1)}, bf16[4,16,1024]{2,1,0:T(8,128)(2,1)S(1)}, u32[]{:S(2)}, u32[]{:S(2)}) %collective-permute-start) | collective-permute-done | bytes 131104 | tf_op jit(solution)/shard_map/ppermute | solution.py:216
  3.6 2.9 %collective-permute-start.1 = (bf16[2,16,1024]{2,1,0:T(8,128)(2,1)S(1)}, bf16[2,16,1024]{2,1,0:T(8,128)(2,1)S(1)}, u32[]{:S(2)}, u32[]{:S(2)}) collective-permute-start(bf16[2,16,1024]{2,1,0:T(8,128)(2,1)S(1)} %get-tuple-element.39), channel_id=1, source_target_pairs={{0,2},{1,3},{2,0},{3,1},{4,6},{5,7},{6,4},{7,5},{8,10},{9,11},{10,... | collective-permute-start | bytes 196616 | tf_op jit(solution)/shard_map/ppermute | solution.py:216
  6.5 1.5 %collective-permute-start.2 = (bf16[2,16,1024]{2,1,0:T(8,128)(2,1)S(1)}, bf16[2,16,1024]{2,1,0:T(8,128)(2,1)S(1)}, u32[]{:S(2)}, u32[]{:S(2)}) collective-permute-start(bf16[2,16,1024]{2,1,0:T(8,128)(2,1)S(1)} %get-tuple-element.40), channel_id=1, source_target_pairs={{0,4},{1,5},{2,6},{3,7},{4,0},{5,1},{6,2},{7,3},{8,12},{9,13},{10,... | collective-permute-start | bytes 196616 | tf_op jit(solution)/shard_map/ppermute | solution.py:216
  8.1 0.0 collective-permute-start.3
  8.1 2.9 %shard_map.121 = (bf16[1024,1024]{1,0:T(8,128)(2,1)S(1)}, bf16[1024,1024]{1,0:T(8,128)(2,1)S(1)}, bf16[1024,1024]{1,0:T(8,128)(2,1)S(1)}) custom-call(bf16[2,16,1024]{2,1,0:T(8,128)(2,1)S(1)} %get-tuple-element.35.after_hbm.refs_0_, bf16[1024,1024]{1,0:T(8,128)(2,1)} %bitcast.6, bf16[1024,1024]{1,0:T(8,128)(2,1)} %bitcast.7, bf16[1024,1024]{1,0:T(8,128)(2,1)} %bitcast.8), custom_call_target="tpu_custom_call" | custom-call | bytes 6291456 | tf_op jit(solution)/shard_map/pallas_call | solution.py:26
  11.0 0.0 collective-permute-done.1.refs_1_
  11.0 2.2 %collective-permute-done.3.refs_3_ = bf16[2,16,1024]{2,1,0:T(8,128)(2,1)S(1)} collective-permute-done((bf16[2,16,1024]{2,1,0:T(8,128)(2,1)S(1)}, bf16[2,16,1024]{2,1,0:T(8,128)(2,1)S(1)}, u32[]{:S(2)}, u32[]{:S(2)}) %collective-permute-start.3) | collective-permute-done | bytes 65568 | tf_op jit(solution)/shard_map/ppermute | solution.py:216
  13.2 1.5 %shard_map.122 = (bf16[3,16,1024]{2,1,0:T(8,128)(2,1)S(1)}, bf16[3,16,1024]{2,1,0:T(8,128)(2,1)S(1)}, bf16[3,16,1024]{2,1,0:T(8,128)(2,1)S(1)}, bf16[3,16,1024]{...) custom-call(bf16[2,16,1024]{2,1,0:T(8,128)(2,1)S(1)} %get-tuple-element.35.after_hbm.refs_0_, ...), custom_call_target="tpu_custom_call" | custom-call | flops 402653184 | tf_op jit(solution)/shard_map/pallas_call | solution.py:26
  14.7 1.6 %collective-permute-start.4 = (bf16[3,16,1024]{2,1,0:T(8,128)(2,1)S(1)}, bf16[3,16,1024]{2,1,0:T(8,128)(2,1)S(1)}, u32[]{:S(2)}, u32[]{:S(2)}) collective-permute-start(bf16[3,16,1024]{2,1,0:T(8,128)(2,1)S(1)} %get-tuple-element.43), channel_id=1, source_target_pairs={{0,8},{8,0},{16,24},{24,16},{1,9},{9,1},{17,25},{25,17},{2,10},{10... | collective-permute-start | bytes 294920 | tf_op jit(solution)/shard_map/ppermute | solution.py:216
  16.4 2.6 %collective-permute-start.5 = (bf16[3,16,1024]{2,1,0:T(8,128)(2,1)S(1)}, bf16[3,16,1024]{2,1,0:T(8,128)(2,1)S(1)}, u32[]{:S(2)}, u32[]{:S(2)}) collective-permute-start(bf16[3,16,1024]{2,1,0:T(8,128)(2,1)S(1)} %get-tuple-element.44), channel_id=1, source_target_pairs={{0,16},{8,24},{16,0},{24,8},{1,17},{9,25},{17,1},{25,9},{2,18},{10... | collective-permute-start | bytes 294920 | tf_op jit(solution)/shard_map/ppermute | solution.py:216
  18.9 0.2 collective-permute-start.6
  19.2 0.9 %collective-permute-done.4.refs_1_ = bf16[3,16,1024]{2,1,0:T(8,128)(2,1)S(1)} collective-permute-done((bf16[3,16,1024]{2,1,0:T(8,128)(2,1)S(1)}, bf16[3,16,1024]{2,1,0:T(8,128)(2,1)S(1)}, u32[]{:S(2)}, u32[]{:S(2)}) %collective-permute-start.4) | collective-permute-done | bytes 98336 | tf_op jit(solution)/shard_map/ppermute | solution.py:216
  20.0 4.3 %collective-permute-done.5.refs_2_ = bf16[3,16,1024]{2,1,0:T(8,128)(2,1)S(1)} collective-permute-done((bf16[3,16,1024]{2,1,0:T(8,128)(2,1)S(1)}, bf16[3,16,1024]{2,1,0:T(8,128)(2,1)S(1)}, u32[]{:S(2)}, u32[]{:S(2)}) %collective-permute-start.5) | collective-permute-done | bytes 98336 | tf_op jit(solution)/shard_map/ppermute | solution.py:216
  24.3 1.1 %collective-permute-done.6.refs_3_ = bf16[3,16,1024]{2,1,0:T(8,128)(2,1)S(1)} collective-permute-done((bf16[3,16,1024]{2,1,0:T(8,128)(2,1)S(1)}, bf16[3,16,1024]{2,1,0:T(8,128)(2,1)S(1)}, u32[]{:S(2)}, u32[]{:S(2)}) %collective-permute-start.6) | collective-permute-done | bytes 98336 | tf_op jit(solution)/shard_map/ppermute | solution.py:216
  25.5 0.1 shard_map.123.refs_3_.refs_2_
  25.5 2.5 %collective-permute-start.9 = (bf16[3,16,1024]{2,1,0:T(8,128)(2,1)S(1)}, bf16[3,16,1024]{2,1,0:T(8,128)(2,1)S(1)}, u32[]{:S(2)}, u32[]{:S(2)}) collective-permute-start(bf16[3,16,1024]{2,1,0:T(8,128)(2,1)S(1)} %shard_map.123.refs_3_.refs_2_), channel_id=1, source_target_pairs={{0,24},{8,16},{16,8},{24,0},{1,25},{9,17},{17,9},{25,1},{2,26},{10... | collective-permute-start | bytes 294920 | tf_op jit(solution)/shard_map/ppermute | solution.py:216
  28.0 0.6 %collective-permute-start.8 = (bf16[3,16,1024]{2,1,0:T(8,128)(2,1)S(1)}, bf16[3,16,1024]{2,1,0:T(8,128)(2,1)S(1)}, u32[]{:S(2)}, u32[]{:S(2)}) collective-permute-start(bf16[3,16,1024]{2,1,0:T(8,128)(2,1)S(1)} %shard_map.123.refs_3_.refs_2_), channel_id=1, source_target_pairs={{0,16},{8,24},{16,0},{24,8},{1,17},{9,25},{17,1},{25,9},{2,18},{10... | collective-permute-start | bytes 294920 | tf_op jit(solution)/shard_map/ppermute | solution.py:216
  28.6 1.4 %collective-permute-start.7 = (bf16[3,16,1024]{2,1,0:T(8,128)(2,1)S(1)}, bf16[3,16,1024]{2,1,0:T(8,128)(2,1)S(1)}, u32[]{:S(2)}, u32[]{:S(2)}) collective-permute-start(bf16[3,16,1024]{2,1,0:T(8,128)(2,1)S(1)} %shard_map.123.refs_3_.refs_2_), channel_id=1, source_target_pairs={{0,8},{8,0},{16,24},{24,16},{1,9},{9,1},{17,25},{25,17},{2,10},{10... | collective-permute-start | bytes 294920 | tf_op jit(solution)/shard_map/ppermute | solution.py:216
  30.0 2.7 %collective-permute-done.9.refs_6_.refs_5_ = bf16[3,16,1024]{2,1,0:T(8,128)(2,1)S(1)} collective-permute-done((bf16[3,16,1024]{2,1,0:T(8,128)(2,1)S(1)}, bf16[3,16,1024]{2,1,0:T(8,128)(2,1)S(1)}, u32[]{:S(2)}, u32[]{:S(2)}) %collective-permute-start.9) | collective-permute-done | bytes 98336 | tf_op jit(solution)/shard_map/ppermute | solution.py:216
  32.7 2.7 %collective-permute-done.8.refs_5_.refs_4_ = bf16[3,16,1024]{2,1,0:T(8,128)(2,1)S(1)} collective-permute-done((bf16[3,16,1024]{2,1,0:T(8,128)(2,1)S(1)}, bf16[3,16,1024]{2,1,0:T(8,128)(2,1)S(1)}, u32[]{:S(2)}, u32[]{:S(2)}) %collective-permute-start.8) | collective-permute-done | bytes 98336 | tf_op jit(solution)/shard_map/ppermute | solution.py:216
  35.4 1.8 %shard_map.124 = (bf16[4,16,1024]{2,1,0:T(8,128)(2,1)S(1)}, bf16[4,16,1024]{2,1,0:T(8,128)(2,1)S(1)}) custom-call(bf16[1024,1024]{1,0:T(8,128)(2,1)S(1)} %get-tuple-element.36.refs_4_.refs_0_, bf16[1024,1024]{1,0:T(8,128)(2,1)S(1)} %get-tuple-element.37.refs_5_.refs_1_, bf16[1024,1024]{1,0:T(8,128)(2,1)S(1)} %get-tuple-element.38.refs_6_.refs_2_, ...), custom_call_target="tpu_custom_call" | custom-call | flops 402653184 | tf_op jit(solution)/shard_map/pallas_call | solution.py:26
  37.2 0.1 collective-permute-start.10
  37.2 1.3 %collective-permute-done.10.got_ref = bf16[4,16,1024]{2,1,0:T(8,128)(2,1)S(1)} collective-permute-done((bf16[4,16,1024]{2,1,0:T(8,128)(2,1)S(1)}, bf16[4,16,1024]{2,1,0:T(8,128)(2,1)S(1)}, u32[]{:S(2)}, u32[]{:S(2)}) %collective-permute-start.10) | collective-permute-done | bytes 131104 | tf_op jit(solution)/shard_map/ppermute | solution.py:216
  38.6 0.7 %collective-permute-start.11 = (bf16[2,16,1024]{2,1,0:T(8,128)(2,1)S(1)}, bf16[2,16,1024]{2,1,0:T(8,128)(2,1)S(1)}, u32[]{:S(2)}, u32[]{:S(2)}) collective-permute-start(bf16[2,16,1024]{2,1,0:T(8,128)(2,1)S(1)} %get-tuple-element.49), channel_id=1, source_target_pairs={{0,2},{1,3},{2,0},{3,1},{4,6},{5,7},{6,4},{7,5},{8,10},{9,11},{10,... | collective-permute-start | bytes 196616 | tf_op jit(solution)/shard_map/ppermute | solution.py:216
  39.3 2.1 %collective-permute-start.12 = (bf16[2,16,1024]{2,1,0:T(8,128)(2,1)S(1)}, bf16[2,16,1024]{2,1,0:T(8,128)(2,1)S(1)}, u32[]{:S(2)}, u32[]{:S(2)}) collective-permute-start(bf16[2,16,1024]{2,1,0:T(8,128)(2,1)S(1)} %get-tuple-element.50), channel_id=1, source_target_pairs={{0,4},{1,5},{2,6},{3,7},{4,0},{5,1},{6,2},{7,3},{8,12},{9,13},{10,... | collective-permute-start | bytes 196616 | tf_op jit(solution)/shard_map/ppermute | solution.py:216
  41.4 0.8 %collective-permute-start.13 = (bf16[2,16,1024]{2,1,0:T(8,128)(2,1)S(1)}, bf16[2,16,1024]{2,1,0:T(8,128)(2,1)S(1)}, u32[]{:S(2)}, u32[]{:S(2)}) collective-permute-start(bf16[2,16,1024]{2,1,0:T(8,128)(2,1)S(1)} %get-tuple-element.51), channel_id=1, source_target_pairs={{0,6},{1,7},{2,4},{3,5},{4,2},{5,3},{6,0},{7,1},{8,14},{9,15},{10,... | collective-permute-start | bytes 196616 | tf_op jit(solution)/shard_map/ppermute | solution.py:216
  42.1 3.4 %shard_map.127 = (bf16[1,1024,1024]{2,1,0:T(8,128)(2,1)}, bf16[1,1024,1024]{2,1,0:T(8,128)(2,1)}, bf16[1,1024,1024]{2,1,0:T(8,128)(2,1)}) custom-call(bf16[64,1024]{1,0:T(8,128)(2,1)S(1)} %get-tuple-element.56.refs_0_, bf16[64,1024]{1,0:T(8,128)(2,1)S(1)} %get-tuple-element.57.refs_1_, bf16[3,16,1024]{2,1,0:T(8,128)(2,1)S(1)} %shard_map.123.refs_3_.refs_2_, ...), custom_call_target="tpu_custom_call" | custom-call | flops 402653184 | bytes 6291456 | tf_op jit(solution)/shard_map/pallas_call | solution.py:26
  45.6 0.0 collective-permute-done.11.refs_1_
  45.6 1.0 %collective-permute-done.13.refs_3_ = bf16[2,16,1024]{2,1,0:T(8,128)(2,1)S(1)} collective-permute-done((bf16[2,16,1024]{2,1,0:T(8,128)(2,1)S(1)}, bf16[2,16,1024]{2,1,0:T(8,128)(2,1)S(1)}, u32[]{:S(2)}, u32[]{:S(2)}) %collective-permute-start.13) | collective-permute-done | bytes 65568 | tf_op jit(solution)/shard_map/ppermute | solution.py:216
  46.5 1.0 %shard_map.126 = (bf16[128,1024]{1,0:T(8,128)(2,1)}, bf16[128,1024]{1,0:T(8,128)(2,1)}) custom-call(bf16[2,16,1024]{2,1,0:T(8,128)(2,1)S(1)} %get-tuple-element.48.refs_0_, bf16[2,16,1024]{2,1,0:T(8,128)(2,1)S(1)} %collective-permute-done.11.refs_1_, bf16[2,16,1024]{2,1,0:T(8,128)(2,1)S(1)} %collective-permute-done.12.refs_2_, ...), custom_call_target="tpu_custom_call" | custom-call | tf_op jit(solution)/shard_map/pallas_call | solution.py:26
  (5 shorter events, 0.0 us)
Async XLA Ops:
  2.1 1.5 %collective-permute-start = (bf16[4,16,1024]{2,1,0:T(8,128)(2,1)S(1)}, bf16[4,16,1024]{2,1,0:T(8,128)(2,1)S(1)}, u32[]{:S(2)}, u32[]{:S(2)}) collective-permute-start(bf16[4,16,1024]{2,1,0:T(8,128)(2,1)S(1)} %get-tuple-element.34), channel_id=1, source_target_pairs={{0,1},{1,0},{2,3},{3,2},{4,5},{5,4},{6,7},{7,6},{8,9},{9,8},{10,11... | collective-permute-start | bytes 393224 | tf_op jit(solution)/shard_map/ppermute | solution.py:216
  3.6 7.3 %collective-permute-start.1 = (bf16[2,16,1024]{2,1,0:T(8,128)(2,1)S(1)}, bf16[2,16,1024]{2,1,0:T(8,128)(2,1)S(1)}, u32[]{:S(2)}, u32[]{:S(2)}) collective-permute-start(bf16[2,16,1024]{2,1,0:T(8,128)(2,1)S(1)} %get-tuple-element.39), channel_id=1, source_target_pairs={{0,2},{1,3},{2,0},{3,1},{4,6},{5,7},{6,4},{7,5},{8,10},{9,11},{10,... | collective-permute-start | bytes 196616 | tf_op jit(solution)/shard_map/ppermute | solution.py:216
  6.5 4.4 %collective-permute-start.2 = (bf16[2,16,1024]{2,1,0:T(8,128)(2,1)S(1)}, bf16[2,16,1024]{2,1,0:T(8,128)(2,1)S(1)}, u32[]{:S(2)}, u32[]{:S(2)}) collective-permute-start(bf16[2,16,1024]{2,1,0:T(8,128)(2,1)S(1)} %get-tuple-element.40), channel_id=1, source_target_pairs={{0,4},{1,5},{2,6},{3,7},{4,0},{5,1},{6,2},{7,3},{8,12},{9,13},{10,... | collective-permute-start | bytes 196616 | tf_op jit(solution)/shard_map/ppermute | solution.py:216
  8.1 5.2 %collective-permute-start.3 = (bf16[2,16,1024]{2,1,0:T(8,128)(2,1)S(1)}, bf16[2,16,1024]{2,1,0:T(8,128)(2,1)S(1)}, u32[]{:S(2)}, u32[]{:S(2)}) collective-permute-start(bf16[2,16,1024]{2,1,0:T(8,128)(2,1)S(1)} %get-tuple-element.41), channel_id=1, source_target_pairs={{0,6},{1,7},{2,4},{3,5},{4,2},{5,3},{6,0},{7,1},{8,14},{9,15},{10,... | collective-permute-start | bytes 196616 | tf_op jit(solution)/shard_map/ppermute | solution.py:216
  14.7 5.3 %collective-permute-start.4 = (bf16[3,16,1024]{2,1,0:T(8,128)(2,1)S(1)}, bf16[3,16,1024]{2,1,0:T(8,128)(2,1)S(1)}, u32[]{:S(2)}, u32[]{:S(2)}) collective-permute-start(bf16[3,16,1024]{2,1,0:T(8,128)(2,1)S(1)} %get-tuple-element.43), channel_id=1, source_target_pairs={{0,8},{8,0},{16,24},{24,16},{1,9},{9,1},{17,25},{25,17},{2,10},{10... | collective-permute-start | bytes 294920 | tf_op jit(solution)/shard_map/ppermute | solution.py:216
  16.4 8.0 %collective-permute-start.5 = (bf16[3,16,1024]{2,1,0:T(8,128)(2,1)S(1)}, bf16[3,16,1024]{2,1,0:T(8,128)(2,1)S(1)}, u32[]{:S(2)}, u32[]{:S(2)}) collective-permute-start(bf16[3,16,1024]{2,1,0:T(8,128)(2,1)S(1)} %get-tuple-element.44), channel_id=1, source_target_pairs={{0,16},{8,24},{16,0},{24,8},{1,17},{9,25},{17,1},{25,9},{2,18},{10... | collective-permute-start | bytes 294920 | tf_op jit(solution)/shard_map/ppermute | solution.py:216
  18.9 6.5 %collective-permute-start.6 = (bf16[3,16,1024]{2,1,0:T(8,128)(2,1)S(1)}, bf16[3,16,1024]{2,1,0:T(8,128)(2,1)S(1)}, u32[]{:S(2)}, u32[]{:S(2)}) collective-permute-start(bf16[3,16,1024]{2,1,0:T(8,128)(2,1)S(1)} %get-tuple-element.45), channel_id=1, source_target_pairs={{0,24},{8,16},{16,8},{24,0},{1,25},{9,17},{17,9},{25,1},{2,26},{10... | collective-permute-start | bytes 294920 | tf_op jit(solution)/shard_map/ppermute | solution.py:216
  25.5 7.1 %collective-permute-start.9 = (bf16[3,16,1024]{2,1,0:T(8,128)(2,1)S(1)}, bf16[3,16,1024]{2,1,0:T(8,128)(2,1)S(1)}, u32[]{:S(2)}, u32[]{:S(2)}) collective-permute-start(bf16[3,16,1024]{2,1,0:T(8,128)(2,1)S(1)} %shard_map.123.refs_3_.refs_2_), channel_id=1, source_target_pairs={{0,24},{8,16},{16,8},{24,0},{1,25},{9,17},{17,9},{25,1},{2,26},{10... | collective-permute-start | bytes 294920 | tf_op jit(solution)/shard_map/ppermute | solution.py:216
  28.0 7.4 %collective-permute-start.8 = (bf16[3,16,1024]{2,1,0:T(8,128)(2,1)S(1)}, bf16[3,16,1024]{2,1,0:T(8,128)(2,1)S(1)}, u32[]{:S(2)}, u32[]{:S(2)}) collective-permute-start(bf16[3,16,1024]{2,1,0:T(8,128)(2,1)S(1)} %shard_map.123.refs_3_.refs_2_), channel_id=1, source_target_pairs={{0,16},{8,24},{16,0},{24,8},{1,17},{9,25},{17,1},{25,9},{2,18},{10... | collective-permute-start | bytes 294920 | tf_op jit(solution)/shard_map/ppermute | solution.py:216
  28.6 6.8 %collective-permute-start.7 = (bf16[3,16,1024]{2,1,0:T(8,128)(2,1)S(1)}, bf16[3,16,1024]{2,1,0:T(8,128)(2,1)S(1)}, u32[]{:S(2)}, u32[]{:S(2)}) collective-permute-start(bf16[3,16,1024]{2,1,0:T(8,128)(2,1)S(1)} %shard_map.123.refs_3_.refs_2_), channel_id=1, source_target_pairs={{0,8},{8,0},{16,24},{24,16},{1,9},{9,1},{17,25},{25,17},{2,10},{10... | collective-permute-start | bytes 294920 | tf_op jit(solution)/shard_map/ppermute | solution.py:216
  37.2 1.4 %collective-permute-start.10 = (bf16[4,16,1024]{2,1,0:T(8,128)(2,1)S(1)}, bf16[4,16,1024]{2,1,0:T(8,128)(2,1)S(1)}, u32[]{:S(2)}, u32[]{:S(2)}) collective-permute-start(bf16[4,16,1024]{2,1,0:T(8,128)(2,1)S(1)} %get-tuple-element.47), channel_id=1, source_target_pairs={{0,1},{1,0},{2,3},{3,2},{4,5},{5,4},{6,7},{7,6},{8,9},{9,8},{10,11... | collective-permute-start | bytes 393224 | tf_op jit(solution)/shard_map/ppermute | solution.py:216
  38.6 7.0 %collective-permute-start.11 = (bf16[2,16,1024]{2,1,0:T(8,128)(2,1)S(1)}, bf16[2,16,1024]{2,1,0:T(8,128)(2,1)S(1)}, u32[]{:S(2)}, u32[]{:S(2)}) collective-permute-start(bf16[2,16,1024]{2,1,0:T(8,128)(2,1)S(1)} %get-tuple-element.49), channel_id=1, source_target_pairs={{0,2},{1,3},{2,0},{3,1},{4,6},{5,7},{6,4},{7,5},{8,10},{9,11},{10,... | collective-permute-start | bytes 196616 | tf_op jit(solution)/shard_map/ppermute | solution.py:216
  39.3 6.3 %collective-permute-start.12 = (bf16[2,16,1024]{2,1,0:T(8,128)(2,1)S(1)}, bf16[2,16,1024]{2,1,0:T(8,128)(2,1)S(1)}, u32[]{:S(2)}, u32[]{:S(2)}) collective-permute-start(bf16[2,16,1024]{2,1,0:T(8,128)(2,1)S(1)} %get-tuple-element.50), channel_id=1, source_target_pairs={{0,4},{1,5},{2,6},{3,7},{4,0},{5,1},{6,2},{7,3},{8,12},{9,13},{10,... | collective-permute-start | bytes 196616 | tf_op jit(solution)/shard_map/ppermute | solution.py:216
  41.4 5.2 %collective-permute-start.13 = (bf16[2,16,1024]{2,1,0:T(8,128)(2,1)S(1)}, bf16[2,16,1024]{2,1,0:T(8,128)(2,1)S(1)}, u32[]{:S(2)}, u32[]{:S(2)}) collective-permute-start(bf16[2,16,1024]{2,1,0:T(8,128)(2,1)S(1)} %get-tuple-element.51), channel_id=1, source_target_pairs={{0,6},{1,7},{2,4},{3,5},{4,2},{5,3},{6,0},{7,1},{8,14},{9,15},{10,... | collective-permute-start | bytes 196616 | tf_op jit(solution)/shard_map/ppermute | solution.py:216

commit v3 on v2

--- a/solution.py
+++ b/solution.py
@@ -7,6 +7,7 @@
 
 CAP = 8
 CORES = 2
+TILE = 256
 F32 = jnp.float32
 BF16 = jnp.bfloat16
 VMEM_SPEC = pl.BlockSpec(memory_space=pltpu.VMEM)
@@ -19,7 +20,9 @@
     )
 
 
-def call(kernel, out_shape, in_specs=None, scratch=(), flops=0, bytes_accessed=0, mib=8):
+def call(
+    kernel, out_shape, in_specs=None, out_specs=None, scratch=(), flops=0, bytes_accessed=0, mib=8
+):
     many = isinstance(out_shape, (tuple, list))
 
     def run(*args):
@@ -27,7 +30,7 @@
             kernel,
             out_shape=out_shape,
             in_specs=in_specs or [VMEM_SPEC] * len(args),
-            out_specs=[VMEM_SPEC] * len(out_shape) if many else VMEM_SPEC,
+            out_specs=out_specs or ([VMEM_SPEC] * len(out_shape) if many else VMEM_SPEC),
             scratch_shapes=scratch,
             compiler_params=pltpu.CompilerParams(vmem_limit_bytes=mib << 20),
             cost_estimate=pl.CostEstimate(
@@ -142,7 +145,7 @@
     sends = refs[-1 - shares - 2 : -3]
     rows_ref, grads_ref = refs[-3:-1]
     gate_ref, up_ref, down_ref = refs[-1 - shares - 5 : -1 - shares - 2]
-    got = refs[: -1 - shares - 5]
+    got = sort_back(refs[: -1 - shares - 5])
     for k, ref in enumerate(got):
         blocks_ref[CORES * k : CORES * k + CORES] = ref[...]
     owners = blocks_ref.shape[0]
@@ -176,7 +179,7 @@
 
 
 def output_kernel(*refs):
-    (gate_ref, up_ref, down_ref), acts = refs[:3], refs[3:-3]
+    (gate_ref, up_ref, down_ref), acts = refs[:3], sort_back(refs[3:-3])
     mine_ref, theirs_ref, blocks_ref = refs[-3:]
     owners, _, features = blocks_ref.shape
     step = owners // len(acts)
@@ -195,20 +198,43 @@
 
 
 def weight_kernel(*refs):
-    (rows_ref, grads_ref), acts = refs[:2], refs[2:-3]
-    gate_ref, up_ref, down_ref = refs[-3:]
+    (rows_ref, grads_ref), acts = refs[:2], sort_back(refs[2:-7])
+    gate_hbm, up_hbm, down_hbm, gate_ref, up_ref, down_ref, sems = refs[-7:]
     rows, grads = rows_ref[...], grads_ref[...]
     hidden, gate_grad, up_grad = (jnp.concatenate([a[i] for a in acts], axis=0) for i in range(3))
-    gate_ref[0] = dot(rows, gate_grad, 0, 0).astype(BF16)
-    up_ref[0] = dot(rows, up_grad, 0, 0).astype(BF16)
-    down_ref[0] = dot(hidden, grads, 0, 0).astype(BF16)
+    copies = []
+    for i, (left, right, out_ref, out_hbm) in enumerate(
+        (
+            (rows, gate_grad, gate_ref, gate_hbm),
+            (rows, up_grad, up_ref, up_hbm),
+            (hidden, grads, down_ref, down_hbm),
+        )
+    ):
+        count = out_ref.shape[0] // TILE
+        for j in range(count):
+            part = slice(j * TILE, (j + 1) * TILE)
+            out_ref[part] = dot(left[:, part], right, 0, 0).astype(BF16)
+            copy = pltpu.make_async_copy(out_ref.at[part], out_hbm.at[0, part], sems.at[i, j])
+            copy.start()
+            copies.append(copy)
+    for copy in copies:
+        copy.wait()
 
 
 def combine_kernel(*refs):
-    got, (place_ref, blend_ref, mixed_ref, rows_ref) = refs[:-4], refs[-4:]
+    got, (place_ref, blend_ref, mixed_ref, rows_ref) = sort_back(refs[:-4]), refs[-4:]
     outs, backs = unpack(jnp.concatenate([ref[...] for ref in got], axis=0))
     mixed_ref[...] = dot(blend_ref[...], outs, 0, 0).astype(BF16)
     rows_ref[...] = dot(place_ref[...], backs, 0, 0).astype(BF16)
+
+
+def most_bits_first(count):
+    return sorted(range(count), key=lambda k: (k > 0, -k.bit_count(), k))
+
+
+def sort_back(refs):
+    order = most_bits_first(len(refs))
+    return [refs[order.index(k)] for k in range(len(refs))]
 
 
 def trade(array, axis, distance):
@@ -222,7 +248,7 @@
     packed = call(
         pack_kernel, (jax.ShapeDtypeStruct((CORES, rows, features), BF16),) * chips
     )(mine, got)
-    return [packed[0]] + [trade(packed[k], "expert", CORES * k) for k in range(1, chips)]
+    return [trade(packed[k], "expert", CORES * k) if k else packed[0] for k in most_bits_first(chips)]
 
 
 def on_device(row_codes, scales, routes, mix_weights, w_gate, w_up, w_down, grad_out):
@@ -261,11 +287,11 @@
         scratch=[blocks],
         flops=3 * one,
     )(*got, *weights)
-    summed = [partials[0]] + [trade(partials[s], "dp", s) for s in range(1, shares)]
+    summed = [trade(partials[s], "dp", s) if s else partials[0] for s in range(shares)]
     act = call(gating_kernel, shape((3, share, width), BF16))(*summed)
-    acts = [act] + [trade(act, "dp", s) for s in range(1, shares)]
+    acts = [trade(act, "dp", s) if s else act for s in most_bits_first(shares)]
     back = swap(
-        *call(output_kernel, (half, half), scratch=[blocks], flops=3 * one)(*weights, *acts)
+        *call(output_kernel, (half, half), scratch=[blocks], flops=3 * one)(*weights, *acts),
     )
     grad_gate, grad_up, grad_down = call(
         weight_kernel,
@@ -274,6 +300,13 @@
             shape((1, features, width), BF16),
             shape((1, width, features), BF16),
         ),
+        out_specs=[HBM_SPEC] * 3,
+        scratch=[
+            pltpu.VMEM((features, width), BF16),
+            pltpu.VMEM((features, width), BF16),
+            pltpu.VMEM((width, features), BF16),
+            pltpu.SemaphoreType.DMA((3, max(features, width) // TILE)),
+        ],
         flops=3 * one,
         bytes_accessed=6 * features * width,
         mib=16,

time: 47.8 us -> 46.4 us (0.971)
  waiting for transfers between devices: 17.2 us -> 16.1 us
    ppermute x14, waiting for transfers between devices: 17.2 us -> 16.1 us  [trade(): return lax.ppermute(array, axis, [(i, i ^ distance) for i in range(count)])]
where the time goes in v3:
time: 46.4 us; the launch traced here: 46.2 us
  starting transfers between devices  17.6 us (38%)
  waiting for transfers between devices  16.1 us (35%)
  Pallas kernels  11.8 us (25%)
  between operations  0.73 us (2%)
    ppermute x14, starting transfers between devices, trade(): return lax.ppermute(array, axis, [(i, i ^ distance) for i in range(count)])  17.6 us
    ppermute x14, waiting for transfers between devices, trade(): return lax.ppermute(array, axis, [(i, i ^ distance) for i in range(count)])  16.1 us
    pallas_call x9, Pallas kernels, run(): pl.pallas_call(kernel, out_shape=out_shape, in_specs=in_specs or [VMEM_SP...  11.8 us
  transfers between devices with their start and end apart: 14, of which 9 were waited for; matrix products, arithmetic and copies ran while one was open for 0% of the time, Pallas kernels for 13%

profile of v3, /device:TPU:0, one launch (start us, length us, event | category | flops | bytes accessed | tf_op | source)
XLA Modules:
  0.0 46.2 jit_solution(10052831232814703796)
XLA Ops:
  0.6 1.5 %shard_map.119 = (bf16[4,16,1024]{2,1,0:T(8,128)(2,1)S(1)}, bf16[4,16,1024]{2,1,0:T(8,128)(2,1)S(1)}, bf16[64,128]{1,0:T(8,128)(2,1)S(1)}, bf16[64,128]{1,0:T(8,128)(2,1)S(1)}) custom-call(s32[8,128]{1,0:T(8,128)} %bitcast.9, f32[8,128]{1,0:T(8,128)} %bitcast.10, bf16[8,128]{1,0:T(8,128)(2,1)} %bitcast.11, bf16[128,1024]{1,0:T(8,128)(2,1)} %codes_hbm.1, ...), custom_call_target="tpu_custom_call" | custom-call | tf_op jit(solution)/shard_map/pallas_call | solution.py:29
  2.1 0.5 %collective-permute-start = (bf16[4,16,1024]{2,1,0:T(8,128)(2,1)S(1)}, bf16[4,16,1024]{2,1,0:T(8,128)(2,1)S(1)}, u32[]{:S(2)}, u32[]{:S(2)}) collective-permute-start(bf16[4,16,1024]{2,1,0:T(8,128)(2,1)S(1)} %get-tuple-element.34), channel_id=1, source_target_pairs={{0,1},{1,0},{2,3},{3,2},{4,5},{5,4},{6,7},{7,6},{8,9},{9,8},{10,11... | collective-permute-start | bytes 393224 | tf_op jit(solution)/shard_map/ppermute | solution.py:242
  2.6 1.0 %collective-permute-done.got_ref = bf16[4,16,1024]{2,1,0:T(8,128)(2,1)S(1)} collective-permute-done((bf16[4,16,1024]{2,1,0:T(8,128)(2,1)S(1)}, bf16[4,16,1024]{2,1,0:T(8,128)(2,1)S(1)}, u32[]{:S(2)}, u32[]{:S(2)}) %collective-permute-start) | collective-permute-done | bytes 131104 | tf_op jit(solution)/shard_map/ppermute | solution.py:242
  3.6 3.9 %collective-permute-start.1 = (bf16[2,16,1024]{2,1,0:T(8,128)(2,1)S(1)}, bf16[2,16,1024]{2,1,0:T(8,128)(2,1)S(1)}, u32[]{:S(2)}, u32[]{:S(2)}) collective-permute-start(bf16[2,16,1024]{2,1,0:T(8,128)(2,1)S(1)} %get-tuple-element.39), channel_id=1, source_target_pairs={{0,6},{1,7},{2,4},{3,5},{4,2},{5,3},{6,0},{7,1},{8,14},{9,15},{10,... | collective-permute-start | bytes 196616 | tf_op jit(solution)/shard_map/ppermute | solution.py:242
  7.5 0.5 %collective-permute-start.2 = (bf16[2,16,1024]{2,1,0:T(8,128)(2,1)S(1)}, bf16[2,16,1024]{2,1,0:T(8,128)(2,1)S(1)}, u32[]{:S(2)}, u32[]{:S(2)}) collective-permute-start(bf16[2,16,1024]{2,1,0:T(8,128)(2,1)S(1)} %get-tuple-element.40), channel_id=1, source_target_pairs={{0,2},{1,3},{2,0},{3,1},{4,6},{5,7},{6,4},{7,5},{8,10},{9,11},{10,... | collective-permute-start | bytes 196616 | tf_op jit(solution)/shard_map/ppermute | solution.py:242
  8.0 0.1 collective-permute-start.3
  8.1 2.9 %shard_map.121 = (bf16[1024,1024]{1,0:T(8,128)(2,1)S(1)}, bf16[1024,1024]{1,0:T(8,128)(2,1)S(1)}, bf16[1024,1024]{1,0:T(8,128)(2,1)S(1)}) custom-call(bf16[2,16,1024]{2,1,0:T(8,128)(2,1)S(1)} %get-tuple-element.35.after_hbm.refs_0_, bf16[1024,1024]{1,0:T(8,128)(2,1)} %bitcast.6, bf16[1024,1024]{1,0:T(8,128)(2,1)} %bitcast.7, bf16[1024,1024]{1,0:T(8,128)(2,1)} %bitcast.8), custom_call_target="tpu_custom_call" | custom-call | bytes 6291456 | tf_op jit(solution)/shard_map/pallas_call | solution.py:29
  11.0 0.7 %collective-permute-done.2.refs_2_ = bf16[2,16,1024]{2,1,0:T(8,128)(2,1)S(1)} collective-permute-done((bf16[2,16,1024]{2,1,0:T(8,128)(2,1)S(1)}, bf16[2,16,1024]{2,1,0:T(8,128)(2,1)S(1)}, u32[]{:S(2)}, u32[]{:S(2)}) %collective-permute-start.2) | collective-permute-done | bytes 65568 | tf_op jit(solution)/shard_map/ppermute | solution.py:242
  11.8 0.5 %collective-permute-done.3.refs_3_ = bf16[2,16,1024]{2,1,0:T(8,128)(2,1)S(1)} collective-permute-done((bf16[2,16,1024]{2,1,0:T(8,128)(2,1)S(1)}, bf16[2,16,1024]{2,1,0:T(8,128)(2,1)S(1)}, u32[]{:S(2)}, u32[]{:S(2)}) %collective-permute-start.3) | collective-permute-done | bytes 65568 | tf_op jit(solution)/shard_map/ppermute | solution.py:242
  12.3 1.5 %shard_map.122 = (bf16[3,16,1024]{2,1,0:T(8,128)(2,1)S(1)}, bf16[3,16,1024]{2,1,0:T(8,128)(2,1)S(1)}, bf16[3,16,1024]{2,1,0:T(8,128)(2,1)S(1)}, bf16[3,16,1024]{...) custom-call(bf16[2,16,1024]{2,1,0:T(8,128)(2,1)S(1)} %get-tuple-element.35.after_hbm.refs_0_, ...), custom_call_target="tpu_custom_call" | custom-call | flops 402653184 | tf_op jit(solution)/shard_map/pallas_call | solution.py:29
  13.8 1.6 %collective-permute-start.4 = (bf16[3,16,1024]{2,1,0:T(8,128)(2,1)S(1)}, bf16[3,16,1024]{2,1,0:T(8,128)(2,1)S(1)}, u32[]{:S(2)}, u32[]{:S(2)}) collective-permute-start(bf16[3,16,1024]{2,1,0:T(8,128)(2,1)S(1)} %get-tuple-element.43), channel_id=1, source_target_pairs={{0,8},{8,0},{16,24},{24,16},{1,9},{9,1},{17,25},{25,17},{2,10},{10... | collective-permute-start | bytes 294920 | tf_op jit(solution)/shard_map/ppermute | solution.py:242
  15.4 2.6 %collective-permute-start.5 = (bf16[3,16,1024]{2,1,0:T(8,128)(2,1)S(1)}, bf16[3,16,1024]{2,1,0:T(8,128)(2,1)S(1)}, u32[]{:S(2)}, u32[]{:S(2)}) collective-permute-start(bf16[3,16,1024]{2,1,0:T(8,128)(2,1)S(1)} %get-tuple-element.44), channel_id=1, source_target_pairs={{0,16},{8,24},{16,0},{24,8},{1,17},{9,25},{17,1},{25,9},{2,18},{10... | collective-permute-start | bytes 294920 | tf_op jit(solution)/shard_map/ppermute | solution.py:242
  18.0 0.2 collective-permute-start.6
  18.2 1.2 %collective-permute-done.4.refs_1_ = bf16[3,16,1024]{2,1,0:T(8,128)(2,1)S(1)} collective-permute-done((bf16[3,16,1024]{2,1,0:T(8,128)(2,1)S(1)}, bf16[3,16,1024]{2,1,0:T(8,128)(2,1)S(1)}, u32[]{:S(2)}, u32[]{:S(2)}) %collective-permute-start.4) | collective-permute-done | bytes 98336 | tf_op jit(solution)/shard_map/ppermute | solution.py:242
  19.4 5.5 %collective-permute-done.5.refs_2_ = bf16[3,16,1024]{2,1,0:T(8,128)(2,1)S(1)} collective-permute-done((bf16[3,16,1024]{2,1,0:T(8,128)(2,1)S(1)}, bf16[3,16,1024]{2,1,0:T(8,128)(2,1)S(1)}, u32[]{:S(2)}, u32[]{:S(2)}) %collective-permute-start.5) | collective-permute-done | bytes 98336 | tf_op jit(solution)/shard_map/ppermute | solution.py:242
  24.9 0.1 shard_map.123.refs_3_.refs_2_
  25.0 2.7 %collective-permute-start.9 = (bf16[3,16,1024]{2,1,0:T(8,128)(2,1)S(1)}, bf16[3,16,1024]{2,1,0:T(8,128)(2,1)S(1)}, u32[]{:S(2)}, u32[]{:S(2)}) collective-permute-start(bf16[3,16,1024]{2,1,0:T(8,128)(2,1)S(1)} %shard_map.123.refs_3_.refs_2_), channel_id=1, source_target_pairs={{0,16},{8,24},{16,0},{24,8},{1,17},{9,25},{17,1},{25,9},{2,18},{10... | collective-permute-start | bytes 294920 | tf_op jit(solution)/shard_map/ppermute | solution.py:242
  27.7 0.4 collective-permute-start.8
  28.1 1.3 %collective-permute-start.7 = (bf16[3,16,1024]{2,1,0:T(8,128)(2,1)S(1)}, bf16[3,16,1024]{2,1,0:T(8,128)(2,1)S(1)}, u32[]{:S(2)}, u32[]{:S(2)}) collective-permute-start(bf16[3,16,1024]{2,1,0:T(8,128)(2,1)S(1)} %shard_map.123.refs_3_.refs_2_), channel_id=1, source_target_pairs={{0,24},{8,16},{16,8},{24,0},{1,25},{9,17},{17,9},{25,1},{2,26},{10... | collective-permute-start | bytes 294920 | tf_op jit(solution)/shard_map/ppermute | solution.py:242
  29.5 4.0 %collective-permute-done.9.refs_6_.refs_5_ = bf16[3,16,1024]{2,1,0:T(8,128)(2,1)S(1)} collective-permute-done((bf16[3,16,1024]{2,1,0:T(8,128)(2,1)S(1)}, bf16[3,16,1024]{2,1,0:T(8,128)(2,1)S(1)}, u32[]{:S(2)}, u32[]{:S(2)}) %collective-permute-start.9) | collective-permute-done | bytes 98336 | tf_op jit(solution)/shard_map/ppermute | solution.py:242
  33.5 0.0 collective-permute-done.8.refs_5_.refs_4_
  33.5 1.1 %collective-permute-done.7.refs_4_.refs_3_ = bf16[3,16,1024]{2,1,0:T(8,128)(2,1)S(1)} collective-permute-done((bf16[3,16,1024]{2,1,0:T(8,128)(2,1)S(1)}, bf16[3,16,1024]{2,1,0:T(8,128)(2,1)S(1)}, u32[]{:S(2)}, u32[]{:S(2)}) %collective-permute-start.7) | collective-permute-done | bytes 98336 | tf_op jit(solution)/shard_map/ppermute | solution.py:242
  34.7 1.8 %shard_map.124 = (bf16[4,16,1024]{2,1,0:T(8,128)(2,1)S(1)}, bf16[4,16,1024]{2,1,0:T(8,128)(2,1)S(1)}) custom-call(bf16[1024,1024]{1,0:T(8,128)(2,1)S(1)} %get-tuple-element.36.refs_4_.refs_0_, bf16[1024,1024]{1,0:T(8,128)(2,1)S(1)} %get-tuple-element.37.refs_5_.refs_1_, bf16[1024,1024]{1,0:T(8,128)(2,1)S(1)} %get-tuple-element.38.refs_6_.refs_2_, ...), custom_call_target="tpu_custom_call" | custom-call | flops 402653184 | tf_op jit(solution)/shard_map/pallas_call | solution.py:29
  36.4 0.1 collective-permute-start.10
  36.5 1.3 %collective-permute-done.10.got_ref = bf16[4,16,1024]{2,1,0:T(8,128)(2,1)S(1)} collective-permute-done((bf16[4,16,1024]{2,1,0:T(8,128)(2,1)S(1)}, bf16[4,16,1024]{2,1,0:T(8,128)(2,1)S(1)}, u32[]{:S(2)}, u32[]{:S(2)}) %collective-permute-start.10) | collective-permute-done | bytes 131104 | tf_op jit(solution)/shard_map/ppermute | solution.py:242
  37.9 2.3 %collective-permute-start.11 = (bf16[2,16,1024]{2,1,0:T(8,128)(2,1)S(1)}, bf16[2,16,1024]{2,1,0:T(8,128)(2,1)S(1)}, u32[]{:S(2)}, u32[]{:S(2)}) collective-permute-start(bf16[2,16,1024]{2,1,0:T(8,128)(2,1)S(1)} %get-tuple-element.49), channel_id=1, source_target_pairs={{0,6},{1,7},{2,4},{3,5},{4,2},{5,3},{6,0},{7,1},{8,14},{9,15},{10,... | collective-permute-start | bytes 196616 | tf_op jit(solution)/shard_map/ppermute | solution.py:242
  40.2 0.7 %collective-permute-start.12 = (bf16[2,16,1024]{2,1,0:T(8,128)(2,1)S(1)}, bf16[2,16,1024]{2,1,0:T(8,128)(2,1)S(1)}, u32[]{:S(2)}, u32[]{:S(2)}) collective-permute-start(bf16[2,16,1024]{2,1,0:T(8,128)(2,1)S(1)} %get-tuple-element.50), channel_id=1, source_target_pairs={{0,2},{1,3},{2,0},{3,1},{4,6},{5,7},{6,4},{7,5},{8,10},{9,11},{10,... | collective-permute-start | bytes 196616 | tf_op jit(solution)/shard_map/ppermute | solution.py:242
  40.9 0.5 %collective-permute-start.13 = (bf16[2,16,1024]{2,1,0:T(8,128)(2,1)S(1)}, bf16[2,16,1024]{2,1,0:T(8,128)(2,1)S(1)}, u32[]{:S(2)}, u32[]{:S(2)}) collective-permute-start(bf16[2,16,1024]{2,1,0:T(8,128)(2,1)S(1)} %get-tuple-element.51), channel_id=1, source_target_pairs={{0,4},{1,5},{2,6},{3,7},{4,0},{5,1},{6,2},{7,3},{8,12},{9,13},{10,... | collective-permute-start | bytes 196616 | tf_op jit(solution)/shard_map/ppermute | solution.py:242
  41.4 3.1 %shard_map.127 = (bf16[1,1024,1024]{2,1,0:T(8,128)(2,1)}, bf16[1,1024,1024]{2,1,0:T(8,128)(2,1)}, bf16[1,1024,1024]{2,1,0:T(8,128)(2,1)}) custom-call(bf16[64,1024]{1,0:T(8,128)(2,1)S(1)} %get-tuple-element.56.refs_0_, bf16[64,1024]{1,0:T(8,128)(2,1)S(1)} %get-tuple-element.57.refs_1_, bf16[3,16,1024]{2,1,0:T(8,128)(2,1)S(1)} %shard_map.123.refs_3_.refs_2_, ...), custom_call_target="tpu_custom_call" | custom-call | flops 402653184 | bytes 6291456 | tf_op jit(solution)/shard_map/pallas_call | solution.py:29
  44.5 0.0 collective-permute-done.12.refs_2_
  44.5 0.6 %collective-permute-done.13.refs_3_ = bf16[2,16,1024]{2,1,0:T(8,128)(2,1)S(1)} collective-permute-done((bf16[2,16,1024]{2,1,0:T(8,128)(2,1)S(1)}, bf16[2,16,1024]{2,1,0:T(8,128)(2,1)S(1)}, u32[]{:S(2)}, u32[]{:S(2)}) %collective-permute-start.13) | collective-permute-done | bytes 65568 | tf_op jit(solution)/shard_map/ppermute | solution.py:242
  45.1 1.0 %shard_map.126 = (bf16[128,1024]{1,0:T(8,128)(2,1)}, bf16[128,1024]{1,0:T(8,128)(2,1)}) custom-call(bf16[2,16,1024]{2,1,0:T(8,128)(2,1)S(1)} %get-tuple-element.48.refs_0_, bf16[2,16,1024]{2,1,0:T(8,128)(2,1)S(1)} %collective-permute-done.11.refs_1_, bf16[2,16,1024]{2,1,0:T(8,128)(2,1)S(1)} %collective-permute-done.12.refs_2_, ...), custom_call_target="tpu_custom_call" | custom-call | tf_op jit(solution)/shard_map/pallas_call | solution.py:29
  (5 shorter events, 0.0 us)
Async XLA Ops:
  2.1 1.5 %collective-permute-start = (bf16[4,16,1024]{2,1,0:T(8,128)(2,1)S(1)}, bf16[4,16,1024]{2,1,0:T(8,128)(2,1)S(1)}, u32[]{:S(2)}, u32[]{:S(2)}) collective-permute-start(bf16[4,16,1024]{2,1,0:T(8,128)(2,1)S(1)} %get-tuple-element.34), channel_id=1, source_target_pairs={{0,1},{1,0},{2,3},{3,2},{4,5},{5,4},{6,7},{7,6},{8,9},{9,8},{10,11... | collective-permute-start | bytes 393224 | tf_op jit(solution)/shard_map/ppermute | solution.py:242
  3.6 7.4 %collective-permute-start.1 = (bf16[2,16,1024]{2,1,0:T(8,128)(2,1)S(1)}, bf16[2,16,1024]{2,1,0:T(8,128)(2,1)S(1)}, u32[]{:S(2)}, u32[]{:S(2)}) collective-permute-start(bf16[2,16,1024]{2,1,0:T(8,128)(2,1)S(1)} %get-tuple-element.39), channel_id=1, source_target_pairs={{0,6},{1,7},{2,4},{3,5},{4,2},{5,3},{6,0},{7,1},{8,14},{9,15},{10,... | collective-permute-start | bytes 196616 | tf_op jit(solution)/shard_map/ppermute | solution.py:242
  7.5 4.3 %collective-permute-start.2 = (bf16[2,16,1024]{2,1,0:T(8,128)(2,1)S(1)}, bf16[2,16,1024]{2,1,0:T(8,128)(2,1)S(1)}, u32[]{:S(2)}, u32[]{:S(2)}) collective-permute-start(bf16[2,16,1024]{2,1,0:T(8,128)(2,1)S(1)} %get-tuple-element.40), channel_id=1, source_target_pairs={{0,2},{1,3},{2,0},{3,1},{4,6},{5,7},{6,4},{7,5},{8,10},{9,11},{10,... | collective-permute-start | bytes 196616 | tf_op jit(solution)/shard_map/ppermute | solution.py:242
  8.0 4.3 %collective-permute-start.3 = (bf16[2,16,1024]{2,1,0:T(8,128)(2,1)S(1)}, bf16[2,16,1024]{2,1,0:T(8,128)(2,1)S(1)}, u32[]{:S(2)}, u32[]{:S(2)}) collective-permute-start(bf16[2,16,1024]{2,1,0:T(8,128)(2,1)S(1)} %get-tuple-element.41), channel_id=1, source_target_pairs={{0,4},{1,5},{2,6},{3,7},{4,0},{5,1},{6,2},{7,3},{8,12},{9,13},{10,... | collective-permute-start | bytes 196616 | tf_op jit(solution)/shard_map/ppermute | solution.py:242
  13.8 5.7 %collective-permute-start.4 = (bf16[3,16,1024]{2,1,0:T(8,128)(2,1)S(1)}, bf16[3,16,1024]{2,1,0:T(8,128)(2,1)S(1)}, u32[]{:S(2)}, u32[]{:S(2)}) collective-permute-start(bf16[3,16,1024]{2,1,0:T(8,128)(2,1)S(1)} %get-tuple-element.43), channel_id=1, source_target_pairs={{0,8},{8,0},{16,24},{24,16},{1,9},{9,1},{17,25},{25,17},{2,10},{10... | collective-permute-start | bytes 294920 | tf_op jit(solution)/shard_map/ppermute | solution.py:242
  15.4 9.5 %collective-permute-start.5 = (bf16[3,16,1024]{2,1,0:T(8,128)(2,1)S(1)}, bf16[3,16,1024]{2,1,0:T(8,128)(2,1)S(1)}, u32[]{:S(2)}, u32[]{:S(2)}) collective-permute-start(bf16[3,16,1024]{2,1,0:T(8,128)(2,1)S(1)} %get-tuple-element.44), channel_id=1, source_target_pairs={{0,16},{8,24},{16,0},{24,8},{1,17},{9,25},{17,1},{25,9},{2,18},{10... | collective-permute-start | bytes 294920 | tf_op jit(solution)/shard_map/ppermute | solution.py:242
  18.0 6.9 %collective-permute-start.6 = (bf16[3,16,1024]{2,1,0:T(8,128)(2,1)S(1)}, bf16[3,16,1024]{2,1,0:T(8,128)(2,1)S(1)}, u32[]{:S(2)}, u32[]{:S(2)}) collective-permute-start(bf16[3,16,1024]{2,1,0:T(8,128)(2,1)S(1)} %get-tuple-element.45), channel_id=1, source_target_pairs={{0,24},{8,16},{16,8},{24,0},{1,25},{9,17},{17,9},{25,1},{2,26},{10... | collective-permute-start | bytes 294920 | tf_op jit(solution)/shard_map/ppermute | solution.py:242
  25.0 8.5 %collective-permute-start.9 = (bf16[3,16,1024]{2,1,0:T(8,128)(2,1)S(1)}, bf16[3,16,1024]{2,1,0:T(8,128)(2,1)S(1)}, u32[]{:S(2)}, u32[]{:S(2)}) collective-permute-start(bf16[3,16,1024]{2,1,0:T(8,128)(2,1)S(1)} %shard_map.123.refs_3_.refs_2_), channel_id=1, source_target_pairs={{0,16},{8,24},{16,0},{24,8},{1,17},{9,25},{17,1},{25,9},{2,18},{10... | collective-permute-start | bytes 294920 | tf_op jit(solution)/shard_map/ppermute | solution.py:242
  27.7 5.8 %collective-permute-start.8 = (bf16[3,16,1024]{2,1,0:T(8,128)(2,1)S(1)}, bf16[3,16,1024]{2,1,0:T(8,128)(2,1)S(1)}, u32[]{:S(2)}, u32[]{:S(2)}) collective-permute-start(bf16[3,16,1024]{2,1,0:T(8,128)(2,1)S(1)} %shard_map.123.refs_3_.refs_2_), channel_id=1, source_target_pairs={{0,8},{8,0},{16,24},{24,16},{1,9},{9,1},{17,25},{25,17},{2,10},{10... | collective-permute-start | bytes 294920 | tf_op jit(solution)/shard_map/ppermute | solution.py:242
  28.1 6.5 %collective-permute-start.7 = (bf16[3,16,1024]{2,1,0:T(8,128)(2,1)S(1)}, bf16[3,16,1024]{2,1,0:T(8,128)(2,1)S(1)}, u32[]{:S(2)}, u32[]{:S(2)}) collective-permute-start(bf16[3,16,1024]{2,1,0:T(8,128)(2,1)S(1)} %shard_map.123.refs_3_.refs_2_), channel_id=1, source_target_pairs={{0,24},{8,16},{16,8},{24,0},{1,25},{9,17},{17,9},{25,1},{2,26},{10... | collective-permute-start | bytes 294920 | tf_op jit(solution)/shard_map/ppermute | solution.py:242
  36.4 1.4 %collective-permute-start.10 = (bf16[4,16,1024]{2,1,0:T(8,128)(2,1)S(1)}, bf16[4,16,1024]{2,1,0:T(8,128)(2,1)S(1)}, u32[]{:S(2)}, u32[]{:S(2)}) collective-permute-start(bf16[4,16,1024]{2,1,0:T(8,128)(2,1)S(1)} %get-tuple-element.47), channel_id=1, source_target_pairs={{0,1},{1,0},{2,3},{3,2},{4,5},{5,4},{6,7},{7,6},{8,9},{9,8},{10,11... | collective-permute-start | bytes 393224 | tf_op jit(solution)/shard_map/ppermute | solution.py:242
  37.9 6.6 %collective-permute-start.11 = (bf16[2,16,1024]{2,1,0:T(8,128)(2,1)S(1)}, bf16[2,16,1024]{2,1,0:T(8,128)(2,1)S(1)}, u32[]{:S(2)}, u32[]{:S(2)}) collective-permute-start(bf16[2,16,1024]{2,1,0:T(8,128)(2,1)S(1)} %get-tuple-element.49), channel_id=1, source_target_pairs={{0,6},{1,7},{2,4},{3,5},{4,2},{5,3},{6,0},{7,1},{8,14},{9,15},{10,... | collective-permute-start | bytes 196616 | tf_op jit(solution)/shard_map/ppermute | solution.py:242
  40.2 4.3 %collective-permute-start.12 = (bf16[2,16,1024]{2,1,0:T(8,128)(2,1)S(1)}, bf16[2,16,1024]{2,1,0:T(8,128)(2,1)S(1)}, u32[]{:S(2)}, u32[]{:S(2)}) collective-permute-start(bf16[2,16,1024]{2,1,0:T(8,128)(2,1)S(1)} %get-tuple-element.50), channel_id=1, source_target_pairs={{0,2},{1,3},{2,0},{3,1},{4,6},{5,7},{6,4},{7,5},{8,10},{9,11},{10,... | collective-permute-start | bytes 196616 | tf_op jit(solution)/shard_map/ppermute | solution.py:242
  40.9 4.3 %collective-permute-start.13 = (bf16[2,16,1024]{2,1,0:T(8,128)(2,1)S(1)}, bf16[2,16,1024]{2,1,0:T(8,128)(2,1)S(1)}, u32[]{:S(2)}, u32[]{:S(2)}) collective-permute-start(bf16[2,16,1024]{2,1,0:T(8,128)(2,1)S(1)} %get-tuple-element.51), channel_id=1, source_target_pairs={{0,4},{1,5},{2,6},{3,7},{4,0},{5,1},{6,2},{7,3},{8,12},{9,13},{10,... | collective-permute-start | bytes 196616 | tf_op jit(solution)/shard_map/ppermute | solution.py:242

commit v4 on v3

--- a/solution.py
+++ b/solution.py
@@ -43,6 +43,16 @@
 
 def in_hbm(array):
     return pltpu.with_memory_space_constraint(array, pltpu.HBM)
+
+
+def distances(shares, core):
+    return [0] + (list(range(1, shares)) if core == 0 else list(range(shares - 1, 0, -1)))
+
+
+def peer(shares, s):
+    near, far = distances(shares, 0)[s], distances(shares, 1)[s]
+    core = lax.rem(lax.axis_index("expert"), CORES)
+    return lax.axis_index("dp") ^ jnp.where(core == 0, near, far)
 
 
 def load_all(sources, targets, sems):
@@ -126,9 +136,19 @@
         out[1] = got_ref[k]
 
 
-def fetch_kernel(after_hbm, gate_hbm, up_hbm, down_hbm, gate_ref, up_ref, down_ref, sems):
-    for copy in load_all((gate_hbm, up_hbm, down_hbm), (gate_ref, up_ref, down_ref), sems):
-        copy.wait()
+def fetch_kernel(
+    after_hbm, gate_hbm, up_hbm, down_hbm, gate_ref, up_ref, down_ref, flipped_ref, sems
+):
+    copies = load_all((down_hbm, gate_hbm, up_hbm), (down_ref, gate_ref, up_ref), sems)
+    copies[0].wait()
+    flipped_ref[...] = down_ref[...].T
+    copies[1].wait()
+    copies[2].wait()
+
+
+def flip_kernel(after_hbm, gate_ref, up_ref, gate_out, up_out):
+    gate_out[...] = gate_ref[...].T
+    up_out[...] = up_ref[...].T
 
 
 def unpack(blocks):
@@ -150,9 +170,8 @@
         blocks_ref[CORES * k : CORES * k + CORES] = ref[...]
     owners = blocks_ref.shape[0]
     step = owners // shares
-    me = lax.axis_index("dp")
     rows, grads = unpack(
-        jnp.concatenate([blocks_ref[pl.ds((me ^ s) * step, step)] for s in range(shares)], axis=0)
+        jnp.concatenate([blocks_ref[pl.ds(peer(shares, s) * step, step)] for s in range(shares)], axis=0)
     )
     rows_ref[...] = rows
     grads_ref[...] = grads
@@ -161,7 +180,7 @@
         (
             dot(rows, gate_ref[...], 1, 0),
             dot(rows, up_ref[...], 1, 0),
-            dot(grads, down_ref[...], 1, 1),
+            dot(grads, down_ref[...], 1, 0),
         )
     ):
         for s, send in enumerate(sends):
@@ -185,13 +204,13 @@
     step = owners // len(acts)
     hidden, gate_grad, up_grad = (jnp.concatenate([a[i] for a in acts], axis=0) for i in range(3))
     out = dot(hidden, down_ref[...], 1, 0)
-    back = dot(gate_grad, gate_ref[...], 1, 1) + dot(up_grad, up_ref[...], 1, 1)
+    back = dot(gate_grad, gate_ref[...], 1, 0) + dot(up_grad, up_ref[...], 1, 0)
     both = jnp.concatenate(
         [out.reshape(owners, CAP, features), back.reshape(owners, CAP, features)], axis=1
     ).astype(BF16)
-    me = lax.axis_index("dp")
-    for s in range(len(acts)):
-        blocks_ref[pl.ds((me ^ s) * step, step)] = both[s * step : (s + 1) * step]
+    shares = len(acts)
+    for s in range(shares):
+        blocks_ref[pl.ds(peer(shares, s) * step, step)] = both[s * step : (s + 1) * step]
     for k in range(owners // CORES):
         mine_ref[k] = blocks_ref[CORES * k]
         theirs_ref[k] = blocks_ref[CORES * k + 1]
@@ -242,6 +261,16 @@
     return lax.ppermute(array, axis, [(i, i ^ distance) for i in range(count)])
 
 
+def trade_dp(array, s):
+    shares, owners = lax.axis_size("dp"), lax.axis_size("expert")
+    pairs = [
+        (d * owners + e, (d ^ distances(shares, e % CORES)[s]) * owners + e)
+        for d in range(shares)
+        for e in range(owners)
+    ]
+    return lax.ppermute(array, ("dp", "expert"), pairs)
+
+
 def swap(mine, theirs):
     chips, rows, features = mine.shape
     got = trade(theirs, "expert", 1)
@@ -276,7 +305,8 @@
     weights = tuple(in_hbm(w[0]) for w in (w_gate, w_up, w_down))
     weights = call(
         fetch_kernel,
-        tuple(pltpu.VMEM(w.shape, w.dtype) for w in weights),
+        tuple(pltpu.VMEM(w.shape, w.dtype) for w in weights)
+        + (pltpu.VMEM((features, width), BF16),),
         in_specs=[HBM_SPEC] * 4,
         scratch=[pltpu.SemaphoreType.DMA((3,))],
         bytes_accessed=6 * features * width,
@@ -286,12 +316,19 @@
         (shape((3, share, width), BF16),) * shares + (shape((slots, features), BF16),) * 2,
         scratch=[blocks],
         flops=3 * one,
-    )(*got, *weights)
-    summed = [trade(partials[s], "dp", s) if s else partials[0] for s in range(shares)]
+    )(*got, *weights[:2], weights[3])
+    gate_w, up_w, down_w, _ = weights
+    flipped = call(
+        flip_kernel,
+        (pltpu.VMEM((width, features), BF16),) * 2,
+        in_specs=[HBM_SPEC, VMEM_SPEC, VMEM_SPEC],
+        bytes_accessed=16 * features * width,
+    )(partials[0], gate_w, up_w)
+    summed = [trade_dp(partials[s], s) if s else partials[0] for s in range(shares)]
     act = call(gating_kernel, shape((3, share, width), BF16))(*summed)
-    acts = [trade(act, "dp", s) if s else act for s in most_bits_first(shares)]
+    acts = [trade_dp(act, s) if s else act for s in most_bits_first(shares)]
     back = swap(
-        *call(output_kernel, (half, half), scratch=[blocks], flops=3 * one)(*weights, *acts),
+        *call(output_kernel, (half, half), scratch=[blocks], flops=3 * one)(*flipped, down_w, *acts),
     )
     grad_gate, grad_up, grad_down = call(
         weight_kernel,

time: 46.4 us -> 45.2 us (0.974)
  waiting for transfers between devices: 16.1 us -> 14.5 us
    ppermute x14 -> x8, waiting for transfers between devices: 16.1 us -> 4.01 us  [trade(): return lax.ppermute(array, axis, [(i, i ^ distance) for i in range(count)])]
    ppermute x0 -> x6, waiting for transfers between devices: none -> 10.4 us  [trade_dp(): return lax.ppermute(array, ('dp', 'expert'), pairs)]
    ppermute x14 -> x8, starting transfers between devices: 17.6 us -> 8.66 us  [trade(): return lax.ppermute(array, axis, [(i, i ^ distance) for i in range(count)])]
    ppermute x0 -> x6, starting transfers between devices: none -> 8.9 us  [trade_dp(): return lax.ppermute(array, ('dp', 'expert'), pairs)]
    pallas_call x9 -> x10, Pallas kernels: 11.8 us -> 12.2 us  [run(): pl.pallas_call(kernel, out_shape=out_shape, in_specs=in_specs or [VMEM_SP...]
  transfers between devices with their start and end apart: 14 -> 14, of which waited for: 9 -> 11; matrix products, arithmetic and copies ran while one was open for 0% -> 0% of each run, Pallas kernels for 13% -> 16%
where the time goes in v4:
time: 45.2 us; the launch traced here: 45 us
  starting transfers between devices  17.6 us (39%)
  waiting for transfers between devices  14.5 us (32%)
  Pallas kernels  12.2 us (27%)
  between operations  0.73 us (2%)
    pallas_call x10, Pallas kernels, run(): pl.pallas_call(kernel, out_shape=out_shape, in_specs=in_specs or [VMEM_SP...  12.2 us
    ppermute x6, waiting for transfers between devices, trade_dp(): return lax.ppermute(array, ('dp', 'expert'), pairs)  10.4 us
    ppermute x6, starting transfers between devices, trade_dp(): return lax.ppermute(array, ('dp', 'expert'), pairs)  8.9 us
    ppermute x8, starting transfers between devices, trade(): return lax.ppermute(array, axis, [(i, i ^ distance) for i in range(count)])  8.66 us
    ppermute x8, waiting for transfers between devices, trade(): return lax.ppermute(array, axis, [(i, i ^ distance) for i in range(count)])  4.01 us
  transfers between devices with their start and end apart: 14, of which 11 were waited for; matrix products, arithmetic and copies ran while one was open for 0% of the time, Pallas kernels for 16%

profile of v4, /device:TPU:0, one launch (start us, length us, event | category | flops | bytes accessed | tf_op | source)
XLA Modules:
  0.0 45.0 jit_solution(9701662896710862123)
XLA Ops:
  0.6 1.5 %shard_map.119 = (bf16[4,16,1024]{2,1,0:T(8,128)(2,1)S(1)}, bf16[4,16,1024]{2,1,0:T(8,128)(2,1)S(1)}, bf16[64,128]{1,0:T(8,128)(2,1)S(1)}, bf16[64,128]{1,0:T(8,128)(2,1)S(1)}) custom-call(s32[8,128]{1,0:T(8,128)} %bitcast.9, f32[8,128]{1,0:T(8,128)} %bitcast.10, bf16[8,128]{1,0:T(8,128)(2,1)} %bitcast.11, bf16[128,1024]{1,0:T(8,128)(2,1)} %codes_hbm.1, ...), custom_call_target="tpu_custom_call" | custom-call | tf_op jit(solution)/shard_map/pallas_call | solution.py:29
  2.1 0.5 %collective-permute-start = (bf16[4,16,1024]{2,1,0:T(8,128)(2,1)S(1)}, bf16[4,16,1024]{2,1,0:T(8,128)(2,1)S(1)}, u32[]{:S(2)}, u32[]{:S(2)}) collective-permute-start(bf16[4,16,1024]{2,1,0:T(8,128)(2,1)S(1)} %get-tuple-element.37), channel_id=1, source_target_pairs={{0,1},{1,0},{2,3},{3,2},{4,5},{5,4},{6,7},{7,6},{8,9},{9,8},{10,11... | collective-permute-start | bytes 393224 | tf_op jit(solution)/shard_map/ppermute | solution.py:261
  2.6 1.0 %collective-permute-done.got_ref = bf16[4,16,1024]{2,1,0:T(8,128)(2,1)S(1)} collective-permute-done((bf16[4,16,1024]{2,1,0:T(8,128)(2,1)S(1)}, bf16[4,16,1024]{2,1,0:T(8,128)(2,1)S(1)}, u32[]{:S(2)}, u32[]{:S(2)}) %collective-permute-start) | collective-permute-done | bytes 131104 | tf_op jit(solution)/shard_map/ppermute | solution.py:261
  3.6 3.9 %collective-permute-start.1 = (bf16[2,16,1024]{2,1,0:T(8,128)(2,1)S(1)}, bf16[2,16,1024]{2,1,0:T(8,128)(2,1)S(1)}, u32[]{:S(2)}, u32[]{:S(2)}) collective-permute-start(bf16[2,16,1024]{2,1,0:T(8,128)(2,1)S(1)} %get-tuple-element.39), channel_id=1, source_target_pairs={{0,6},{1,7},{2,4},{3,5},{4,2},{5,3},{6,0},{7,1},{8,14},{9,15},{10,... | collective-permute-start | bytes 196616 | tf_op jit(solution)/shard_map/ppermute | solution.py:261
  7.5 0.5 %collective-permute-start.2 = (bf16[2,16,1024]{2,1,0:T(8,128)(2,1)S(1)}, bf16[2,16,1024]{2,1,0:T(8,128)(2,1)S(1)}, u32[]{:S(2)}, u32[]{:S(2)}) collective-permute-start(bf16[2,16,1024]{2,1,0:T(8,128)(2,1)S(1)} %get-tuple-element.40), channel_id=1, source_target_pairs={{0,2},{1,3},{2,0},{3,1},{4,6},{5,7},{6,4},{7,5},{8,10},{9,11},{10,... | collective-permute-start | bytes 196616 | tf_op jit(solution)/shard_map/ppermute | solution.py:261
  8.0 0.1 collective-permute-start.3
  8.1 2.9 %shard_map.121 = (bf16[1024,1024]{1,0:T(8,128)(2,1)S(1)}, bf16[1024,1024]{1,0:T(8,128)(2,1)S(1)}, bf16[1024,1024]{1,0:T(8,128)(2,1)S(1)}, bf16[1024,1024]{1,0:T(8,128)(2,1)S(1)}) custom-call(bf16[2,16,1024]{2,1,0:T(8,128)(2,1)S(1)} %get-tuple-element.38.after_hbm.refs_0_, bf16[1024,1024]{1,0:T(8,128)(2,1)} %bitcast.6, bf16[1024,1024]{1,0:T(8,128)(2,1)} %bitcast.7, ...), custom_call_target="tpu_custom_call" | custom-call | bytes 6291456 | tf_op jit(solution)/shard_map/pallas_call | solution.py:29
  11.0 0.7 %collective-permute-done.2.refs_2_ = bf16[2,16,1024]{2,1,0:T(8,128)(2,1)S(1)} collective-permute-done((bf16[2,16,1024]{2,1,0:T(8,128)(2,1)S(1)}, bf16[2,16,1024]{2,1,0:T(8,128)(2,1)S(1)}, u32[]{:S(2)}, u32[]{:S(2)}) %collective-permute-start.2) | collective-permute-done | bytes 65568 | tf_op jit(solution)/shard_map/ppermute | solution.py:261
  11.8 0.5 %collective-permute-done.3.refs_3_ = bf16[2,16,1024]{2,1,0:T(8,128)(2,1)S(1)} collective-permute-done((bf16[2,16,1024]{2,1,0:T(8,128)(2,1)S(1)}, bf16[2,16,1024]{2,1,0:T(8,128)(2,1)S(1)}, u32[]{:S(2)}, u32[]{:S(2)}) %collective-permute-start.3) | collective-permute-done | bytes 65568 | tf_op jit(solution)/shard_map/ppermute | solution.py:261
  12.3 1.2 %shard_map.122 = (bf16[3,16,1024]{2,1,0:T(8,128)(2,1)S(1)}, bf16[3,16,1024]{2,1,0:T(8,128)(2,1)S(1)}, bf16[3,16,1024]{2,1,0:T(8,128)(2,1)S(1)}, bf16[3,16,1024]{...) custom-call(bf16[2,16,1024]{2,1,0:T(8,128)(2,1)S(1)} %get-tuple-element.38.after_hbm.refs_0_, ...), custom_call_target="tpu_custom_call" | custom-call | flops 402653184 | tf_op jit(solution)/shard_map/pallas_call | solution.py:29
  13.5 1.6 %collective-permute-start.4 = (bf16[3,16,1024]{2,1,0:T(8,128)(2,1)S(1)}, bf16[3,16,1024]{2,1,0:T(8,128)(2,1)S(1)}, u32[]{:S(2)}, u32[]{:S(2)}) collective-permute-start(bf16[3,16,1024]{2,1,0:T(8,128)(2,1)S(1)} %get-tuple-element.49), channel_id=1, source_target_pairs={{0,8},{1,25},{2,10},{3,27},{4,12},{5,29},{6,14},{7,31},{8,0},{9,17... | collective-permute-start | bytes 294920 | tf_op jit(solution)/shard_map/ppermute | solution.py:271
  15.1 2.6 %collective-permute-start.5 = (bf16[3,16,1024]{2,1,0:T(8,128)(2,1)S(1)}, bf16[3,16,1024]{2,1,0:T(8,128)(2,1)S(1)}, u32[]{:S(2)}, u32[]{:S(2)}) collective-permute-start(bf16[3,16,1024]{2,1,0:T(8,128)(2,1)S(1)} %get-tuple-element.50), channel_id=1, source_target_pairs={{0,16},{1,17},{2,18},{3,19},{4,20},{5,21},{6,22},{7,23},{8,24},{9,... | collective-permute-start | bytes 294920 | tf_op jit(solution)/shard_map/ppermute | solution.py:271
  17.7 0.2 collective-permute-start.6
  18.0 3.2 %collective-permute-done.4.refs_1_ = bf16[3,16,1024]{2,1,0:T(8,128)(2,1)S(1)} collective-permute-done((bf16[3,16,1024]{2,1,0:T(8,128)(2,1)S(1)}, bf16[3,16,1024]{2,1,0:T(8,128)(2,1)S(1)}, u32[]{:S(2)}, u32[]{:S(2)}) %collective-permute-start.4) | collective-permute-done | bytes 98336 | tf_op jit(solution)/shard_map/ppermute | solution.py:271
  21.2 1.4 %collective-permute-done.5.refs_2_ = bf16[3,16,1024]{2,1,0:T(8,128)(2,1)S(1)} collective-permute-done((bf16[3,16,1024]{2,1,0:T(8,128)(2,1)S(1)}, bf16[3,16,1024]{2,1,0:T(8,128)(2,1)S(1)}, u32[]{:S(2)}, u32[]{:S(2)}) %collective-permute-start.5) | collective-permute-done | bytes 98336 | tf_op jit(solution)/shard_map/ppermute | solution.py:271
  22.6 1.6 %collective-permute-done.6.refs_3_ = bf16[3,16,1024]{2,1,0:T(8,128)(2,1)S(1)} collective-permute-done((bf16[3,16,1024]{2,1,0:T(8,128)(2,1)S(1)}, bf16[3,16,1024]{2,1,0:T(8,128)(2,1)S(1)}, u32[]{:S(2)}, u32[]{:S(2)}) %collective-permute-start.6) | collective-permute-done | bytes 98336 | tf_op jit(solution)/shard_map/ppermute | solution.py:271
  24.3 0.1 shard_map.124.refs_3_.refs_2_
  24.3 2.5 %collective-permute-start.9 = (bf16[3,16,1024]{2,1,0:T(8,128)(2,1)S(1)}, bf16[3,16,1024]{2,1,0:T(8,128)(2,1)S(1)}, u32[]{:S(2)}, u32[]{:S(2)}) collective-permute-start(bf16[3,16,1024]{2,1,0:T(8,128)(2,1)S(1)} %shard_map.124.refs_3_.refs_2_), channel_id=1, source_target_pairs={{0,16},{1,17},{2,18},{3,19},{4,20},{5,21},{6,22},{7,23},{8,24},{9,... | collective-permute-start | bytes 294920 | tf_op jit(solution)/shard_map/ppermute | solution.py:271
  26.9 0.8 %collective-permute-start.8 = (bf16[3,16,1024]{2,1,0:T(8,128)(2,1)S(1)}, bf16[3,16,1024]{2,1,0:T(8,128)(2,1)S(1)}, u32[]{:S(2)}, u32[]{:S(2)}) collective-permute-start(bf16[3,16,1024]{2,1,0:T(8,128)(2,1)S(1)} %shard_map.124.refs_3_.refs_2_), channel_id=1, source_target_pairs={{0,8},{1,25},{2,10},{3,27},{4,12},{5,29},{6,14},{7,31},{8,0},{9,17... | collective-permute-start | bytes 294920 | tf_op jit(solution)/shard_map/ppermute | solution.py:271
  27.6 1.2 %collective-permute-start.7 = (bf16[3,16,1024]{2,1,0:T(8,128)(2,1)S(1)}, bf16[3,16,1024]{2,1,0:T(8,128)(2,1)S(1)}, u32[]{:S(2)}, u32[]{:S(2)}) collective-permute-start(bf16[3,16,1024]{2,1,0:T(8,128)(2,1)S(1)} %shard_map.124.refs_3_.refs_2_), channel_id=1, source_target_pairs={{0,24},{1,9},{2,26},{3,11},{4,28},{5,13},{6,30},{7,15},{8,16},{9,1... | collective-permute-start | bytes 294920 | tf_op jit(solution)/shard_map/ppermute | solution.py:271
  28.8 1.2 %shard_map.123 = (bf16[1024,1024]{1,0:T(8,128)(2,1)S(1)}, bf16[1024,1024]{1,0:T(8,128)(2,1)S(1)}) custom-call(bf16[3,16,1024]{2,1,0:T(8,128)(2,1)S(1)} %get-tuple-element.45.after_hbm.refs_0_, bf16[1024,1024]{1,0:T(8,128)(2,1)S(1)} %get-tuple-element.42.refs_4_.gate_ref, bf16[1024,1024]{1,0:T(8,128)(2,1)S(1)} %get-tuple-element.43.refs_5_.up_ref), custom_call_target="tpu_custom_call" | custom-call | bytes 16777216 | tf_op jit(solution)/shard_map/pallas_call | solution.py:29
  30.0 2.6 %collective-permute-done.9.refs_6_.refs_5_ = bf16[3,16,1024]{2,1,0:T(8,128)(2,1)S(1)} collective-permute-done((bf16[3,16,1024]{2,1,0:T(8,128)(2,1)S(1)}, bf16[3,16,1024]{2,1,0:T(8,128)(2,1)S(1)}, u32[]{:S(2)}, u32[]{:S(2)}) %collective-permute-start.9) | collective-permute-done | bytes 98336 | tf_op jit(solution)/shard_map/ppermute | solution.py:271
  32.6 0.5 %collective-permute-done.8.refs_5_.refs_4_ = bf16[3,16,1024]{2,1,0:T(8,128)(2,1)S(1)} collective-permute-done((bf16[3,16,1024]{2,1,0:T(8,128)(2,1)S(1)}, bf16[3,16,1024]{2,1,0:T(8,128)(2,1)S(1)}, u32[]{:S(2)}, u32[]{:S(2)}) %collective-permute-start.8) | collective-permute-done | bytes 98336 | tf_op jit(solution)/shard_map/ppermute | solution.py:271
  33.1 1.1 %collective-permute-done.7.refs_4_.refs_3_ = bf16[3,16,1024]{2,1,0:T(8,128)(2,1)S(1)} collective-permute-done((bf16[3,16,1024]{2,1,0:T(8,128)(2,1)S(1)}, bf16[3,16,1024]{2,1,0:T(8,128)(2,1)S(1)}, u32[]{:S(2)}, u32[]{:S(2)}) %collective-permute-start.7) | collective-permute-done | bytes 98336 | tf_op jit(solution)/shard_map/ppermute | solution.py:271
  34.2 1.2 %shard_map.125 = (bf16[4,16,1024]{2,1,0:T(8,128)(2,1)S(1)}, bf16[4,16,1024]{2,1,0:T(8,128)(2,1)S(1)}) custom-call(bf16[1024,1024]{1,0:T(8,128)(2,1)S(1)} %get-tuple-element.46.refs_0_, bf16[1024,1024]{1,0:T(8,128)(2,1)S(1)} %get-tuple-element.47.refs_1_, bf16[1024,1024]{1,0:T(8,128)(2,1)S(1)} %get-tuple-element.48.refs_2_, ...), custom_call_target="tpu_custom_call" | custom-call | flops 402653184 | tf_op jit(solution)/shard_map/pallas_call | solution.py:29
  35.5 1.3 %collective-permute-done.10.got_ref = bf16[4,16,1024]{2,1,0:T(8,128)(2,1)S(1)} collective-permute-done((bf16[4,16,1024]{2,1,0:T(8,128)(2,1)S(1)}, bf16[4,16,1024]{2,1,0:T(8,128)(2,1)S(1)}, u32[]{:S(2)}, u32[]{:S(2)}) %collective-permute-start.10) | collective-permute-done | bytes 131104 | tf_op jit(solution)/shard_map/ppermute | solution.py:261
  36.8 2.3 %collective-permute-start.11 = (bf16[2,16,1024]{2,1,0:T(8,128)(2,1)S(1)}, bf16[2,16,1024]{2,1,0:T(8,128)(2,1)S(1)}, u32[]{:S(2)}, u32[]{:S(2)}) collective-permute-start(bf16[2,16,1024]{2,1,0:T(8,128)(2,1)S(1)} %get-tuple-element.55), channel_id=1, source_target_pairs={{0,6},{1,7},{2,4},{3,5},{4,2},{5,3},{6,0},{7,1},{8,14},{9,15},{10,... | collective-permute-start | bytes 196616 | tf_op jit(solution)/shard_map/ppermute | solution.py:261
  39.1 0.5 %collective-permute-start.12 = (bf16[2,16,1024]{2,1,0:T(8,128)(2,1)S(1)}, bf16[2,16,1024]{2,1,0:T(8,128)(2,1)S(1)}, u32[]{:S(2)}, u32[]{:S(2)}) collective-permute-start(bf16[2,16,1024]{2,1,0:T(8,128)(2,1)S(1)} %get-tuple-element.56), channel_id=1, source_target_pairs={{0,2},{1,3},{2,0},{3,1},{4,6},{5,7},{6,4},{7,5},{8,10},{9,11},{10,... | collective-permute-start | bytes 196616 | tf_op jit(solution)/shard_map/ppermute | solution.py:261
  39.7 0.7 %collective-permute-start.13 = (bf16[2,16,1024]{2,1,0:T(8,128)(2,1)S(1)}, bf16[2,16,1024]{2,1,0:T(8,128)(2,1)S(1)}, u32[]{:S(2)}, u32[]{:S(2)}) collective-permute-start(bf16[2,16,1024]{2,1,0:T(8,128)(2,1)S(1)} %get-tuple-element.57), channel_id=1, source_target_pairs={{0,4},{1,5},{2,6},{3,7},{4,0},{5,1},{6,2},{7,3},{8,12},{9,13},{10,... | collective-permute-start | bytes 196616 | tf_op jit(solution)/shard_map/ppermute | solution.py:261
  40.4 3.1 %shard_map.128 = (bf16[1,1024,1024]{2,1,0:T(8,128)(2,1)}, bf16[1,1024,1024]{2,1,0:T(8,128)(2,1)}, bf16[1,1024,1024]{2,1,0:T(8,128)(2,1)}) custom-call(bf16[64,1024]{1,0:T(8,128)(2,1)S(1)} %get-tuple-element.62.refs_0_, bf16[64,1024]{1,0:T(8,128)(2,1)S(1)} %get-tuple-element.63.refs_1_, bf16[3,16,1024]{2,1,0:T(8,128)(2,1)S(1)} %shard_map.124.refs_3_.refs_2_, ...), custom_call_target="tpu_custom_call" | custom-call | flops 402653184 | bytes 6291456 | tf_op jit(solution)/shard_map/pallas_call | solution.py:29
  43.5 0.4 collective-permute-done.13.refs_3_
  43.9 1.0 %shard_map.127 = (bf16[128,1024]{1,0:T(8,128)(2,1)}, bf16[128,1024]{1,0:T(8,128)(2,1)}) custom-call(bf16[2,16,1024]{2,1,0:T(8,128)(2,1)S(1)} %get-tuple-element.54.refs_0_, bf16[2,16,1024]{2,1,0:T(8,128)(2,1)S(1)} %collective-permute-done.11.refs_1_, bf16[2,16,1024]{2,1,0:T(8,128)(2,1)S(1)} %collective-permute-done.12.refs_2_, ...), custom_call_target="tpu_custom_call" | custom-call | tf_op jit(solution)/shard_map/pallas_call | solution.py:29
  (6 shorter events, 0.1 us)
Async XLA Ops:
  2.1 1.5 %collective-permute-start = (bf16[4,16,1024]{2,1,0:T(8,128)(2,1)S(1)}, bf16[4,16,1024]{2,1,0:T(8,128)(2,1)S(1)}, u32[]{:S(2)}, u32[]{:S(2)}) collective-permute-start(bf16[4,16,1024]{2,1,0:T(8,128)(2,1)S(1)} %get-tuple-element.37), channel_id=1, source_target_pairs={{0,1},{1,0},{2,3},{3,2},{4,5},{5,4},{6,7},{7,6},{8,9},{9,8},{10,11... | collective-permute-start | bytes 393224 | tf_op jit(solution)/shard_map/ppermute | solution.py:261
  3.6 7.4 %collective-permute-start.1 = (bf16[2,16,1024]{2,1,0:T(8,128)(2,1)S(1)}, bf16[2,16,1024]{2,1,0:T(8,128)(2,1)S(1)}, u32[]{:S(2)}, u32[]{:S(2)}) collective-permute-start(bf16[2,16,1024]{2,1,0:T(8,128)(2,1)S(1)} %get-tuple-element.39), channel_id=1, source_target_pairs={{0,6},{1,7},{2,4},{3,5},{4,2},{5,3},{6,0},{7,1},{8,14},{9,15},{10,... | collective-permute-start | bytes 196616 | tf_op jit(solution)/shard_map/ppermute | solution.py:261
  7.5 4.3 %collective-permute-start.2 = (bf16[2,16,1024]{2,1,0:T(8,128)(2,1)S(1)}, bf16[2,16,1024]{2,1,0:T(8,128)(2,1)S(1)}, u32[]{:S(2)}, u32[]{:S(2)}) collective-permute-start(bf16[2,16,1024]{2,1,0:T(8,128)(2,1)S(1)} %get-tuple-element.40), channel_id=1, source_target_pairs={{0,2},{1,3},{2,0},{3,1},{4,6},{5,7},{6,4},{7,5},{8,10},{9,11},{10,... | collective-permute-start | bytes 196616 | tf_op jit(solution)/shard_map/ppermute | solution.py:261
  8.0 4.3 %collective-permute-start.3 = (bf16[2,16,1024]{2,1,0:T(8,128)(2,1)S(1)}, bf16[2,16,1024]{2,1,0:T(8,128)(2,1)S(1)}, u32[]{:S(2)}, u32[]{:S(2)}) collective-permute-start(bf16[2,16,1024]{2,1,0:T(8,128)(2,1)S(1)} %get-tuple-element.41), channel_id=1, source_target_pairs={{0,4},{1,5},{2,6},{3,7},{4,0},{5,1},{6,2},{7,3},{8,12},{9,13},{10,... | collective-permute-start | bytes 196616 | tf_op jit(solution)/shard_map/ppermute | solution.py:261
  13.5 7.7 %collective-permute-start.4 = (bf16[3,16,1024]{2,1,0:T(8,128)(2,1)S(1)}, bf16[3,16,1024]{2,1,0:T(8,128)(2,1)S(1)}, u32[]{:S(2)}, u32[]{:S(2)}) collective-permute-start(bf16[3,16,1024]{2,1,0:T(8,128)(2,1)S(1)} %get-tuple-element.49), channel_id=1, source_target_pairs={{0,8},{1,25},{2,10},{3,27},{4,12},{5,29},{6,14},{7,31},{8,0},{9,17... | collective-permute-start | bytes 294920 | tf_op jit(solution)/shard_map/ppermute | solution.py:271
  15.1 7.5 %collective-permute-start.5 = (bf16[3,16,1024]{2,1,0:T(8,128)(2,1)S(1)}, bf16[3,16,1024]{2,1,0:T(8,128)(2,1)S(1)}, u32[]{:S(2)}, u32[]{:S(2)}) collective-permute-start(bf16[3,16,1024]{2,1,0:T(8,128)(2,1)S(1)} %get-tuple-element.50), channel_id=1, source_target_pairs={{0,16},{1,17},{2,18},{3,19},{4,20},{5,21},{6,22},{7,23},{8,24},{9,... | collective-permute-start | bytes 294920 | tf_op jit(solution)/shard_map/ppermute | solution.py:271
  17.7 6.5 %collective-permute-start.6 = (bf16[3,16,1024]{2,1,0:T(8,128)(2,1)S(1)}, bf16[3,16,1024]{2,1,0:T(8,128)(2,1)S(1)}, u32[]{:S(2)}, u32[]{:S(2)}) collective-permute-start(bf16[3,16,1024]{2,1,0:T(8,128)(2,1)S(1)} %get-tuple-element.51), channel_id=1, source_target_pairs={{0,24},{1,9},{2,26},{3,11},{4,28},{5,13},{6,30},{7,15},{8,16},{9,1... | collective-permute-start | bytes 294920 | tf_op jit(solution)/shard_map/ppermute | solution.py:271
  24.3 8.3 %collective-permute-start.9 = (bf16[3,16,1024]{2,1,0:T(8,128)(2,1)S(1)}, bf16[3,16,1024]{2,1,0:T(8,128)(2,1)S(1)}, u32[]{:S(2)}, u32[]{:S(2)}) collective-permute-start(bf16[3,16,1024]{2,1,0:T(8,128)(2,1)S(1)} %shard_map.124.refs_3_.refs_2_), channel_id=1, source_target_pairs={{0,16},{1,17},{2,18},{3,19},{4,20},{5,21},{6,22},{7,23},{8,24},{9,... | collective-permute-start | bytes 294920 | tf_op jit(solution)/shard_map/ppermute | solution.py:271
  26.9 6.2 %collective-permute-start.8 = (bf16[3,16,1024]{2,1,0:T(8,128)(2,1)S(1)}, bf16[3,16,1024]{2,1,0:T(8,128)(2,1)S(1)}, u32[]{:S(2)}, u32[]{:S(2)}) collective-permute-start(bf16[3,16,1024]{2,1,0:T(8,128)(2,1)S(1)} %shard_map.124.refs_3_.refs_2_), channel_id=1, source_target_pairs={{0,8},{1,25},{2,10},{3,27},{4,12},{5,29},{6,14},{7,31},{8,0},{9,17... | collective-permute-start | bytes 294920 | tf_op jit(solution)/shard_map/ppermute | solution.py:271
  27.6 6.5 %collective-permute-start.7 = (bf16[3,16,1024]{2,1,0:T(8,128)(2,1)S(1)}, bf16[3,16,1024]{2,1,0:T(8,128)(2,1)S(1)}, u32[]{:S(2)}, u32[]{:S(2)}) collective-permute-start(bf16[3,16,1024]{2,1,0:T(8,128)(2,1)S(1)} %shard_map.124.refs_3_.refs_2_), channel_id=1, source_target_pairs={{0,24},{1,9},{2,26},{3,11},{4,28},{5,13},{6,30},{7,15},{8,16},{9,1... | collective-permute-start | bytes 294920 | tf_op jit(solution)/shard_map/ppermute | solution.py:271
  35.4 1.4 %collective-permute-start.10 = (bf16[4,16,1024]{2,1,0:T(8,128)(2,1)S(1)}, bf16[4,16,1024]{2,1,0:T(8,128)(2,1)S(1)}, u32[]{:S(2)}, u32[]{:S(2)}) collective-permute-start(bf16[4,16,1024]{2,1,0:T(8,128)(2,1)S(1)} %get-tuple-element.53), channel_id=1, source_target_pairs={{0,1},{1,0},{2,3},{3,2},{4,5},{5,4},{6,7},{7,6},{8,9},{9,8},{10,11... | collective-permute-start | bytes 393224 | tf_op jit(solution)/shard_map/ppermute | solution.py:261
  36.8 6.6 %collective-permute-start.11 = (bf16[2,16,1024]{2,1,0:T(8,128)(2,1)S(1)}, bf16[2,16,1024]{2,1,0:T(8,128)(2,1)S(1)}, u32[]{:S(2)}, u32[]{:S(2)}) collective-permute-start(bf16[2,16,1024]{2,1,0:T(8,128)(2,1)S(1)} %get-tuple-element.55), channel_id=1, source_target_pairs={{0,6},{1,7},{2,4},{3,5},{4,2},{5,3},{6,0},{7,1},{8,14},{9,15},{10,... | collective-permute-start | bytes 196616 | tf_op jit(solution)/shard_map/ppermute | solution.py:261
  39.1 4.3 %collective-permute-start.12 = (bf16[2,16,1024]{2,1,0:T(8,128)(2,1)S(1)}, bf16[2,16,1024]{2,1,0:T(8,128)(2,1)S(1)}, u32[]{:S(2)}, u32[]{:S(2)}) collective-permute-start(bf16[2,16,1024]{2,1,0:T(8,128)(2,1)S(1)} %get-tuple-element.56), channel_id=1, source_target_pairs={{0,2},{1,3},{2,0},{3,1},{4,6},{5,7},{6,4},{7,5},{8,10},{9,11},{10,... | collective-permute-start | bytes 196616 | tf_op jit(solution)/shard_map/ppermute | solution.py:261
  39.7 4.3 %collective-permute-start.13 = (bf16[2,16,1024]{2,1,0:T(8,128)(2,1)S(1)}, bf16[2,16,1024]{2,1,0:T(8,128)(2,1)S(1)}, u32[]{:S(2)}, u32[]{:S(2)}) collective-permute-start(bf16[2,16,1024]{2,1,0:T(8,128)(2,1)S(1)} %get-tuple-element.57), channel_id=1, source_target_pairs={{0,4},{1,5},{2,6},{3,7},{4,0},{5,1},{6,2},{7,3},{8,12},{9,13},{10,... | collective-permute-start | bytes 196616 | tf_op jit(solution)/shard_map/ppermute | solution.py:261

commit v5 on v4

--- a/solution.py
+++ b/solution.py
@@ -8,6 +8,7 @@
 CAP = 8
 CORES = 2
 TILE = 256
+EARLY = 2
 F32 = jnp.float32
 BF16 = jnp.bfloat16
 VMEM_SPEC = pl.BlockSpec(memory_space=pltpu.VMEM)
@@ -21,7 +22,8 @@
 
 
 def call(
-    kernel, out_shape, in_specs=None, out_specs=None, scratch=(), flops=0, bytes_accessed=0, mib=8
+    kernel, out_shape, in_specs=None, out_specs=None, scratch=(), flops=0, bytes_accessed=0, mib=8,
+    aliases=None,
 ):
     many = isinstance(out_shape, (tuple, list))
 
@@ -32,6 +34,7 @@
             in_specs=in_specs or [VMEM_SPEC] * len(args),
             out_specs=out_specs or ([VMEM_SPEC] * len(out_shape) if many else VMEM_SPEC),
             scratch_shapes=scratch,
+            input_output_aliases=aliases or {},
             compiler_params=pltpu.CompilerParams(vmem_limit_bytes=mib << 20),
             cost_estimate=pl.CostEstimate(
                 flops=flops, bytes_accessed=bytes_accessed, transcendentals=0
@@ -198,39 +201,34 @@
 
 
 def output_kernel(*refs):
-    (gate_ref, up_ref, down_ref), acts = refs[:3], sort_back(refs[3:-3])
-    mine_ref, theirs_ref, blocks_ref = refs[-3:]
+    (gate_ref, up_ref, down_ref), refs, blocks_ref = refs[:3], refs[3:-1], refs[-1]
     owners, _, features = blocks_ref.shape
-    step = owners // len(acts)
+    chips = owners // CORES
+    acts, sends = sort_back(refs[:-chips]), refs[-chips:]
+    shares = len(acts)
+    step = owners // shares
     hidden, gate_grad, up_grad = (jnp.concatenate([a[i] for a in acts], axis=0) for i in range(3))
     out = dot(hidden, down_ref[...], 1, 0)
     back = dot(gate_grad, gate_ref[...], 1, 0) + dot(up_grad, up_ref[...], 1, 0)
     both = jnp.concatenate(
         [out.reshape(owners, CAP, features), back.reshape(owners, CAP, features)], axis=1
     ).astype(BF16)
-    shares = len(acts)
     for s in range(shares):
         blocks_ref[pl.ds(peer(shares, s) * step, step)] = both[s * step : (s + 1) * step]
-    for k in range(owners // CORES):
-        mine_ref[k] = blocks_ref[CORES * k]
-        theirs_ref[k] = blocks_ref[CORES * k + 1]
-
-
-def weight_kernel(*refs):
-    (rows_ref, grads_ref), acts = refs[:2], sort_back(refs[2:-7])
-    gate_hbm, up_hbm, down_hbm, gate_ref, up_ref, down_ref, sems = refs[-7:]
-    rows, grads = rows_ref[...], grads_ref[...]
-    hidden, gate_grad, up_grad = (jnp.concatenate([a[i] for a in acts], axis=0) for i in range(3))
+    for k, send in enumerate(sends):
+        send[...] = blocks_ref[CORES * k : CORES * k + CORES]
+
+
+def pass_kernel(*refs):
+    direct, out_ref = refs[1:-1], refs[-1]
+    for k, ref in enumerate(sort_back(direct)):
+        out_ref[k] = ref[1]
+
+
+def stream_products(products, sems):
     copies = []
-    for i, (left, right, out_ref, out_hbm) in enumerate(
-        (
-            (rows, gate_grad, gate_ref, gate_hbm),
-            (rows, up_grad, up_ref, up_hbm),
-            (hidden, grads, down_ref, down_hbm),
-        )
-    ):
-        count = out_ref.shape[0] // TILE
-        for j in range(count):
+    for i, (left, right, out_ref, out_hbm, first, last) in enumerate(products):
+        for j in range(first, last):
             part = slice(j * TILE, (j + 1) * TILE)
             out_ref[part] = dot(left[:, part], right, 0, 0).astype(BF16)
             copy = pltpu.make_async_copy(out_ref.at[part], out_hbm.at[0, part], sems.at[i, j])
@@ -240,9 +238,37 @@
         copy.wait()
 
 
+def weight_kernel(*refs):
+    (rows_ref, grads_ref), acts = refs[:2], sort_back(refs[2:-8])
+    gate_hbm, up_hbm, down_hbm, done_ref, gate_ref, up_ref, down_ref, sems = refs[-8:]
+    done_ref[...] = jnp.zeros_like(done_ref)
+    rows, grads = rows_ref[...], grads_ref[...]
+    hidden, gate_grad, up_grad = (jnp.concatenate([a[i] for a in acts], axis=0) for i in range(3))
+    tiles = gate_ref.shape[0] // TILE
+    stream_products(
+        (
+            (rows, gate_grad, gate_ref, gate_hbm, 0, tiles),
+            (rows, up_grad, up_ref, up_hbm, 0, tiles),
+            (hidden, grads, down_ref, down_hbm, 0, EARLY),
+        ),
+        sems,
+    )
+
+
+def down_kernel(*refs):
+    grads_ref, acts = refs[2], sort_back(refs[3:-3])
+    down_hbm, down_ref, sems = refs[-3:]
+    hidden = jnp.concatenate([a[0] for a in acts], axis=0)
+    last = down_ref.shape[0] // TILE
+    stream_products(((hidden, grads_ref[...], down_ref, down_hbm, EARLY, last),), sems)
+
+
 def combine_kernel(*refs):
-    got, (place_ref, blend_ref, mixed_ref, rows_ref) = sort_back(refs[:-4]), refs[-4:]
-    outs, backs = unpack(jnp.concatenate([ref[...] for ref in got], axis=0))
+    direct, (passed_ref, place_ref, blend_ref, mixed_ref, rows_ref) = refs[:-5], refs[-5:]
+    blocks = []
+    for k, ref in enumerate(sort_back(direct)):
+        blocks += [ref[0], passed_ref[k]]
+    outs, backs = unpack(jnp.stack(blocks, axis=0))
     mixed_ref[...] = dot(blend_ref[...], outs, 0, 0).astype(BF16)
     rows_ref[...] = dot(place_ref[...], backs, 0, 0).astype(BF16)
 
@@ -327,17 +353,24 @@
     summed = [trade_dp(partials[s], s) if s else partials[0] for s in range(shares)]
     act = call(gating_kernel, shape((3, share, width), BF16))(*summed)
     acts = [trade_dp(act, s) if s else act for s in most_bits_first(shares)]
-    back = swap(
-        *call(output_kernel, (half, half), scratch=[blocks], flops=3 * one)(*flipped, down_w, *acts),
-    )
-    grad_gate, grad_up, grad_down = call(
+    outs = call(
+        output_kernel,
+        (shape((CORES, 2 * CAP, features), BF16),) * chips,
+        scratch=[blocks],
+        flops=3 * one,
+    )(*flipped, down_w, *acts)
+    back = [
+        trade(outs[k], "expert", CORES * k) if k else outs[0] for k in most_bits_first(chips)
+    ]
+    grad_gate, grad_up, grad_down, done = call(
         weight_kernel,
         (
             shape((1, features, width), BF16),
             shape((1, features, width), BF16),
             shape((1, width, features), BF16),
+            pltpu.VMEM((8, 128), F32),
         ),
-        out_specs=[HBM_SPEC] * 3,
+        out_specs=[HBM_SPEC] * 3 + [VMEM_SPEC],
         scratch=[
             pltpu.VMEM((features, width), BF16),
             pltpu.VMEM((features, width), BF16),
@@ -348,9 +381,28 @@
         bytes_accessed=6 * features * width,
         mib=16,
     )(rows, grads, *acts)
+    passed = call(
+        pass_kernel,
+        shape((chips, 2 * CAP, features), BF16),
+        in_specs=[VMEM_SPEC] * (chips + 1),
+    )(done, *back)
+    any_spec = pl.BlockSpec(memory_space=pl.ANY)
+    grad_down = call(
+        down_kernel,
+        shape((1, width, features), BF16),
+        in_specs=[any_spec] * 2 + [VMEM_SPEC] * (shares + 1),
+        out_specs=any_spec,
+        scratch=[
+            pltpu.VMEM((width, features), BF16),
+            pltpu.SemaphoreType.DMA((1, width // TILE)),
+        ],
+        flops=one // 2,
+        bytes_accessed=features * width,
+        aliases={0: 0},
+    )(grad_down, passed, grads, *acts)
     mixed_out, grad_rows = call(
         combine_kernel, (shape((tokens, features), BF16), shape((tokens, features), BF16))
-    )(*back, place, blend)
+    )(*back, trade(passed, "expert", 1), place, blend)
     return mixed_out, grad_rows, grad_gate, grad_up, grad_down
 
 

time: 45.2 us -> 45.2 us (level)
  Pallas kernels: 12.2 us -> 13.2 us
  waiting for transfers between devices: 14.5 us -> 13.5 us
    ppermute x8, waiting for transfers between devices: 4.01 us -> 3.01 us  [trade(): return lax.ppermute(array, axis, [(i, i ^ distance) for i in range(count)])]
    pallas_call x10 -> x11, Pallas kernels: 12.2 us -> 13.2 us  [run(): pl.pallas_call(kernel, out_shape=out_shape, in_specs=in_specs or [VMEM_SP...]
  transfers between devices with their start and end apart: 14 -> 14, of which waited for: 11 -> 11; matrix products, arithmetic and copies ran while one was open for 0% -> 0% of each run, Pallas kernels for 16% -> 18%
where the time goes in v5:
time: 45.2 us; the launch traced here: 45 us
  starting transfers between devices  17.6 us (39%)
  waiting for transfers between devices  13.5 us (30%)
  Pallas kernels  13.2 us (29%)
  between operations  0.74 us (2%)
    pallas_call x11, Pallas kernels, run(): pl.pallas_call(kernel, out_shape=out_shape, in_specs=in_specs or [VMEM_SP...  13.2 us
    ppermute x6, waiting for transfers between devices, trade_dp(): return lax.ppermute(array, ('dp', 'expert'), pairs)  10.4 us
    ppermute x6, starting transfers between devices, trade_dp(): return lax.ppermute(array, ('dp', 'expert'), pairs)  8.9 us
    ppermute x8, starting transfers between devices, trade(): return lax.ppermute(array, axis, [(i, i ^ distance) for i in range(count)])  8.66 us
    ppermute x8, waiting for transfers between devices, trade(): return lax.ppermute(array, axis, [(i, i ^ distance) for i in range(count)])  3.01 us
  transfers between devices with their start and end apart: 14, of which 11 were waited for; matrix products, arithmetic and copies ran while one was open for 0% of the time, Pallas kernels for 18%

profile of v5, /device:TPU:0, one launch (start us, length us, event | category | flops | bytes accessed | tf_op | source)
XLA Modules:
  0.0 45.0 jit_solution(11413723233826247510)
XLA Ops:
  0.6 1.5 %shard_map.119 = (bf16[4,16,1024]{2,1,0:T(8,128)(2,1)S(1)}, bf16[4,16,1024]{2,1,0:T(8,128)(2,1)S(1)}, bf16[64,128]{1,0:T(8,128)(2,1)S(1)}, bf16[64,128]{1,0:T(8,128)(2,1)S(1)}) custom-call(s32[8,128]{1,0:T(8,128)} %bitcast.9, f32[8,128]{1,0:T(8,128)} %bitcast.10, bf16[8,128]{1,0:T(8,128)(2,1)} %bitcast.11, bf16[128,1024]{1,0:T(8,128)(2,1)} %codes_hbm.1, ...), custom_call_target="tpu_custom_call" | custom-call | tf_op jit(solution)/shard_map/pallas_call | solution.py:31
  2.1 0.5 %collective-permute-start = (bf16[4,16,1024]{2,1,0:T(8,128)(2,1)S(1)}, bf16[4,16,1024]{2,1,0:T(8,128)(2,1)S(1)}, u32[]{:S(2)}, u32[]{:S(2)}) collective-permute-start(bf16[4,16,1024]{2,1,0:T(8,128)(2,1)S(1)} %get-tuple-element.36), channel_id=1, source_target_pairs={{0,1},{1,0},{2,3},{3,2},{4,5},{5,4},{6,7},{7,6},{8,9},{9,8},{10,11... | collective-permute-start | bytes 393224 | tf_op jit(solution)/shard_map/ppermute | solution.py:287
  2.6 1.0 %collective-permute-done.got_ref = bf16[4,16,1024]{2,1,0:T(8,128)(2,1)S(1)} collective-permute-done((bf16[4,16,1024]{2,1,0:T(8,128)(2,1)S(1)}, bf16[4,16,1024]{2,1,0:T(8,128)(2,1)S(1)}, u32[]{:S(2)}, u32[]{:S(2)}) %collective-permute-start) | collective-permute-done | bytes 131104 | tf_op jit(solution)/shard_map/ppermute | solution.py:287
  3.6 3.9 %collective-permute-start.1 = (bf16[2,16,1024]{2,1,0:T(8,128)(2,1)S(1)}, bf16[2,16,1024]{2,1,0:T(8,128)(2,1)S(1)}, u32[]{:S(2)}, u32[]{:S(2)}) collective-permute-start(bf16[2,16,1024]{2,1,0:T(8,128)(2,1)S(1)} %get-tuple-element.38), channel_id=1, source_target_pairs={{0,6},{1,7},{2,4},{3,5},{4,2},{5,3},{6,0},{7,1},{8,14},{9,15},{10,... | collective-permute-start | bytes 196616 | tf_op jit(solution)/shard_map/ppermute | solution.py:287
  7.5 0.5 %collective-permute-start.2 = (bf16[2,16,1024]{2,1,0:T(8,128)(2,1)S(1)}, bf16[2,16,1024]{2,1,0:T(8,128)(2,1)S(1)}, u32[]{:S(2)}, u32[]{:S(2)}) collective-permute-start(bf16[2,16,1024]{2,1,0:T(8,128)(2,1)S(1)} %get-tuple-element.39), channel_id=1, source_target_pairs={{0,2},{1,3},{2,0},{3,1},{4,6},{5,7},{6,4},{7,5},{8,10},{9,11},{10,... | collective-permute-start | bytes 196616 | tf_op jit(solution)/shard_map/ppermute | solution.py:287
  8.0 0.1 collective-permute-start.3
  8.1 2.9 %shard_map.121 = (bf16[1024,1024]{1,0:T(8,128)(2,1)S(1)}, bf16[1024,1024]{1,0:T(8,128)(2,1)S(1)}, bf16[1024,1024]{1,0:T(8,128)(2,1)S(1)}, bf16[1024,1024]{1,0:T(8,128)(2,1)S(1)}) custom-call(bf16[2,16,1024]{2,1,0:T(8,128)(2,1)S(1)} %get-tuple-element.37.after_hbm.refs_0_, bf16[1024,1024]{1,0:T(8,128)(2,1)} %bitcast.6, bf16[1024,1024]{1,0:T(8,128)(2,1)} %bitcast.7, ...), custom_call_target="tpu_custom_call" | custom-call | bytes 6291456 | tf_op jit(solution)/shard_map/pallas_call | solution.py:31
  11.0 0.7 %collective-permute-done.2.refs_2_ = bf16[2,16,1024]{2,1,0:T(8,128)(2,1)S(1)} collective-permute-done((bf16[2,16,1024]{2,1,0:T(8,128)(2,1)S(1)}, bf16[2,16,1024]{2,1,0:T(8,128)(2,1)S(1)}, u32[]{:S(2)}, u32[]{:S(2)}) %collective-permute-start.2) | collective-permute-done | bytes 65568 | tf_op jit(solution)/shard_map/ppermute | solution.py:287
  11.8 0.5 %collective-permute-done.3.refs_3_ = bf16[2,16,1024]{2,1,0:T(8,128)(2,1)S(1)} collective-permute-done((bf16[2,16,1024]{2,1,0:T(8,128)(2,1)S(1)}, bf16[2,16,1024]{2,1,0:T(8,128)(2,1)S(1)}, u32[]{:S(2)}, u32[]{:S(2)}) %collective-permute-start.3) | collective-permute-done | bytes 65568 | tf_op jit(solution)/shard_map/ppermute | solution.py:287
  12.3 1.2 %shard_map.122 = (bf16[3,16,1024]{2,1,0:T(8,128)(2,1)S(1)}, bf16[3,16,1024]{2,1,0:T(8,128)(2,1)S(1)}, bf16[3,16,1024]{2,1,0:T(8,128)(2,1)S(1)}, bf16[3,16,1024]{...) custom-call(bf16[2,16,1024]{2,1,0:T(8,128)(2,1)S(1)} %get-tuple-element.37.after_hbm.refs_0_, ...), custom_call_target="tpu_custom_call" | custom-call | flops 402653184 | tf_op jit(solution)/shard_map/pallas_call | solution.py:31
  13.5 1.6 %collective-permute-start.4 = (bf16[3,16,1024]{2,1,0:T(8,128)(2,1)S(1)}, bf16[3,16,1024]{2,1,0:T(8,128)(2,1)S(1)}, u32[]{:S(2)}, u32[]{:S(2)}) collective-permute-start(bf16[3,16,1024]{2,1,0:T(8,128)(2,1)S(1)} %get-tuple-element.48), channel_id=1, source_target_pairs={{0,8},{1,25},{2,10},{3,27},{4,12},{5,29},{6,14},{7,31},{8,0},{9,17... | collective-permute-start | bytes 294920 | tf_op jit(solution)/shard_map/ppermute | solution.py:297
  15.1 2.6 %collective-permute-start.5 = (bf16[3,16,1024]{2,1,0:T(8,128)(2,1)S(1)}, bf16[3,16,1024]{2,1,0:T(8,128)(2,1)S(1)}, u32[]{:S(2)}, u32[]{:S(2)}) collective-permute-start(bf16[3,16,1024]{2,1,0:T(8,128)(2,1)S(1)} %get-tuple-element.49), channel_id=1, source_target_pairs={{0,16},{1,17},{2,18},{3,19},{4,20},{5,21},{6,22},{7,23},{8,24},{9,... | collective-permute-start | bytes 294920 | tf_op jit(solution)/shard_map/ppermute | solution.py:297
  17.7 0.2 collective-permute-start.6
  18.0 3.2 %collective-permute-done.4.refs_1_ = bf16[3,16,1024]{2,1,0:T(8,128)(2,1)S(1)} collective-permute-done((bf16[3,16,1024]{2,1,0:T(8,128)(2,1)S(1)}, bf16[3,16,1024]{2,1,0:T(8,128)(2,1)S(1)}, u32[]{:S(2)}, u32[]{:S(2)}) %collective-permute-start.4) | collective-permute-done | bytes 98336 | tf_op jit(solution)/shard_map/ppermute | solution.py:297
  21.2 1.4 %collective-permute-done.5.refs_2_ = bf16[3,16,1024]{2,1,0:T(8,128)(2,1)S(1)} collective-permute-done((bf16[3,16,1024]{2,1,0:T(8,128)(2,1)S(1)}, bf16[3,16,1024]{2,1,0:T(8,128)(2,1)S(1)}, u32[]{:S(2)}, u32[]{:S(2)}) %collective-permute-start.5) | collective-permute-done | bytes 98336 | tf_op jit(solution)/shard_map/ppermute | solution.py:297
  22.6 1.6 %collective-permute-done.6.refs_3_ = bf16[3,16,1024]{2,1,0:T(8,128)(2,1)S(1)} collective-permute-done((bf16[3,16,1024]{2,1,0:T(8,128)(2,1)S(1)}, bf16[3,16,1024]{2,1,0:T(8,128)(2,1)S(1)}, u32[]{:S(2)}, u32[]{:S(2)}) %collective-permute-start.6) | collective-permute-done | bytes 98336 | tf_op jit(solution)/shard_map/ppermute | solution.py:297
  24.3 2.5 %collective-permute-start.9 = (bf16[3,16,1024]{2,1,0:T(8,128)(2,1)S(1)}, bf16[3,16,1024]{2,1,0:T(8,128)(2,1)S(1)}, u32[]{:S(2)}, u32[]{:S(2)}) collective-permute-start(bf16[3,16,1024]{2,1,0:T(8,128)(2,1)S(1)} %shard_map.124.refs_3_.refs_2_), channel_id=1, source_target_pairs={{0,16},{1,17},{2,18},{3,19},{4,20},{5,21},{6,22},{7,23},{8,24},{9,... | collective-permute-start | bytes 294920 | tf_op jit(solution)/shard_map/ppermute | solution.py:297
  26.9 0.8 %collective-permute-start.8 = (bf16[3,16,1024]{2,1,0:T(8,128)(2,1)S(1)}, bf16[3,16,1024]{2,1,0:T(8,128)(2,1)S(1)}, u32[]{:S(2)}, u32[]{:S(2)}) collective-permute-start(bf16[3,16,1024]{2,1,0:T(8,128)(2,1)S(1)} %shard_map.124.refs_3_.refs_2_), channel_id=1, source_target_pairs={{0,8},{1,25},{2,10},{3,27},{4,12},{5,29},{6,14},{7,31},{8,0},{9,17... | collective-permute-start | bytes 294920 | tf_op jit(solution)/shard_map/ppermute | solution.py:297
  27.6 1.2 %collective-permute-start.7 = (bf16[3,16,1024]{2,1,0:T(8,128)(2,1)S(1)}, bf16[3,16,1024]{2,1,0:T(8,128)(2,1)S(1)}, u32[]{:S(2)}, u32[]{:S(2)}) collective-permute-start(bf16[3,16,1024]{2,1,0:T(8,128)(2,1)S(1)} %shard_map.124.refs_3_.refs_2_), channel_id=1, source_target_pairs={{0,24},{1,9},{2,26},{3,11},{4,28},{5,13},{6,30},{7,15},{8,16},{9,1... | collective-permute-start | bytes 294920 | tf_op jit(solution)/shard_map/ppermute | solution.py:297
  28.8 1.2 %shard_map.123 = (bf16[1024,1024]{1,0:T(8,128)(2,1)S(1)}, bf16[1024,1024]{1,0:T(8,128)(2,1)S(1)}) custom-call(bf16[3,16,1024]{2,1,0:T(8,128)(2,1)S(1)} %get-tuple-element.44.after_hbm.refs_0_, bf16[1024,1024]{1,0:T(8,128)(2,1)S(1)} %get-tuple-element.41.refs_4_.gate_ref, bf16[1024,1024]{1,0:T(8,128)(2,1)S(1)} %get-tuple-element.42.refs_5_.up_ref), custom_call_target="tpu_custom_call" | custom-call | bytes 16777216 | tf_op jit(solution)/shard_map/pallas_call | solution.py:31
  30.0 2.6 %collective-permute-done.9.refs_6_.refs_5_ = bf16[3,16,1024]{2,1,0:T(8,128)(2,1)S(1)} collective-permute-done((bf16[3,16,1024]{2,1,0:T(8,128)(2,1)S(1)}, bf16[3,16,1024]{2,1,0:T(8,128)(2,1)S(1)}, u32[]{:S(2)}, u32[]{:S(2)}) %collective-permute-start.9) | collective-permute-done | bytes 98336 | tf_op jit(solution)/shard_map/ppermute | solution.py:297
  32.6 0.5 %collective-permute-done.8.refs_5_.refs_4_ = bf16[3,16,1024]{2,1,0:T(8,128)(2,1)S(1)} collective-permute-done((bf16[3,16,1024]{2,1,0:T(8,128)(2,1)S(1)}, bf16[3,16,1024]{2,1,0:T(8,128)(2,1)S(1)}, u32[]{:S(2)}, u32[]{:S(2)}) %collective-permute-start.8) | collective-permute-done | bytes 98336 | tf_op jit(solution)/shard_map/ppermute | solution.py:297
  33.1 1.1 %collective-permute-done.7.refs_4_.refs_3_ = bf16[3,16,1024]{2,1,0:T(8,128)(2,1)S(1)} collective-permute-done((bf16[3,16,1024]{2,1,0:T(8,128)(2,1)S(1)}, bf16[3,16,1024]{2,1,0:T(8,128)(2,1)S(1)}, u32[]{:S(2)}, u32[]{:S(2)}) %collective-permute-start.7) | collective-permute-done | bytes 98336 | tf_op jit(solution)/shard_map/ppermute | solution.py:297
  34.2 1.2 %shard_map.125 = (bf16[2,16,1024]{2,1,0:T(8,128)(2,1)S(1)}, bf16[2,16,1024]{2,1,0:T(8,128)(2,1)S(1)}, bf16[2,16,1024]{2,1,0:T(8,128)(2,1)S(1)}, bf16[2,16,1024]{2,1,0:T(8,128)(2,1)S(1)}) custom-call(bf16[1024,1024]{1,0:T(8,128)(2,1)S(1)} %get-tuple-element.45.refs_0_, bf16[1024,1024]{1,0:T(8,128)(2,1)S(1)} %get-tuple-element.46.refs_1_, ...), custom_call_target="tpu_custom_call" | custom-call | flops 402653184 | tf_op jit(solution)/shard_map/pallas_call | solution.py:31
  35.4 2.3 %collective-permute-start.10 = (bf16[2,16,1024]{2,1,0:T(8,128)(2,1)S(1)}, bf16[2,16,1024]{2,1,0:T(8,128)(2,1)S(1)}, u32[]{:S(2)}, u32[]{:S(2)}) collective-permute-start(bf16[2,16,1024]{2,1,0:T(8,128)(2,1)S(1)} %get-tuple-element.52), channel_id=1, source_target_pairs={{0,6},{1,7},{2,4},{3,5},{4,2},{5,3},{6,0},{7,1},{8,14},{9,15},{10,... | collective-permute-start | bytes 196616 | tf_op jit(solution)/shard_map/ppermute | solution.py:287
  37.7 0.5 %collective-permute-start.11 = (bf16[2,16,1024]{2,1,0:T(8,128)(2,1)S(1)}, bf16[2,16,1024]{2,1,0:T(8,128)(2,1)S(1)}, u32[]{:S(2)}, u32[]{:S(2)}) collective-permute-start(bf16[2,16,1024]{2,1,0:T(8,128)(2,1)S(1)} %get-tuple-element.53), channel_id=1, source_target_pairs={{0,2},{1,3},{2,0},{3,1},{4,6},{5,7},{6,4},{7,5},{8,10},{9,11},{10,... | collective-permute-start | bytes 196616 | tf_op jit(solution)/shard_map/ppermute | solution.py:287
  38.2 0.7 %collective-permute-start.12 = (bf16[2,16,1024]{2,1,0:T(8,128)(2,1)S(1)}, bf16[2,16,1024]{2,1,0:T(8,128)(2,1)S(1)}, u32[]{:S(2)}, u32[]{:S(2)}) collective-permute-start(bf16[2,16,1024]{2,1,0:T(8,128)(2,1)S(1)} %get-tuple-element.54), channel_id=1, source_target_pairs={{0,4},{1,5},{2,6},{3,7},{4,0},{5,1},{6,2},{7,3},{8,12},{9,13},{10,... | collective-permute-start | bytes 196616 | tf_op jit(solution)/shard_map/ppermute | solution.py:287
  39.0 2.8 %shard_map.126 = (bf16[1,1024,1024]{2,1,0:T(8,128)(2,1)}, bf16[1,1024,1024]{2,1,0:T(8,128)(2,1)}, bf16[1,1024,1024]{2,1,0:T(8,128)(2,1)}, f32[8,128]{1,0:T(8,128)S(1)}) custom-call(bf16[64,1024]{1,0:T(8,128)(2,1)S(1)} %get-tuple-element.55.refs_0_, bf16[64,1024]{1,0:T(8,128)(2,1)S(1)} %get-tuple-element.56.refs_1_.refs_2_, ...), custom_call_target="tpu_custom_call" | custom-call | flops 402653184 | bytes 6291456 | tf_op jit(solution)/shard_map/pallas_call | solution.py:31
  41.7 0.2 collective-permute-done.11.refs_3_.refs_2_
  42.0 0.5 %collective-permute-done.12.refs_4_.refs_3_ = bf16[2,16,1024]{2,1,0:T(8,128)(2,1)S(1)} collective-permute-done((bf16[2,16,1024]{2,1,0:T(8,128)(2,1)S(1)}, bf16[2,16,1024]{2,1,0:T(8,128)(2,1)S(1)}, u32[]{:S(2)}, u32[]{:S(2)}) %collective-permute-start.12) | collective-permute-done | bytes 65568 | tf_op jit(solution)/shard_map/ppermute | solution.py:287
  42.6 1.3 %shard_map.129 = bf16[1,1024,1024]{2,1,0:T(8,128)(2,1)} custom-call(bf16[1,1024,1024]{2,1,0:T(8,128)(2,1)} %get-tuple-element.64.refs_0_, bf16[4,16,1024]{2,1,0:T(8,128)(2,1)S(1)} %shard_map.127.refs_1_, bf16[64,1024]{1,0:T(8,128)(2,1)S(1)} %get-tuple-element.56.refs_1_.refs_2_, ...), custom_call_target="tpu_custom_call", output_to_operand_aliasing={{}: (0, {})} | custom-call | flops 67108864 | bytes 1048576 | tf_op jit(solution)/shard_map/pallas_call | solution.py:31
  43.9 1.0 %shard_map.128 = (bf16[128,1024]{1,0:T(8,128)(2,1)}, bf16[128,1024]{1,0:T(8,128)(2,1)}) custom-call(bf16[2,16,1024]{2,1,0:T(8,128)(2,1)S(1)} %get-tuple-element.51.refs_1_.refs_0_, bf16[2,16,1024]{2,1,0:T(8,128)(2,1)S(1)} %collective-permute-done.10.refs_2_.refs_1_, bf16[2,16,1024]{2,1,0:T(8,128)(2,1)S(1)} %collective-permute-done.11.refs_3_.refs_2_, ...), custom_call_target="tpu_custom_call" | custom-call | tf_op jit(solution)/shard_map/pallas_call | solution.py:31
  (7 shorter events, 0.2 us)
Async XLA Ops:
  2.1 1.5 %collective-permute-start = (bf16[4,16,1024]{2,1,0:T(8,128)(2,1)S(1)}, bf16[4,16,1024]{2,1,0:T(8,128)(2,1)S(1)}, u32[]{:S(2)}, u32[]{:S(2)}) collective-permute-start(bf16[4,16,1024]{2,1,0:T(8,128)(2,1)S(1)} %get-tuple-element.36), channel_id=1, source_target_pairs={{0,1},{1,0},{2,3},{3,2},{4,5},{5,4},{6,7},{7,6},{8,9},{9,8},{10,11... | collective-permute-start | bytes 393224 | tf_op jit(solution)/shard_map/ppermute | solution.py:287
  3.6 7.4 %collective-permute-start.1 = (bf16[2,16,1024]{2,1,0:T(8,128)(2,1)S(1)}, bf16[2,16,1024]{2,1,0:T(8,128)(2,1)S(1)}, u32[]{:S(2)}, u32[]{:S(2)}) collective-permute-start(bf16[2,16,1024]{2,1,0:T(8,128)(2,1)S(1)} %get-tuple-element.38), channel_id=1, source_target_pairs={{0,6},{1,7},{2,4},{3,5},{4,2},{5,3},{6,0},{7,1},{8,14},{9,15},{10,... | collective-permute-start | bytes 196616 | tf_op jit(solution)/shard_map/ppermute | solution.py:287
  7.5 4.3 %collective-permute-start.2 = (bf16[2,16,1024]{2,1,0:T(8,128)(2,1)S(1)}, bf16[2,16,1024]{2,1,0:T(8,128)(2,1)S(1)}, u32[]{:S(2)}, u32[]{:S(2)}) collective-permute-start(bf16[2,16,1024]{2,1,0:T(8,128)(2,1)S(1)} %get-tuple-element.39), channel_id=1, source_target_pairs={{0,2},{1,3},{2,0},{3,1},{4,6},{5,7},{6,4},{7,5},{8,10},{9,11},{10,... | collective-permute-start | bytes 196616 | tf_op jit(solution)/shard_map/ppermute | solution.py:287
  8.0 4.3 %collective-permute-start.3 = (bf16[2,16,1024]{2,1,0:T(8,128)(2,1)S(1)}, bf16[2,16,1024]{2,1,0:T(8,128)(2,1)S(1)}, u32[]{:S(2)}, u32[]{:S(2)}) collective-permute-start(bf16[2,16,1024]{2,1,0:T(8,128)(2,1)S(1)} %get-tuple-element.40), channel_id=1, source_target_pairs={{0,4},{1,5},{2,6},{3,7},{4,0},{5,1},{6,2},{7,3},{8,12},{9,13},{10,... | collective-permute-start | bytes 196616 | tf_op jit(solution)/shard_map/ppermute | solution.py:287
  13.5 7.7 %collective-permute-start.4 = (bf16[3,16,1024]{2,1,0:T(8,128)(2,1)S(1)}, bf16[3,16,1024]{2,1,0:T(8,128)(2,1)S(1)}, u32[]{:S(2)}, u32[]{:S(2)}) collective-permute-start(bf16[3,16,1024]{2,1,0:T(8,128)(2,1)S(1)} %get-tuple-element.48), channel_id=1, source_target_pairs={{0,8},{1,25},{2,10},{3,27},{4,12},{5,29},{6,14},{7,31},{8,0},{9,17... | collective-permute-start | bytes 294920 | tf_op jit(solution)/shard_map/ppermute | solution.py:297
  15.1 7.5 %collective-permute-start.5 = (bf16[3,16,1024]{2,1,0:T(8,128)(2,1)S(1)}, bf16[3,16,1024]{2,1,0:T(8,128)(2,1)S(1)}, u32[]{:S(2)}, u32[]{:S(2)}) collective-permute-start(bf16[3,16,1024]{2,1,0:T(8,128)(2,1)S(1)} %get-tuple-element.49), channel_id=1, source_target_pairs={{0,16},{1,17},{2,18},{3,19},{4,20},{5,21},{6,22},{7,23},{8,24},{9,... | collective-permute-start | bytes 294920 | tf_op jit(solution)/shard_map/ppermute | solution.py:297
  17.7 6.5 %collective-permute-start.6 = (bf16[3,16,1024]{2,1,0:T(8,128)(2,1)S(1)}, bf16[3,16,1024]{2,1,0:T(8,128)(2,1)S(1)}, u32[]{:S(2)}, u32[]{:S(2)}) collective-permute-start(bf16[3,16,1024]{2,1,0:T(8,128)(2,1)S(1)} %get-tuple-element.50), channel_id=1, source_target_pairs={{0,24},{1,9},{2,26},{3,11},{4,28},{5,13},{6,30},{7,15},{8,16},{9,1... | collective-permute-start | bytes 294920 | tf_op jit(solution)/shard_map/ppermute | solution.py:297
  24.3 8.3 %collective-permute-start.9 = (bf16[3,16,1024]{2,1,0:T(8,128)(2,1)S(1)}, bf16[3,16,1024]{2,1,0:T(8,128)(2,1)S(1)}, u32[]{:S(2)}, u32[]{:S(2)}) collective-permute-start(bf16[3,16,1024]{2,1,0:T(8,128)(2,1)S(1)} %shard_map.124.refs_3_.refs_2_), channel_id=1, source_target_pairs={{0,16},{1,17},{2,18},{3,19},{4,20},{5,21},{6,22},{7,23},{8,24},{9,... | collective-permute-start | bytes 294920 | tf_op jit(solution)/shard_map/ppermute | solution.py:297
  26.9 6.2 %collective-permute-start.8 = (bf16[3,16,1024]{2,1,0:T(8,128)(2,1)S(1)}, bf16[3,16,1024]{2,1,0:T(8,128)(2,1)S(1)}, u32[]{:S(2)}, u32[]{:S(2)}) collective-permute-start(bf16[3,16,1024]{2,1,0:T(8,128)(2,1)S(1)} %shard_map.124.refs_3_.refs_2_), channel_id=1, source_target_pairs={{0,8},{1,25},{2,10},{3,27},{4,12},{5,29},{6,14},{7,31},{8,0},{9,17... | collective-permute-start | bytes 294920 | tf_op jit(solution)/shard_map/ppermute | solution.py:297
  27.6 6.5 %collective-permute-start.7 = (bf16[3,16,1024]{2,1,0:T(8,128)(2,1)S(1)}, bf16[3,16,1024]{2,1,0:T(8,128)(2,1)S(1)}, u32[]{:S(2)}, u32[]{:S(2)}) collective-permute-start(bf16[3,16,1024]{2,1,0:T(8,128)(2,1)S(1)} %shard_map.124.refs_3_.refs_2_), channel_id=1, source_target_pairs={{0,24},{1,9},{2,26},{3,11},{4,28},{5,13},{6,30},{7,15},{8,16},{9,1... | collective-permute-start | bytes 294920 | tf_op jit(solution)/shard_map/ppermute | solution.py:297
  35.4 6.3 %collective-permute-start.10 = (bf16[2,16,1024]{2,1,0:T(8,128)(2,1)S(1)}, bf16[2,16,1024]{2,1,0:T(8,128)(2,1)S(1)}, u32[]{:S(2)}, u32[]{:S(2)}) collective-permute-start(bf16[2,16,1024]{2,1,0:T(8,128)(2,1)S(1)} %get-tuple-element.52), channel_id=1, source_target_pairs={{0,6},{1,7},{2,4},{3,5},{4,2},{5,3},{6,0},{7,1},{8,14},{9,15},{10,... | collective-permute-start | bytes 196616 | tf_op jit(solution)/shard_map/ppermute | solution.py:287
  37.7 4.3 %collective-permute-start.11 = (bf16[2,16,1024]{2,1,0:T(8,128)(2,1)S(1)}, bf16[2,16,1024]{2,1,0:T(8,128)(2,1)S(1)}, u32[]{:S(2)}, u32[]{:S(2)}) collective-permute-start(bf16[2,16,1024]{2,1,0:T(8,128)(2,1)S(1)} %get-tuple-element.53), channel_id=1, source_target_pairs={{0,2},{1,3},{2,0},{3,1},{4,6},{5,7},{6,4},{7,5},{8,10},{9,11},{10,... | collective-permute-start | bytes 196616 | tf_op jit(solution)/shard_map/ppermute | solution.py:287
  38.2 4.3 %collective-permute-start.12 = (bf16[2,16,1024]{2,1,0:T(8,128)(2,1)S(1)}, bf16[2,16,1024]{2,1,0:T(8,128)(2,1)S(1)}, u32[]{:S(2)}, u32[]{:S(2)}) collective-permute-start(bf16[2,16,1024]{2,1,0:T(8,128)(2,1)S(1)} %get-tuple-element.54), channel_id=1, source_target_pairs={{0,4},{1,5},{2,6},{3,7},{4,0},{5,1},{6,2},{7,3},{8,12},{9,13},{10,... | collective-permute-start | bytes 196616 | tf_op jit(solution)/shard_map/ppermute | solution.py:287
  42.5 1.4 %collective-permute-start.13 = (bf16[4,16,1024]{2,1,0:T(8,128)(2,1)S(1)}, bf16[4,16,1024]{2,1,0:T(8,128)(2,1)S(1)}, u32[]{:S(2)}, u32[]{:S(2)}) collective-permute-start(bf16[4,16,1024]{2,1,0:T(8,128)(2,1)S(1)} %shard_map.127.refs_1_), channel_id=1, source_target_pairs={{0,1},{1,0},{2,3},{3,2},{4,5},{5,4},{6,7},{7,6},{8,9},{9,8},{10,11... | collective-permute-start | bytes 393224 | tf_op jit(solution)/shard_map/ppermute | solution.py:287
